TPU v7x, 128 devices: a whole 4x4x4 slice. The times are simulated.
128 devices in a mesh: role: 2 (over core), dev: 64 (over z, y, x).
Axes of the slice: x: 4, y: 4, z: 4, core: 2. Of those that a mesh axis runs over, the one named last changes fastest.
Arguments:
- resid: bfloat16 [512, 3584], P('dev'), may hold values from -1.5 to 1.5
- query: bfloat16 [512, 64, 576], P('dev'), may hold values from -32 to 32
- cache: bfloat16 [512, 128, 576], P('dev'), may hold values from -6 to 6
- lengths: int32 [512], P('dev'), may hold values from 2 to 128, as said below
- w_uv: bfloat16 [512, 64, 128], P(None, 'dev'), may hold values from -0.25 to 0.25
- w_out: bfloat16 [64, 128, 3584], P('dev', None, 'role'), may hold values from -0.0625 to 0.0625
- norm_gain: float32 [3584], replicated, may hold values from 0.5 to 1.5
- expert_ids: int32 [512, 8], P('dev'), may hold values from 0 to 63, as said below
- gate_scores: float32 [512, 8], P('dev'), may hold values from 0.05 to 1
- w_gate: bfloat16 [64, 3584, 1024], P('dev'), may hold values from -0.09375 to 0.09375
- w_up: bfloat16 [64, 3584, 1024], P('dev'), may hold values from -0.09375 to 0.09375
- w_down: bfloat16 [64, 1024, 3584], P('dev'), may hold values from -0.1875 to 0.1875
Outputs:
- layer_out: bfloat16 [512, 3584], P('dev', 'role')
Inputs may be any that keep to these rules, and one draw needn't show every extreme that they name: `expert_ids`: within the rows of one index of dev, no expert is chosen by more than 2 rows; in the rows of the last index of dev, expert 0 is chosen by exactly 2; each row names 8 different experts. `lengths`: some sequence uses all 128 positions.
All inputs are finite; a program needn't handle non-finite values.
Results may differ from a plain program's by a relative error of at most 0.014.
Values may be sent and summed in bfloat16 or wider, within the bound.
No kernel may reach another device: no remote copies, remote signals or barrier semaphores. Data moves between devices by JAX's collectives and lax.ppermute only.
A program may use at most 128 MiB of HBM per device.

v0:
```python
import jax
import jax.numpy as jnp
from jax import lax
from jax.sharding import PartitionSpec as P

softmax_scale = 0.07216878364870323


def local(
    resid,
    query,
    cache,
    lengths,
    w_uv,
    w_out,
    norm_gain,
    expert_ids,
    gate_scores,
    w_gate,
    w_up,
    w_down,
):
    role_index = lax.axis_index("role")
    tok_dev = resid.shape[0]
    width = resid.shape[1]
    half_width = width // 2
    latent_width = w_uv.shape[0]
    n_dev = lax.axis_size("dev")
    top_count = expert_ids.shape[1]
    capacity = max(2, tok_dev * top_count * 2 // n_dev)
    scores = (
        jnp.einsum("thc,tlc->thl", query, cache, preferred_element_type=jnp.float32) * softmax_scale
    )
    position = jnp.arange(cache.shape[1], dtype=jnp.int32)
    usable = position[None, None, :] < lengths[:, None, None]
    scores = jnp.where(usable, scores, -1e30)
    row_max = jnp.max(scores, axis=-1, keepdims=True)
    exponent = jnp.where(usable, jnp.exp(scores - row_max), 0.0)
    attention = (exponent / jnp.sum(exponent, axis=-1, keepdims=True)).astype(jnp.bfloat16)
    context = jnp.einsum(
        "thl,tlc->thc", attention, cache[:, :, :latent_width], preferred_element_type=jnp.float32
    ).astype(jnp.bfloat16)
    by_head = lax.all_to_all(context, "dev", split_axis=1, concat_axis=0, tiled=True)
    values = jnp.einsum("thc,chv->thv", by_head, w_uv, preferred_element_type=jnp.float32).astype(
        jnp.bfloat16
    )
    flat_values = values.reshape(values.shape[0], -1)
    whole_out = lax.all_gather(w_out, "role", axis=2, tiled=True)
    out_rows = whole_out.reshape(-1, width)
    attended = lax.psum_scatter(
        jnp.dot(flat_values, out_rows, preferred_element_type=jnp.float32),
        "dev",
        scatter_dimension=0,
        tiled=True,
    )
    hidden = resid.astype(jnp.float32) + attended
    normed = (
        hidden * lax.rsqrt(jnp.mean(hidden * hidden, axis=-1, keepdims=True) + 1e-06) * norm_gain
    ).astype(jnp.bfloat16)
    own_half = lax.dynamic_slice_in_dim(hidden, role_index * half_width, half_width, 1)
    flat_ids = expert_ids.reshape(-1)
    onehot = (flat_ids[:, None] == jnp.arange(n_dev, dtype=jnp.int32)[None, :]).astype(jnp.int32)
    slot_rank = jnp.sum((jnp.cumsum(onehot, axis=0) - 1) * onehot, axis=1)
    placed = (flat_ids * capacity + slot_rank).reshape(tok_dev, top_count)
    slot_ids = jnp.arange(n_dev * capacity, dtype=jnp.int32)
    lookup = jnp.any(slot_ids[:, None, None] == placed[None, :, :], axis=-1).astype(jnp.bfloat16)
    packed = jnp.dot(lookup, normed, preferred_element_type=jnp.float32).astype(jnp.bfloat16)
    packed = jnp.where(role_index == 0, packed, jnp.zeros_like(packed))
    outgoing = jnp.concatenate([jnp.zeros_like(packed), packed], axis=0)
    arrived = lax.all_to_all(outgoing, ("role", "dev"), split_axis=0, concat_axis=0, tiled=True)[
        : n_dev * capacity
    ]

    def run_expert(row_block):
        gate_part = jnp.dot(row_block, w_gate[0], preferred_element_type=jnp.float32)
        up_part = jnp.dot(row_block, w_up[0], preferred_element_type=jnp.float32)
        inner = (jax.nn.silu(gate_part) * up_part).astype(jnp.bfloat16)
        return jnp.dot(inner, w_down[0], preferred_element_type=jnp.float32).astype(jnp.bfloat16)

    def skip_expert(row_block):
        return jnp.zeros_like(row_block)

    produced = lax.cond(role_index == 1, run_expert, skip_expert, arrived)
    pieces = jnp.concatenate([produced[:, :half_width], produced[:, half_width:]], axis=0)
    returned = lax.all_to_all(pieces, ("role", "dev"), split_axis=0, concat_axis=0, tiled=True)[
        n_dev * capacity :
    ]
    gate_weights = (2.5 * gate_scores / jnp.sum(gate_scores, axis=-1, keepdims=True)).astype(
        jnp.bfloat16
    )
    spread = jnp.where(
        slot_ids[None, None, :] == placed[:, :, None],
        gate_weights.astype(jnp.float32)[:, :, None],
        0.0,
    )
    combine_weights = jnp.sum(spread, axis=1).astype(jnp.bfloat16)
    combined = jnp.dot(combine_weights, returned, preferred_element_type=jnp.float32)
    return (own_half + combined).astype(jnp.bfloat16)


def solution(mesh):
    return jax.shard_map(
        local,
        mesh=mesh,
        in_specs=(
            P("dev", None),
            P("dev", None, None),
            P("dev", None, None),
            P("dev"),
            P(None, "dev", None),
            P("dev", None, "role"),
            P(),
            P("dev", None),
            P("dev", None),
            P("dev", None, None),
            P("dev", None, None),
            P("dev", None, None),
        ),
        out_specs=P("dev", "role"),
        check_vma=False,
    )
```

profile of v0, /device:TPU:0, one launch (start us, length us, event | category | flops | bytes accessed | tf_op | source)
XLA Modules:
  0.0 483.5 jit_solution(6310144584593855220)
XLA Ops:
  6.5 0.0 copy-start
  6.5 0.0 copy-start.1
  6.5 0.8 iota_compare_fusion.3
  7.3 0.3 copy-done
  7.6 1.6 fusion.30
  9.3 0.2 fusion.48
  9.5 2.2 convolution_convert_fusion.1
  11.8 1.1 copy.22
  12.9 11.5 %all-to-all-start = ((bf16[8,64,512]{2,0,1:T(8,128)(2,1)}), bf16[8,64,512]{2,0,1:T(8,128)(2,1)S(1)}, u32[]{:S(2)}, u32[]{:S(2)}) async-start(bf16[8,64,512]{2,0,1:T(8,128)(2,1)} %copy.22), calls=%async_computation | async-start | bytes 1048576 | tf_op jit(solution)/shard_map/all_to_all | solution.py:43
  24.4 0.0 reduce-scatter.2.cloned.1.call-start
  24.4 2.7 all_gather.3
  27.1 0.0 copy-start.3
  27.1 0.0 copy-start.2
  27.1 0.0 copy-start.5
  27.1 10.6 %all-to-all-done = bf16[8,64,512]{2,0,1:T(8,128)(2,1)S(1)} async-done(((bf16[8,64,512]{2,0,1:T(8,128)(2,1)}), bf16[8,64,512]{2,0,1:T(8,128)(2,1)S(1)}, u32[]{:S(2)}, u32[]{:S(2)}) %all-to-all-start) | async-done | bytes 524320 | tf_op jit(solution)/shard_map/all_to_all | solution.py:43
  37.7 0.0 copy-done.1
  37.7 4.5 fusion.31
  42.2 0.0 reduce-scatter.2.cloned.1.call-update
  42.2 0.0 copy-done.3
  42.2 0.1 eq.48
  42.3 0.1 fusion.41
  42.4 0.1 reduce_window_sum.11
  42.5 0.2 select_reduce_fusion.1
  42.7 0.1 reduce_sum.49
  42.8 0.1 fusion.42
  42.9 360.0 %reduce-scatter.2.cloned.1.call-done = f32[8,3584]{1,0:T(8,128)} async-done(((f32[512,3584]{1,0:T(8,128)}), f32[8,3584]{1,0:T(8,128)}) %reduce-scatter.2.cloned.1.call-update) | async-done | bytes 114704 | tf_op jit(solution)/shard_map/reduce_scatter | solution.py:50
  402.9 0.0 copy-done.2
  402.9 1.0 multiply_reduce_fusion
  403.9 0.0 copy-done.5
  403.9 0.5 fusion.25
  404.4 0.1 concatenate.6
  404.5 1.7 all_to_all.26
  406.2 4.6 all-to-all-start.1
  410.9 26.1 %all-to-all-done.1 = bf16[128,2,3584]{2,1,0:T(2,128)(2,1)S(1)} async-done(((bf16[128,2,3584]{2,1,0:T(2,128)(2,1)}), bf16[128,2,3584]{2,1,0:T(2,128)(2,1)S(1)}, u32[]{:S(2)}, u32[]{:S(2)}) %all-to-all-start.1) | async-done | bytes 1835040 | tf_op jit(solution)/shard_map/all_to_all | solution.py:70
  437.0 1.0 conditional.1
  437.0 1.0 broadcast.49
  438.0 0.0 copy-start.4
  438.0 1.2 fusion.47
  439.2 0.1 pad_maximum_fusion
  439.3 1.3 all_to_all.28
  440.5 17.7 %all-to-all-start.2 = ((bf16[128,2,1792]{2,1,0:T(2,128)(2,1)}), bf16[128,2,1792]{2,1,0:T(2,128)(2,1)S(1)}, u32[]{:S(2)}, u32[]{:S(2)}) async-start(bf16[128,2,1792]{2,1,0:T(2,128)(2,1)} %all_to_all.28), calls=%async_computation.3 | async-start | bytes 1835008 | tf_op jit(solution)/shard_map/all_to_all | solution.py:85
  458.2 0.0 copy-done.4
  458.3 0.1 reduce_sum.50
  458.4 0.1 fusion.43
  458.5 0.1 select_reduce_fusion
  458.6 16.8 %all-to-all-done.2 = bf16[128,2,1792]{2,1,0:T(2,128)(2,1)S(1)} async-done(((bf16[128,2,1792]{2,1,0:T(2,128)(2,1)}), bf16[128,2,1792]{2,1,0:T(2,128)(2,1)S(1)}, u32[]{:S(2)}, u32[]{:S(2)}) %all-to-all-start.2) | async-done | bytes 917536 | tf_op jit(solution)/shard_map/all_to_all | solution.py:85
  475.4 0.3 slice.32
  475.7 0.2 slice.27
  475.9 0.8 fusion.26
  (2 shorter events, 0.0 us)
Async XLA Ops:
  6.5 1.1 copy-start
  6.5 31.2 %copy-start.1 = (bf16[512,1,128]{2,0,1:T(8,128)(2,1)S(1)}, bf16[512,1,128]{2,0,1:T(8,128)(2,1)}, u32[]{:S(2)}) copy-start(bf16[512,1,128]{2,0,1:T(8,128)(2,1)} %param.18) | copy-start | bytes 393220
  12.9 24.9 %all-to-all-start = ((bf16[8,64,512]{2,0,1:T(8,128)(2,1)}), bf16[8,64,512]{2,0,1:T(8,128)(2,1)S(1)}, u32[]{:S(2)}, u32[]{:S(2)}) async-start(bf16[8,64,512]{2,0,1:T(8,128)(2,1)} %copy.22), calls=%async_computation | async-start | bytes 1048576 | tf_op jit(solution)/shard_map/all_to_all | solution.py:43
  24.4 378.5 %reduce-scatter.2.cloned.1.call-start = ((), (), s32[]{:S(2)}) async-start(), calls=%async_computation.4 | async-start | bytes 7454720 | tf_op jit(solution)/shard_map/reduce_scatter | solution.py:50
  27.1 15.1 %copy-start.3 = (s32[8,8]{1,0:T(8,128)S(1)}, s32[8,8]{1,0:T(8,128)}, u32[]{:S(2)}) copy-start(s32[8,8]{1,0:T(8,128)} %param.21) | copy-start | bytes 772
  27.1 375.8 %copy-start.2 = (bf16[8,3584]{1,0:T(8,128)(2,1)S(1)}, bf16[8,3584]{1,0:T(8,128)(2,1)}, u32[]{:S(2)}) copy-start(bf16[8,3584]{1,0:T(8,128)(2,1)} %param.14) | copy-start | bytes 172036
  27.1 376.8 %copy-start.5 = (f32[3584]{0:T(1024)S(1)}, f32[3584]{0:T(1024)}, u32[]{:S(2)}) copy-start(f32[3584]{0:T(1024)} %param.20) | copy-start | bytes 43012
  406.2 30.7 %all-to-all-start.1 = ((bf16[128,2,3584]{2,1,0:T(2,128)(2,1)}), bf16[128,2,3584]{2,1,0:T(2,128)(2,1)S(1)}, u32[]{:S(2)}, u32[]{:S(2)}) async-start(bf16[128,2,3584]{2,1,0:T(2,128)(2,1)} %all_to_all.26), calls=%async_computation.2 | async-start | bytes 3670016 | tf_op jit(solution)/shard_map/all_to_all | solution.py:70
  438.0 20.3 %copy-start.4 = (f32[8,8]{1,0:T(8,128)S(1)}, f32[8,8]{1,0:T(8,128)}, u32[]{:S(2)}) copy-start(f32[8,8]{1,0:T(8,128)} %param.22) | copy-start | bytes 772
  440.5 34.9 %all-to-all-start.2 = ((bf16[128,2,1792]{2,1,0:T(2,128)(2,1)}), bf16[128,2,1792]{2,1,0:T(2,128)(2,1)S(1)}, u32[]{:S(2)}, u32[]{:S(2)}) async-start(bf16[128,2,1792]{2,1,0:T(2,128)(2,1)} %all_to_all.28), calls=%async_computation.3 | async-start | bytes 1835008 | tf_op jit(solution)/shard_map/all_to_all | solution.py:85
Sparse Core Ops, SparseCore 0:
  42.4 360.4 reduce-scatter.1
where the time goes:
time: 484 us
  waiting for transfers between devices  414 us (86%)
  starting transfers between devices  33.9 us (7%)
  between operations  13.5 us (3%)
  matrix products  9.61 us (2%)
  local copies, waits for them, and re-layouts  7.36 us (2%)
    reduce_scatter x1, waiting for transfers between devices, local(): lax.psum_scatter(jnp.dot(flat_values, out_rows, preferred_element_type=jn...  360 us
    all_to_all x1, waiting for transfers between devices, local(): lax.all_to_all(outgoing, ('role', 'dev'), split_axis=0, concat_axis=0, ti...  26.1 us
    all_to_all x1, starting transfers between devices, local(): lax.all_to_all(pieces, ('role', 'dev'), split_axis=0, concat_axis=0, tile...  17.7 us
    all_to_all x1, waiting for transfers between devices, local(): lax.all_to_all(pieces, ('role', 'dev'), split_axis=0, concat_axis=0, tile...  16.8 us
    all_to_all x1, starting transfers between devices, local(): lax.all_to_all(context, 'dev', split_axis=1, concat_axis=0, tiled=True)  11.5 us
    all_to_all x1, waiting for transfers between devices, local(): lax.all_to_all(context, 'dev', split_axis=1, concat_axis=0, tiled=True)  10.6 us
  transfers between devices with their start and end apart: 4, of which 4 were waited for; matrix products, arithmetic and copies ran while one was open for 0% of the time, Pallas kernels for 0%

commit v1 on v0

v1 whole, which is shorter than its diff:
```python
import jax
import jax.numpy as jnp
from jax import lax
from jax.sharding import PartitionSpec as P

softmax_scale = 0.07216878364870323
bf16 = jnp.bfloat16
f32 = jnp.float32


def split_terms(value):
    first = lax.reduce_precision(value, 8, 7)
    rest = value - first
    second = lax.reduce_precision(rest, 8, 7)
    third = rest - second
    return jnp.stack([first, second, third], axis=-1).astype(bf16)


def local(
    resid,
    query,
    cache,
    lengths,
    w_uv,
    w_out,
    norm_gain,
    expert_ids,
    gate_scores,
    w_gate,
    w_up,
    w_down,
):
    role_index = lax.axis_index("role")
    tok_dev, width = resid.shape
    half_width = w_out.shape[2]
    latent_width = w_uv.shape[0]
    n_dev = lax.axis_size("dev")
    top_count = expert_ids.shape[1]
    capacity = max(2, tok_dev * top_count * 2 // n_dev)
    slots = n_dev * capacity
    hidden_units = w_gate.shape[2]
    swap = [(0, 1), (1, 0)]

    scores = jnp.einsum("thc,tlc->thl", query, cache, preferred_element_type=f32) * softmax_scale
    position = jnp.arange(cache.shape[1], dtype=jnp.int32)
    usable = position[None, None, :] < lengths[:, None, None]
    scores = jnp.where(usable, scores, -1e30)
    row_max = jnp.max(scores, axis=-1, keepdims=True)
    exponent = jnp.where(usable, jnp.exp(scores - row_max), 0.0)
    attention = (exponent / jnp.sum(exponent, axis=-1, keepdims=True)).astype(bf16)
    context = jnp.einsum(
        "thl,tlc->thc", attention, cache[:, :, :latent_width], preferred_element_type=f32
    ).astype(bf16)
    by_head = lax.all_to_all(context, "dev", split_axis=1, concat_axis=0, tiled=True)
    values = jnp.dot(by_head[:, 0], w_uv[:, 0], preferred_element_type=f32).astype(bf16)
    partial = jnp.dot(values, w_out[0], preferred_element_type=f32).astype(bf16)
    pieces = lax.all_to_all(
        partial.reshape(n_dev, tok_dev, half_width), "dev", split_axis=0, concat_axis=0, tiled=True
    )
    attended = jnp.sum(pieces.astype(f32), axis=0)

    own_resid = lax.dynamic_slice_in_dim(resid, role_index * half_width, half_width, 1)
    own_gain = lax.dynamic_slice_in_dim(norm_gain, role_index * half_width, half_width, 0)
    hidden = own_resid.astype(f32) + attended
    squares = split_terms(jnp.sum(hidden * hidden, axis=-1))
    rows = jnp.concatenate(
        [(hidden * own_gain).astype(bf16), squares, jnp.zeros((tok_dev, 125), bf16)], axis=1
    )

    flat_ids = expert_ids.reshape(-1)
    onehot = (flat_ids[:, None] == jnp.arange(n_dev, dtype=jnp.int32)[None, :]).astype(jnp.int32)
    slot_rank = jnp.sum((jnp.cumsum(onehot, axis=0) - 1) * onehot, axis=1)
    placed = (flat_ids * capacity + slot_rank).reshape(tok_dev, top_count)
    slot_ids = jnp.arange(slots, dtype=jnp.int32)
    lookup = jnp.any(slot_ids[:, None, None] == placed[None, :, :], axis=-1).astype(bf16)
    packed = jnp.dot(lookup, rows, preferred_element_type=f32).astype(bf16)
    arrived = lax.all_to_all(packed, "dev", split_axis=0, concat_axis=0, tiled=True)

    row_block = arrived[:, :half_width]
    own_gate = lax.dynamic_slice_in_dim(w_gate[0], role_index * half_width, half_width, 0)
    own_up = lax.dynamic_slice_in_dim(w_up[0], role_index * half_width, half_width, 0)
    own_down = lax.dynamic_slice_in_dim(w_down[0], role_index * half_width, half_width, 1)
    gate_part = jnp.dot(row_block, own_gate, preferred_element_type=f32)
    up_part = jnp.dot(row_block, own_up, preferred_element_type=f32)
    square_terms = arrived[:, half_width:]
    outward = jnp.concatenate([gate_part.astype(bf16), up_part.astype(bf16), square_terms], axis=1)
    inward = lax.ppermute(outward, "role", swap).astype(f32)
    gate_part = gate_part + inward[:, :hidden_units]
    up_part = up_part + inward[:, hidden_units : 2 * hidden_units]
    total = jnp.sum(square_terms.astype(f32) + inward[:, 2 * hidden_units :], axis=1, keepdims=True)
    scale = lax.rsqrt(total / width + 1e-06)
    inner = (jax.nn.silu(gate_part * scale) * (up_part * scale)).astype(bf16)
    produced = jnp.dot(inner, own_down, preferred_element_type=f32).astype(bf16)
    returned = lax.all_to_all(produced, "dev", split_axis=0, concat_axis=0, tiled=True)

    gate_weights = (2.5 * gate_scores / jnp.sum(gate_scores, axis=-1, keepdims=True)).astype(bf16)
    spread = jnp.where(
        slot_ids[None, None, :] == placed[:, :, None], gate_weights.astype(f32)[:, :, None], 0.0
    )
    combine_weights = jnp.sum(spread, axis=1).astype(bf16)
    combined = jnp.dot(combine_weights, returned, preferred_element_type=f32)
    return (hidden + combined).astype(bf16)


def solution(mesh):
    return jax.shard_map(
        local,
        mesh=mesh,
        in_specs=(
            P("dev", None),
            P("dev", None, None),
            P("dev", None, None),
            P("dev"),
            P(None, "dev", None),
            P("dev", None, "role"),
            P(),
            P("dev", None),
            P("dev", None),
            P("dev", None, None),
            P("dev", None, None),
            P("dev", None, None),
        ),
        out_specs=P("dev", "role"),
        check_vma=False,
    )
```

time: 484 us -> 111 us (0.23)
  waiting for transfers between devices: 414 us -> 39.9 us
  blocking collectives: 2.67 us -> 41.4 us
  starting transfers between devices: 33.9 us -> 9.69 us
  between operations: 13.5 us -> 0.21 us
  local copies, waits for them, and re-layouts: 7.36 us -> 2.5 us
    reduce_scatter x1 -> x0, waiting for transfers between devices: 360 us -> none  [local(): lax.psum_scatter(jnp.dot(flat_values, out_rows, preferred_element_type=jn...]
    all_to_all x0 -> x2, blocking collectives: none -> 41.4 us  [the longest x1 24.7 us: local(): lax.all_to_all(context, 'dev', split_axis=1, concat_axis=0, tiled=True)]
    all_to_all x3 -> x2, starting transfers between devices: 33.9 us -> 9.6 us  [the longest x1 4.86 us: local(): lax.all_to_all(partial.reshape(n_dev, tok_dev, half_width), 'dev', split_...]
    all_to_all x3 -> x2, waiting for transfers between devices: 53.5 us -> 38 us  [the longest x1 25.1 us: local(): lax.all_to_all(partial.reshape(n_dev, tok_dev, half_width), 'dev', split_...]
    dot_general x4 -> x7, matrix products: 7.37 us -> 13.4 us  [the longest x1 2.84 us: local(): produced = jnp.dot(inner, own_down, preferred_element_type=f32).astype(bf16)]
  transfers between devices with their start and end apart: 4 -> 3, of which waited for: 4 -> 3; matrix products, arithmetic and copies ran while one was open for 0% -> 1% of each run, Pallas kernels for 0% -> 0%
where the time goes in v1:
time: 111 us
  blocking collectives  41.4 us (37%)
  waiting for transfers between devices  39.9 us (36%)
  matrix products  14.4 us (13%)
  starting transfers between devices  9.69 us (9%)
  local copies, waits for them, and re-layouts  2.5 us (2%)
  other arithmetic  2.5 us (2%)
    all_to_all x1, waiting for transfers between devices, local(): lax.all_to_all(partial.reshape(n_dev, tok_dev, half_width), 'dev', split_...  25.1 us
    all_to_all x1, blocking collectives, local(): lax.all_to_all(context, 'dev', split_axis=1, concat_axis=0, tiled=True)  24.7 us
    all_to_all x1, blocking collectives, local(): lax.all_to_all(packed, 'dev', split_axis=0, concat_axis=0, tiled=True)  16.8 us
    all_to_all x1, waiting for transfers between devices, local(): lax.all_to_all(produced, 'dev', split_axis=0, concat_axis=0, tiled=True)  12.8 us
    all_to_all x1, starting transfers between devices, local(): lax.all_to_all(partial.reshape(n_dev, tok_dev, half_width), 'dev', split_...  4.86 us
    all_to_all x1, starting transfers between devices, local(): lax.all_to_all(produced, 'dev', split_axis=0, concat_axis=0, tiled=True)  4.74 us
    dot_general x1, matrix products, local(): produced = jnp.dot(inner, own_down, preferred_element_type=f32).astype(bf16)  2.84 us
    dot_general x1, matrix products, local(): gate_part = jnp.dot(row_block, own_gate, preferred_element_type=f32)  2.73 us
  transfers between devices with their start and end apart: 3, of which 3 were waited for; matrix products, arithmetic and copies ran while one was open for 1% of the time, Pallas kernels for 0%

profile of v1, /device:TPU:0, one launch (start us, length us, event | category | flops | bytes accessed | tf_op | source)
XLA Modules:
  0.0 110.7 jit_solution(8607495562088498890)
XLA Ops:
  0.0 0.0 copy-start
  0.0 0.0 copy-start.1
  0.0 0.9 iota_compare_fusion.3
  0.9 0.2 copy-done
  1.1 1.6 %fusion.18 = f32[8,64,128]{2,1,0:T(8,128)S(1)} fusion(bf16[8,64,576]{2,1,0:T(8,128)(2,1)S(1)} %copy-done, bf16[8,128,576]{1,2,0:T(8,128)(2,1)} %param.14, pred[8,128]{1,0:T(8,128)(4,1)S(1)} %iota_compare_fusion.3), kind=kOutput, calls=%fused_computation.22 | convolution fusion | flops 75628544 | bytes 2032640 | tf_op jit(solution)/shard_map/thc,tlc->thl/dot_general | solution.py:44
  2.7 0.2 fusion.47
  3.0 0.0 copy-done.1
  3.0 0.0 copy-start.2
  3.0 0.0 copy-start.3
  3.0 1.0 convolution_convert_fusion.2
  4.0 0.3 copy.25
  4.4 24.7 %all_to_all.44 = bf16[8,64,512]{2,0,1:T(8,128)(2,1)S(1)} all-to-all(bf16[8,64,512]{2,0,1:T(8,128)(2,1)S(1)} %copy.25), channel_id=1, replica_groups=mesh['role'=2,'dev'=64] {'dev'}, dimensions={1} | all-to-all | bytes 1048576 | tf_op jit(solution)/shard_map/all_to_all | solution.py:54
  29.0 0.0 copy-done.2
  29.0 0.0 copy-done.3
  29.0 2.3 %fusion.10 = bf16[64,8,1792]{2,1,0:T(8,128)(2,1)} fusion(bf16[8,64,512]{2,0,1:T(8,128)(2,1)S(1)} %all_to_all.44, bf16[1,128,1792]{2,1,0:T(8,128)(2,1)S(1)} %copy-done.2, bf16[512,1,128]{2,0,1:T(8,128)(2,1)S(1)} %copy-done.3), kind=kOutput, calls=%fused_computation.12 | convolution fusion | flops 302972928 | bytes 2949120 | tf_op jit(solution)/shard_map/dot_general | solution.py:56
  31.4 0.0 copy-start.5
  31.4 0.0 copy-start.7
  31.4 4.9 %all-to-all-start.1 = ((bf16[64,8,1792]{2,1,0:T(8,128)(2,1)}), bf16[64,8,1792]{2,1,0:T(8,128)(2,1)S(1)}, u32[]{:S(2)}, u32[]{:S(2)}) async-start(bf16[64,8,1792]{2,1,0:T(8,128)(2,1)} %fusion.10), calls=%async_computation.1 | async-start | bytes 3670016 | tf_op jit(solution)/shard_map/all_to_all | solution.py:57
  36.2 0.0 copy-start.4
  36.2 0.0 copy-done.5
  36.3 0.1 eq.42
  36.3 0.1 fusion.36
  36.4 0.1 reduce_window_sum.11
  36.5 0.2 select_reduce_fusion.1
  36.7 0.1 reduce_sum.70
  36.8 0.0 copy-done.7
  36.8 0.1 dynamic_slice.22
  36.9 0.1 fusion.37
  37.0 25.1 %all-to-all-done.1 = bf16[64,8,1792]{2,1,0:T(8,128)(2,1)S(1)} async-done(((bf16[64,8,1792]{2,1,0:T(8,128)(2,1)}), bf16[64,8,1792]{2,1,0:T(8,128)(2,1)S(1)}, u32[]{:S(2)}, u32[]{:S(2)}) %all-to-all-start.1) | async-done | bytes 1835040 | tf_op jit(solution)/shard_map/all_to_all | solution.py:57
  62.1 0.3 convert_reduce_fusion
  62.4 0.0 copy-done.4
  62.4 0.1 multiply_reduce_fusion
  62.5 0.1 copy.26
  62.6 0.1 concatenate.7
  62.7 0.3 convolution_convert_fusion.1
  63.1 0.2 all_to_all.34
  63.3 16.8 %all_to_all.45 = bf16[64,2,1920]{2,1,0:T(2,128)(2,1)S(1)} all-to-all(bf16[64,2,1920]{2,1,0:T(2,128)(2,1)S(1)} %all_to_all.34), channel_id=1, replica_groups=mesh['role'=2,'dev'=64] {'dev'}, dimensions={0} | all-to-all | bytes 983040 | tf_op jit(solution)/shard_map/all_to_all | solution.py:77
  80.0 0.2 all_to_all.36
  80.2 2.7 %fusion.49 = (bf16[128,1024]{1,0:T(8,128)(2,1)S(1)}, f32[128,1024]{1,0:T(8,128)S(1)}) fusion(bf16[1,3584,1024]{2,1,0:T(8,128)(2,1)} %param.21, s32[]{:T(128)S(6)} %select_n.18, bf16[128,1920]{1,0:T(8,128)(2,1)S(1)} %all_to_all.36), kind=kOutput, calls=%fused_computation.72 | convolution fusion | flops 469893120 | bytes 4915204 | tf_op jit(solution)/shard_map/dot_general | solution.py:83
  83.0 2.7 %fusion.48 = (bf16[128,1024]{1,0:T(8,128)(2,1)S(1)}, f32[128,1024]{1,0:T(8,128)S(1)}) fusion(bf16[1,3584,1024]{2,1,0:T(8,128)(2,1)} %param.22, s32[]{:T(128)S(6)} %select_n.18, bf16[128,1920]{1,0:T(8,128)(2,1)S(1)} %all_to_all.36), kind=kOutput, calls=%fused_computation.71 | convolution fusion | flops 469893120 | bytes 4915204 | tf_op jit(solution)/shard_map/dot_general | solution.py:84
  85.8 0.1 collective-permute-start
  85.9 1.9 %collective-permute-done = bf16[128,2176]{1,0:T(8,128)(2,1)S(1)} collective-permute-done((bf16[128,2176]{1,0:T(8,128)(2,1)S(1)}, bf16[128,2176]{1,0:T(8,128)(2,1)S(1)}, u32[]{:S(2)}, u32[]{:S(2)}) %collective-permute-start) | collective-permute-done | bytes 557088 | tf_op jit(solution)/shard_map/ppermute | solution.py:87
  87.8 0.1 convert_element_type.73
  87.9 0.1 fusion.35
  88.0 2.8 %fusion.11 = bf16[128,1792]{1,0:T(8,128)(2,1)S(1)} fusion(bf16[1,1024,3584]{2,1,0:T(8,128)(2,1)} %param.23, s32[]{:T(128)S(6)} %select_n.18, f32[128,1024]{1,0:T(8,128)S(1)} %get-tuple-element.11, f32[128,2176]{1,0:T(8,128)S(1)} %convert_element_type.73, f32[128,1024]{1,0:T(8,128)S(1)} %get-tuple-element.13, f32[128]{0:T(128)S(1)} %add_rsqrt_fusion), kind=kOutput, calls=%fused_computation.13 | convolution fusion | flops 471302144 | bytes 6226436 | tf_op jit(solution)/shard_map/dot_general | solution.py:93
  90.9 0.0 copy-start.6
  90.9 0.9 all_to_all.37
  91.8 4.7 %all-to-all-start.3 = ((bf16[64,2,1792]{2,1,0:T(2,128)(2,1)}), bf16[64,2,1792]{2,1,0:T(2,128)(2,1)S(1)}, u32[]{:S(2)}, u32[]{:S(2)}) async-start(bf16[64,2,1792]{2,1,0:T(2,128)(2,1)} %all_to_all.37), calls=%async_computation.3 | async-start | bytes 917504 | tf_op jit(solution)/shard_map/all_to_all | solution.py:94
  96.6 0.0 copy-done.6
  96.6 0.1 reduce_sum.71
  96.7 0.1 fusion.39
  96.8 0.1 select_reduce_fusion
  96.9 12.8 %all-to-all-done.3 = bf16[64,2,1792]{2,1,0:T(2,128)(2,1)S(1)} async-done(((bf16[64,2,1792]{2,1,0:T(2,128)(2,1)}), bf16[64,2,1792]{2,1,0:T(2,128)(2,1)S(1)}, u32[]{:S(2)}, u32[]{:S(2)}) %all-to-all-start.3) | async-done | bytes 458784 | tf_op jit(solution)/shard_map/all_to_all | solution.py:94
  109.7 0.2 all_to_all.39
  109.9 0.8 fusion.14
  (6 shorter events, 0.1 us)
Async XLA Ops:
  0.0 1.1 copy-start
  0.0 3.0 %copy-start.1 = (bf16[8,128,576]{1,2,0:T(8,128)(2,1)S(1)}, bf16[8,128,576]{1,2,0:T(8,128)(2,1)}, u32[]{:S(2)}) copy-start(bf16[8,128,576]{1,2,0:T(8,128)(2,1)} %param.14) | copy-start | bytes 3538948
  3.0 26.0 %copy-start.2 = (bf16[1,128,1792]{2,1,0:T(8,128)(2,1)S(1)}, bf16[1,128,1792]{2,1,0:T(8,128)(2,1)}, u32[]{:S(2)}) copy-start(bf16[1,128,1792]{2,1,0:T(8,128)(2,1)} %param.17) | copy-start | bytes 1376260
  3.0 26.0 %copy-start.3 = (bf16[512,1,128]{2,0,1:T(8,128)(2,1)S(1)}, bf16[512,1,128]{2,0,1:T(8,128)(2,1)}, u32[]{:S(2)}) copy-start(bf16[512,1,128]{2,0,1:T(8,128)(2,1)} %param.16) | copy-start | bytes 393220
  31.4 4.9 %copy-start.5 = (s32[8,8]{1,0:T(8,128)S(1)}, s32[8,8]{1,0:T(8,128)}, u32[]{:S(2)}) copy-start(s32[8,8]{1,0:T(8,128)} %param.19) | copy-start | bytes 772
  31.4 5.4 %copy-start.7 = (f32[3584]{0:T(1024)S(1)}, f32[3584]{0:T(1024)}, u32[]{:S(2)}) copy-start(f32[3584]{0:T(1024)} %param.18) | copy-start | bytes 43012
  31.4 30.7 %all-to-all-start.1 = ((bf16[64,8,1792]{2,1,0:T(8,128)(2,1)}), bf16[64,8,1792]{2,1,0:T(8,128)(2,1)S(1)}, u32[]{:S(2)}, u32[]{:S(2)}) async-start(bf16[64,8,1792]{2,1,0:T(8,128)(2,1)} %fusion.10), calls=%async_computation.1 | async-start | bytes 3670016 | tf_op jit(solution)/shard_map/all_to_all | solution.py:57
  36.2 26.2 %copy-start.4 = (bf16[8,3584]{1,0:T(8,128)(2,1)S(1)}, bf16[8,3584]{1,0:T(8,128)(2,1)}, u32[]{:S(2)}) copy-start(bf16[8,3584]{1,0:T(8,128)(2,1)} %param.12) | copy-start | bytes 172036
  85.8 2.0 %collective-permute-start = (bf16[128,2176]{1,0:T(8,128)(2,1)S(1)}, bf16[128,2176]{1,0:T(8,128)(2,1)S(1)}, u32[]{:S(2)}, u32[]{:S(2)}) collective-permute-start(bf16[128,2176]{1,0:T(8,128)(2,1)S(1)} %pad_maximum_fusion), channel_id=1, source_target_pairs={{0,64},{64,0},{1,65},{65,1},{2,66},{66,2},{3,67},{67,3},{4,68},{68... | collective-permute-start | bytes 1671176 | tf_op jit(solution)/shard_map/ppermute | solution.py:87
  90.9 5.7 %copy-start.6 = (f32[8,8]{1,0:T(8,128)S(1)}, f32[8,8]{1,0:T(8,128)}, u32[]{:S(2)}) copy-start(f32[8,8]{1,0:T(8,128)} %param.20) | copy-start | bytes 772
  91.8 17.9 %all-to-all-start.3 = ((bf16[64,2,1792]{2,1,0:T(2,128)(2,1)}), bf16[64,2,1792]{2,1,0:T(2,128)(2,1)S(1)}, u32[]{:S(2)}, u32[]{:S(2)}) async-start(bf16[64,2,1792]{2,1,0:T(2,128)(2,1)} %all_to_all.37), calls=%async_computation.3 | async-start | bytes 917504 | tf_op jit(solution)/shard_map/all_to_all | solution.py:94

commit v2 on v1

v2 whole, which is shorter than its diff:
```python
import functools

import jax
import jax.numpy as jnp
import numpy as np
from jax import lax
from jax.experimental import pallas as pl
from jax.experimental.pallas import tpu as pltpu
from jax.sharding import PartitionSpec as P

softmax_scale = 0.07216878364870323
bf16 = jnp.bfloat16
f32 = jnp.float32


def split_terms(value):
    first = lax.reduce_precision(value, 8, 7)
    rest = value - first
    second = lax.reduce_precision(rest, 8, 7)
    third = rest - second
    return jnp.stack([first, second, third], axis=-1).astype(bf16)


MIB = 1024 * 1024
in_vmem = pl.BlockSpec(memory_space=pltpu.VMEM)
in_smem = pl.BlockSpec(memory_space=pltpu.SMEM)
in_hbm = pl.BlockSpec(memory_space=pltpu.HBM)


def keep_hbm(value):
    return pltpu.with_memory_space_constraint(value, pltpu.HBM)


def visit_order(n_dev):
    return list(range(n_dev))[::-1]


def attend_kernel(
    role, lengths, query, cache, sort, sent, queries, caches, sorts, valid, staged, done
):
    heads = query.shape[1]
    block = sent.shape[1]
    run = queries.shape[1]
    latent_width = sent.shape[0] * block // (heads * 2 * run)
    chunks = latent_width // block
    loads = [
        pltpu.make_async_copy(lengths, valid, done.at[0]),
        pltpu.make_async_copy(sort, sorts, done.at[1]),
    ]
    for p in range(2):
        first = p * 2 * run + role[0] * run
        loads.append(pltpu.make_async_copy(query.at[pl.ds(first, run)], queries.at[p], done.at[2 + p]))
        loads.append(pltpu.make_async_copy(cache.at[pl.ds(first, run)], caches.at[p], done.at[4 + p]))
    for copy in loads:
        copy.start()
    for copy in loads:
        copy.wait()
    rows = run * chunks * 2
    tokens = [(p, k) for p in range(2) for k in range(run)]
    scores = [
        jnp.dot(queries[p, k], caches[p, k], preferred_element_type=f32) * softmax_scale
        for p, k in tokens
    ]
    position = lax.broadcasted_iota(jnp.int32, scores[0].shape, 1)
    usable = [position < valid[p * 2 * run + role[0] * run + k] for p, k in tokens]
    scores = [jnp.where(u, x, -1e30) for u, x in zip(usable, scores)]
    peaks = [jnp.max(x, axis=1, keepdims=True) for x in scores]
    exponents = [jnp.where(u, jnp.exp(x - m), 0.0) for u, x, m in zip(usable, scores, peaks)]
    sums = [jnp.sum(x, axis=1, keepdims=True) for x in exponents]
    attention = [(x / total).astype(bf16) for x, total in zip(exponents, sums)]
    attention = [
        jnp.dot(sorts[p], x, preferred_element_type=f32).astype(bf16)
        for (p, k), x in zip(tokens, attention)
    ]
    contexts = [
        lax.dot_general(
            x, caches[p, k, :latent_width], (((1,), (1,)), ((), ())), preferred_element_type=f32
        )
        for (p, k), x in zip(tokens, attention)
    ]
    half = heads // 2
    for (p, k), context in zip(tokens, contexts):
        for i in range(2):
            for c in range(chunks):
                at = p * rows + k * 2 * chunks + 2 * c + i
                staged[pl.ds(at, half, stride=2 * rows)] = context[
                    i * half : (i + 1) * half, c * block : (c + 1) * block
                ]
    sent[...] = staged[...].astype(bf16)


def attend(role_index, lengths, query, cache, sort, latent_width, block):
    tokens, heads, key_width = query.shape
    positions = cache.shape[1]
    run = tokens // 4
    rows = heads * run * 2 * latent_width // block
    return pl.pallas_call(
        attend_kernel,
        out_shape=jax.ShapeDtypeStruct((rows, block), bf16),
        in_specs=[in_smem] + [in_hbm] * 4,
        out_specs=in_vmem,
        scratch_shapes=[
            pltpu.VMEM((2, run, heads, key_width), bf16),
            pltpu.VMEM((2, run, key_width, positions), bf16),
            pltpu.VMEM(sort.shape, bf16),
            pltpu.SMEM((tokens,), jnp.int32),
            pltpu.VMEM((rows, block), f32),
            pltpu.SemaphoreType.DMA((6,)),
        ],
        compiler_params=pltpu.CompilerParams(vmem_limit_bytes=8 * MIB),
        name="attend",
    )(
        role_index.reshape(1),
        keep_hbm(lengths),
        keep_hbm(query),
        keep_hbm(jnp.swapaxes(cache, 1, 2)),
        keep_hbm(sort),
    )


def values_kernel(gathered, own, pair, values, staged):
    block = gathered.shape[1]
    rows = values.shape[0]
    stride = gathered.shape[0] // rows
    staged[...] = gathered[...].astype(f32)
    for i, weights in enumerate((own, pair)):
        total = jnp.zeros((rows, block), f32)
        for c in range(stride // 2):
            part = staged[pl.ds(2 * c + i, rows, stride=stride)].astype(bf16)
            total += jnp.dot(
                part, weights[c * block : (c + 1) * block], preferred_element_type=f32
            )
        values[:, i * block : (i + 1) * block] = total.astype(bf16)


def lift_values(gathered, own, pair):
    total, block = gathered.shape
    latent_width = own.shape[0]
    rows = total * block // (2 * latent_width)
    return pl.pallas_call(
        values_kernel,
        out_shape=jax.ShapeDtypeStruct((rows, 2 * block), bf16),
        in_specs=[in_vmem] * 3,
        out_specs=in_vmem,
        scratch_shapes=[pltpu.VMEM((total, block), f32)],
        compiler_params=pltpu.CompilerParams(vmem_limit_bytes=8 * MIB),
        name="lift_values",
    )(gathered, own, pair)


def project_kernel(role, own_values, other_values, own, pair, partial, spread, source):
    rows, block = own_values.shape[0], own.shape[0]
    quarter = partial.shape[1]
    run = 2
    n_dev = rows // run
    spread[...] = jnp.zeros_like(spread)
    for place, values in ((role[0], own_values), (1 - role[0], other_values)):
        for i in range(2):
            source[...] = values[:, i * block : (i + 1) * block].astype(f32)
            for k in range(run):
                part = source[pl.ds(k, n_dev, stride=run)]
                for c in range(2):
                    at = c * 2 * run + place * run + k
                    spread[2 * c + i, pl.ds(at, n_dev, stride=4 * run)] = part
    total = jnp.zeros(partial.shape, f32)
    for c in range(2):
        columns = slice(c * quarter, (c + 1) * quarter)
        left = jnp.concatenate([spread[2 * c], spread[2 * c + 1]], axis=1).astype(bf16)
        right = jnp.concatenate([own[:, columns], pair[:, columns]], axis=0)
        total += jnp.dot(left, right, preferred_element_type=f32)
    partial[...] = total.astype(bf16)


def project(role_index, own_values, other_values, own, pair):
    rows, wide = own_values.shape
    quarter = own.shape[1] // 2
    return pl.pallas_call(
        project_kernel,
        out_shape=jax.ShapeDtypeStruct((4 * rows, quarter), bf16),
        in_specs=[in_smem] + [in_vmem] * 4,
        out_specs=in_vmem,
        scratch_shapes=[
            pltpu.VMEM((4, 4 * rows, wide // 2), f32),
            pltpu.VMEM((rows, wide // 2), f32),
        ],
        compiler_params=pltpu.CompilerParams(vmem_limit_bytes=16 * MIB),
        name="project",
    )(role_index.reshape(1), own_values, other_values, own, pair)


def lift_kernel(role, arrived, gate, up, outward, own, terms, weights, done):
    blocks, step, hidden_units = weights.shape[1:]
    half = blocks * step
    start = pl.multiple_of(role[0] * half, half)
    copies = [
        [
            pltpu.make_async_copy(
                source.at[pl.ds(start + i * step, step)], weights.at[s, i], done.at[s, i]
            )
            for i in range(blocks)
        ]
        for s, source in enumerate((gate, up))
    ]
    for part in copies:
        for copy in part:
            copy.start()
    outward[:, 2 * hidden_units :] = arrived[:, half:]
    terms[...] = arrived[:, half:].astype(f32)
    for s, part in enumerate(copies):
        columns = slice(s * hidden_units, (s + 1) * hidden_units)
        for i, copy in enumerate(part):
            copy.wait()
            product = jnp.dot(
                arrived[:, i * step : (i + 1) * step], weights[s, i], preferred_element_type=f32
            )
            own[:, columns] = product if i == 0 else own[:, columns] + product
        outward[:, columns] = own[:, columns].astype(bf16)


def lift_rows(role_index, arrived, gate, up):
    half, hidden_units = gate.shape[0] // 2, gate.shape[1]
    rows, extra = arrived.shape[0], arrived.shape[1] - half
    step = 256
    blocks = half // step
    return pl.pallas_call(
        lift_kernel,
        out_shape=[
            jax.ShapeDtypeStruct((rows, 2 * hidden_units + extra), bf16),
            jax.ShapeDtypeStruct((rows, 2 * hidden_units), f32),
            jax.ShapeDtypeStruct((rows, extra), f32),
        ],
        in_specs=[in_smem, in_vmem, in_hbm, in_hbm],
        out_specs=[in_vmem] * 3,
        scratch_shapes=[
            pltpu.VMEM((2, blocks, step, hidden_units), bf16),
            pltpu.SemaphoreType.DMA((2, blocks)),
        ],
        compiler_params=pltpu.CompilerParams(vmem_limit_bytes=20 * MIB),
        name="lift_rows",
    )(role_index.reshape(1), arrived, keep_hbm(gate), keep_hbm(up))


def lower_kernel(width, role, own, inward, terms, down, produced, weights, total, done):
    blocks, step, half = weights.shape
    hidden_units = blocks * step
    copies = [
        pltpu.make_async_copy(
            down.at[pl.ds(i * step, step), pl.ds(pl.multiple_of(role[0] * half, half), half)],
            weights.at[i],
            done.at[i],
        )
        for i in range(blocks)
    ]
    for copy in copies:
        copy.start()
    squares = jnp.sum(
        terms[...] + inward[:, 2 * hidden_units :].astype(f32), axis=1, keepdims=True
    )
    scale = lax.rsqrt(squares / width + 1e-06)
    for i, copy in enumerate(copies):
        gate_at = slice(i * step, (i + 1) * step)
        up_at = slice(hidden_units + i * step, hidden_units + (i + 1) * step)
        gate_part = (own[:, gate_at] + inward[:, gate_at].astype(f32)) * scale
        up_part = (own[:, up_at] + inward[:, up_at].astype(f32)) * scale
        inner = (gate_part / (1.0 + jnp.exp(-gate_part)) * up_part).astype(bf16)
        copy.wait()
        product = jnp.dot(inner, weights[i], preferred_element_type=f32)
        total[...] = product if i == 0 else total[...] + product
    produced[...] = total[...].astype(bf16).reshape(produced.shape)


def lower_rows(role_index, width, own, inward, terms, down, capacity):
    rows, hidden_units, half = own.shape[0], down.shape[0], down.shape[1] // 2
    step = 256
    return pl.pallas_call(
        functools.partial(lower_kernel, width),
        out_shape=jax.ShapeDtypeStruct((rows, half), bf16),
        in_specs=[in_smem] + [in_vmem] * 3 + [in_hbm],
        out_specs=in_vmem,
        scratch_shapes=[
            pltpu.VMEM((hidden_units // step, step, half), bf16),
            pltpu.VMEM((rows, half), f32),
            pltpu.SemaphoreType.DMA((hidden_units // step,)),
        ],
        compiler_params=pltpu.CompilerParams(vmem_limit_bytes=16 * MIB),
        name="lower_rows",
    )(role_index.reshape(1), own, inward, terms, keep_hbm(down))


def local(
    resid,
    query,
    cache,
    lengths,
    w_uv,
    w_out,
    norm_gain,
    expert_ids,
    gate_scores,
    w_gate,
    w_up,
    w_down,
):
    role_index = lax.axis_index("role")
    tok_dev, width = resid.shape
    half_width = w_out.shape[2]
    latent_width = w_uv.shape[0]
    n_dev = lax.axis_size("dev")
    top_count = expert_ids.shape[1]
    capacity = max(2, tok_dev * top_count * 2 // n_dev)
    slots = n_dev * capacity
    swap = [(0, 1), (1, 0)]

    pairs = n_dev // 2
    quarter = half_width // 2
    order = visit_order(n_dev)
    exchange = functools.partial(
        lax.all_to_all,
        axis_name="dev",
        split_axis=0,
        concat_axis=0,
        axis_index_groups=[order],
        tiled=True,
    )
    neighbour = [(d, d ^ 1) for d in range(n_dev)]
    wanted = np.zeros((2, n_dev, n_dev), np.float32)
    for p in range(2):
        for i in range(2):
            for g in range(pairs):
                wanted[p, i * pairs + g, order[2 * g + p] ^ i] = 1.0
    own_out, own_lift = w_out[0], w_uv[:, 0]
    pair_out = lax.ppermute(own_out, "dev", neighbour)
    pair_lift = lax.ppermute(own_lift, "dev", neighbour)
    sent = attend(
        role_index,
        lengths,
        query,
        cache,
        jnp.asarray(wanted, bf16),
        latent_width,
        own_lift.shape[1],
    )
    gathered = exchange(sent.reshape(n_dev, -1, sent.shape[1]))
    gathered, pair_out, pair_lift = lax.optimization_barrier((gathered, pair_out, pair_lift))
    own_values = lift_values(gathered.reshape(sent.shape), own_lift, pair_lift)
    other_values = lax.ppermute(own_values, "role", swap)
    partial = project(role_index, own_values, other_values, own_out, pair_out)
    pieces = exchange(partial.reshape(n_dev, tok_dev, quarter))
    sums = jnp.sum(pieces.reshape(pairs, 2, tok_dev, quarter).astype(f32), axis=0)
    attended = (
        sums.reshape(2, 2, tok_dev // 2, quarter).transpose(0, 2, 1, 3).reshape(tok_dev, half_width)
    )

    own_resid = lax.dynamic_slice_in_dim(resid, role_index * half_width, half_width, 1)
    own_gain = lax.dynamic_slice_in_dim(norm_gain, role_index * half_width, half_width, 0)
    hidden = own_resid.astype(f32) + attended
    squares = split_terms(jnp.sum(hidden * hidden, axis=-1))
    rows = jnp.concatenate(
        [(hidden * own_gain).astype(bf16), squares, jnp.zeros((tok_dev, 125), bf16)], axis=1
    )

    flat_ids = expert_ids.reshape(-1)
    onehot = (flat_ids[:, None] == jnp.arange(n_dev, dtype=jnp.int32)[None, :]).astype(jnp.int32)
    slot_rank = jnp.sum((jnp.cumsum(onehot, axis=0) - 1) * onehot, axis=1)
    rank_of = np.zeros((n_dev,), np.int32)
    rank_of[order] = np.arange(n_dev, dtype=np.int32)
    expert_place = jnp.sum(onehot * jnp.asarray(rank_of)[None, :], axis=1)
    placed = (expert_place * capacity + slot_rank).reshape(tok_dev, top_count)
    slot_ids = jnp.arange(slots, dtype=jnp.int32)
    lookup = jnp.any(slot_ids[:, None, None] == placed[None, :, :], axis=-1).astype(bf16)
    packed = jnp.dot(lookup, rows, preferred_element_type=f32).astype(bf16)
    arrived = exchange(packed)

    outward, own_sums, square_terms = lift_rows(role_index, arrived, w_gate[0], w_up[0])
    inward = lax.ppermute(outward, "role", swap)
    produced = lower_rows(role_index, width, own_sums, inward, square_terms, w_down[0], capacity)
    returned = exchange(produced)

    gate_weights = (2.5 * gate_scores / jnp.sum(gate_scores, axis=-1, keepdims=True)).astype(bf16)
    spread = jnp.where(
        slot_ids[None, None, :] == placed[:, :, None], gate_weights.astype(f32)[:, :, None], 0.0
    )
    combine_weights = jnp.sum(spread, axis=1).astype(bf16)
    combined = jnp.dot(combine_weights, returned, preferred_element_type=f32)
    return (hidden + combined).astype(bf16)


def solution(mesh):
    return jax.shard_map(
        local,
        mesh=mesh,
        in_specs=(
            P("dev", None),
            P("dev", None, None),
            P("dev", None, None),
            P("dev"),
            P(None, "dev", None),
            P("dev", None, "role"),
            P(),
            P("dev", None),
            P("dev", None),
            P("dev", None, None),
            P("dev", None, None),
            P("dev", None, None),
        ),
        out_specs=P("dev", "role"),
        check_vma=False,
    )
```

time: 111 us -> 98.1 us (0.88)
  starting transfers between devices: 9.69 us -> 35.8 us
  blocking collectives: 41.4 us -> 17.1 us
  waiting for transfers between devices: 39.9 us -> 25.6 us
  matrix products: 14.4 us -> 1.14 us
  Pallas kernels: 0 us -> 10.8 us
  local copies, waits for them, and re-layouts: 2.5 us -> 5.31 us
    all_to_all x2 -> x1, blocking collectives: 41.4 us -> 17.1 us  [local(): arrived = exchange(packed)]
    all_to_all x2 -> x3, starting transfers between devices: 9.6 us -> 33.1 us  [the longest x1 12.5 us: local(): gathered = exchange(sent.reshape(n_dev, -1, sent.shape[1]))]
    all_to_all x2 -> x3, waiting for transfers between devices: 38 us -> 16.9 us  [the longest x1 9.25 us: local(): pieces = exchange(partial.reshape(n_dev, tok_dev, quarter))]
    dot_general x6 -> x0, matrix products: 13.3 us -> none  [the longest x1 2.84 us: local(): produced = jnp.dot(inner, own_down, preferred_element_type=f32).astype(bf16)]
    pallas_call x0 -> x5, Pallas kernels: none -> 10.8 us  [the longest x1 3.44 us: lift_rows(): pl.pallas_call(lift_kernel, out_shape=[jax.ShapeDtypeStruct((rows, 2 * hi...]
    ppermute x1 -> x4, waiting for transfers between devices: 1.94 us -> 8.7 us  [the longest x1 5.51 us: local(): pair_lift = lax.ppermute(own_lift, 'dev', neighbour)]
    ppermute x1 -> x4, starting transfers between devices: 0.09 us -> 2.67 us  [the longest x1 1.57 us: local(): pair_out = lax.ppermute(own_out, 'dev', neighbour)]
    unnamed x16 -> x9, local copies, waits for them, and re-layouts: 0.28 us -> 1.94 us
  transfers between devices with their start and end apart: 3 -> 7, of which waited for: 3 -> 6; matrix products, arithmetic and copies ran while one was open for 1% -> 3% of each run, Pallas kernels for 0% -> 3%
where the time goes in v2:
time: 98.1 us; the launch traced here: 97.5 us
  starting transfers between devices  35.8 us (36%)
  waiting for transfers between devices  25.6 us (26%)
  blocking collectives  17.1 us (17%)
  Pallas kernels  10.8 us (11%)
  local copies, waits for them, and re-layouts  5.31 us (5%)
  other arithmetic  1.68 us (2%)
  matrix products  1.14 us (1%)
    all_to_all x1, blocking collectives, local(): arrived = exchange(packed)  17.1 us
    all_to_all x1, starting transfers between devices, local(): gathered = exchange(sent.reshape(n_dev, -1, sent.shape[1]))  12.5 us
    all_to_all x1, starting transfers between devices, local(): pieces = exchange(partial.reshape(n_dev, tok_dev, quarter))  10.6 us
    all_to_all x1, starting transfers between devices, local(): returned = exchange(produced)  10.1 us
    all_to_all x1, waiting for transfers between devices, local(): pieces = exchange(partial.reshape(n_dev, tok_dev, quarter))  9.25 us
    all_to_all x1, waiting for transfers between devices, local(): returned = exchange(produced)  7.49 us
    ppermute x1, waiting for transfers between devices, local(): pair_lift = lax.ppermute(own_lift, 'dev', neighbour)  5.51 us
    pallas_call x1, Pallas kernels, lift_rows(): pl.pallas_call(lift_kernel, out_shape=[jax.ShapeDtypeStruct((rows, 2 * hi...  3.44 us
  transfers between devices with their start and end apart: 7, of which 6 were waited for; matrix products, arithmetic and copies ran while one was open for 3% of the time, Pallas kernels for 3%

profile of v2, /device:TPU:0, one launch (start us, length us, event | category | flops | bytes accessed | tf_op | source)
XLA Modules:
  0.0 97.5 jit_solution(1897288238964093571)
XLA Ops:
  0.0 0.0 copy-start.2
  0.0 1.6 %collective-permute-start = (bf16[128,1792]{1,0:T(8,128)(2,1)}, bf16[128,1792]{1,0:T(8,128)(2,1)S(1)}, u32[]{:S(2)}, u32[]{:S(2)}) collective-permute-start(bf16[128,1792]{1,0:T(8,128)(2,1)} %bitcast.24), channel_id=1, source_target_pairs={{0,1},{1,0},{2,3},{3,2},{4,5},{5,4},{6,7},{7,6},{8,9},{9,8},{10,11... | collective-permute-start | bytes 1376264 | tf_op jit(solution)/shard_map/ppermute | solution.py:332
  1.6 3.0 %attend.1 = bf16[1024,128]{1,0:T(8,128)(2,1)} custom-call(s32[1]{0:T(128)} %bitcast.role, s32[8]{0:T(128)} %lengths.1, bf16[8,64,576]{2,1,0:T(8,128)(2,1)} %query.1, bf16[8,576,128]{2,1,0:T(8,128)(2,1)} %bitcast.32, bf16[2,64,64]{2,1,0:T(8,128)(2,1)} %constant.34.clone.sort), custom_call_target="tpu_custom_call" | custom-call | tf_op jit(solution)/shard_map/attend/pallas_call | solution.py:97
  4.5 12.5 %all-to-all-start = ((bf16[64,16,128]{2,1,0:T(8,128)(2,1)}), bf16[64,16,128]{2,1,0:T(8,128)(2,1)S(1)}, u32[]{:S(2)}, u32[]{:S(2)}) async-start(bf16[64,16,128]{2,1,0:T(8,128)(2,1)} %bitcast.2), calls=%async_computation | async-start | bytes 524288 | tf_op jit(solution)/shard_map/all_to_all | solution.py:343
  17.1 0.9 collective-permute-start.1
  18.0 5.5 %collective-permute-done.1.pair = bf16[512,128]{1,0:T(8,128)(2,1)S(1)} collective-permute-done((bf16[512,128]{1,0:T(8,128)(2,1)}, bf16[512,128]{1,0:T(8,128)(2,1)S(1)}, u32[]{:S(2)}, u32[]{:S(2)}) %collective-permute-start.1) | collective-permute-done | bytes 131104 | tf_op jit(solution)/shard_map/ppermute | solution.py:333
  23.5 0.2 all-to-all-done
  23.7 0.0 collective-permute-done.pair
  23.7 0.0 copy-start.1
  23.7 0.9 copy-done.1
  24.6 0.2 lift_values.1.own_values
  24.8 0.1 collective-permute-start.2
  24.9 1.2 %collective-permute-done.2.other_values = bf16[128,256]{1,0:T(8,128)(2,1)S(1)} collective-permute-done((bf16[128,256]{1,0:T(8,128)(2,1)S(1)}, bf16[128,256]{1,0:T(8,128)(2,1)S(1)}, u32[]{:S(2)}, u32[]{:S(2)}) %collective-permute-start.2) | collective-permute-done | bytes 65568 | tf_op jit(solution)/shard_map/ppermute | solution.py:346
  26.2 0.0 copy-start
  26.2 1.0 %copy-done = bf16[1,128,1792]{2,1,0:T(8,128)(2,1)S(1)} copy-done((bf16[1,128,1792]{2,1,0:T(8,128)(2,1)S(1)}, bf16[1,128,1792]{2,1,0:T(8,128)(2,1)}, u32[]{:S(2)}) %copy-start) | copy-done | bytes 458776
  27.2 1.8 %project.1 = bf16[512,896]{1,0:T(8,128)(2,1)} custom-call(s32[1]{0:T(128)} %bitcast.role, bf16[128,256]{1,0:T(8,128)(2,1)S(1)} %lift_values.1.own_values, bf16[128,256]{1,0:T(8,128)(2,1)S(1)} %collective-permute-done.2.other_values, bf16[128,1792]{1,0:T(8,128)(2,1)S(1)} %bitcast.25, bf16[128,1792]{1,0:T(8,128)(2,1)S(1)} %collective-permute-done.pair), custom_call_target="tpu_custom_call" | custom-call | tf_op jit(solution)/shard_map/project/pallas_call | solution.py:177
  28.9 10.6 %all-to-all-start.1 = ((bf16[64,8,896]{2,1,0:T(8,128)(2,1)}), bf16[64,8,896]{2,1,0:T(8,128)(2,1)S(1)}, u32[]{:S(2)}, u32[]{:S(2)}) async-start(bf16[64,8,896]{2,1,0:T(8,128)(2,1)} %bitcast.6), calls=%async_computation.1 | async-start | bytes 1835008 | tf_op jit(solution)/shard_map/all_to_all | solution.py:348
  39.5 0.8 eq.42
  40.3 0.1 fusion.1
  40.4 0.1 reduce_window_sum.11
  40.4 0.8 select_reduce_fusion.2
  41.3 0.1 add.28
  41.4 0.8 dynamic_slice.7
  42.2 0.1 fusion.2
  42.3 9.3 %all-to-all-done.1 = bf16[64,8,896]{2,1,0:T(8,128)(2,1)S(1)} async-done(((bf16[64,8,896]{2,1,0:T(8,128)(2,1)}), bf16[64,8,896]{2,1,0:T(8,128)(2,1)S(1)}, u32[]{:S(2)}, u32[]{:S(2)}) %all-to-all-start.1) | async-done | bytes 917536 | tf_op jit(solution)/shard_map/all_to_all | solution.py:348
  51.5 0.1 convert_reduce_fusion
  51.7 0.0 copy-done.2
  51.7 0.1 multiply_reduce_fusion
  51.9 0.1 copy.26
  52.0 0.1 concatenate.4
  52.1 0.3 convolution_convert_fusion
  52.4 0.2 all_to_all.23
  52.6 17.1 %all_to_all.33 = bf16[64,2,1920]{2,1,0:T(2,128)(2,1)S(1)} all-to-all(bf16[64,2,1920]{2,1,0:T(2,128)(2,1)S(1)} %all_to_all.23), channel_id=1, replica_groups={{63,62,61,60,59,58,57,56,55,54,53,52,51,50,49,48,47,46,45,44,43,42,41,4..., dimensions={0} | all-to-all | bytes 983040 | tf_op jit(solution)/shard_map/all_to_all | solution.py:372
  69.7 0.2 all_to_all.25.arrived
  69.9 3.4 %lift_rows.1 = (bf16[128,2176]{1,0:T(8,128)(2,1)S(1)}, f32[128,2048]{1,0:T(8,128)S(1)}, f32[128,128]{1,0:T(8,128)S(1)}) custom-call(s32[1]{0:T(128)} %bitcast.role, bf16[128,1920]{1,0:T(8,128)(2,1)S(1)} %all_to_all.25.arrived, bf16[3584,1024]{1,0:T(8,128)(2,1)} %bitcast.28, bf16[3584,1024]{1,0:T(8,128)(2,1)} %bitcast.29), custom_call_target="tpu_custom_call" | custom-call | tf_op jit(solution)/shard_map/lift_rows/pallas_call | solution.py:225
  73.3 0.0 copy-start.3
  73.3 0.1 collective-permute-start.3
  73.4 1.9 %collective-permute-done.3.inward = bf16[128,2176]{1,0:T(8,128)(2,1)S(1)} collective-permute-done((bf16[128,2176]{1,0:T(8,128)(2,1)S(1)}, bf16[128,2176]{1,0:T(8,128)(2,1)S(1)}, u32[]{:S(2)}, u32[]{:S(2)}) %collective-permute-start.3) | collective-permute-done | bytes 557088 | tf_op jit(solution)/shard_map/ppermute | solution.py:375
  75.4 2.4 %lower_rows.1 = bf16[128,1792]{1,0:T(8,128)(2,1)S(1)} custom-call(s32[1]{0:T(128)} %bitcast.role, f32[128,2048]{1,0:T(8,128)S(1)} %get-tuple-element.14.own, bf16[128,2176]{1,0:T(8,128)(2,1)S(1)} %collective-permute-done.3.inward, f32[128,128]{1,0:T(8,128)S(1)} %get-tuple-element.16.terms, bf16[1024,3584]{1,0:T(8,128)(2,1)} %bitcast.30), custom_call_target="tpu_custom_call" | custom-call | tf_op jit(solution)/shard_map/lower_rows/pallas_call | solution.py:275
  77.7 0.9 all_to_all.26
  78.7 10.1 %all-to-all-start.3 = ((bf16[64,2,1792]{2,1,0:T(2,128)(2,1)}), bf16[64,2,1792]{2,1,0:T(2,128)(2,1)S(1)}, u32[]{:S(2)}, u32[]{:S(2)}) async-start(bf16[64,2,1792]{2,1,0:T(2,128)(2,1)} %all_to_all.26), calls=%async_computation.3 | async-start | bytes 917504 | tf_op jit(solution)/shard_map/all_to_all | solution.py:377
  88.8 0.0 copy-done.3
  88.8 0.1 reduce_sum.59
  88.9 0.1 fusion.4
  89.0 0.1 select_reduce_fusion
  89.1 7.5 %all-to-all-done.3 = bf16[64,2,1792]{2,1,0:T(2,128)(2,1)S(1)} async-done(((bf16[64,2,1792]{2,1,0:T(2,128)(2,1)}), bf16[64,2,1792]{2,1,0:T(2,128)(2,1)S(1)}, u32[]{:S(2)}, u32[]{:S(2)}) %all-to-all-start.3) | async-done | bytes 458784 | tf_op jit(solution)/shard_map/all_to_all | solution.py:377
  96.6 0.2 all_to_all.28
  96.7 0.8 fusion
  (6 shorter events, 0.1 us)
Async XLA Ops:
  0.0 51.7 %copy-start.2 = (bf16[8,3584]{1,0:T(8,128)(2,1)S(1)}, bf16[8,3584]{1,0:T(8,128)(2,1)}, u32[]{:S(2)}) copy-start(bf16[8,3584]{1,0:T(8,128)(2,1)} %param.14) | copy-start | bytes 172036
  0.0 23.7 %collective-permute-start = (bf16[128,1792]{1,0:T(8,128)(2,1)}, bf16[128,1792]{1,0:T(8,128)(2,1)S(1)}, u32[]{:S(2)}, u32[]{:S(2)}) collective-permute-start(bf16[128,1792]{1,0:T(8,128)(2,1)} %bitcast.24), channel_id=1, source_target_pairs={{0,1},{1,0},{2,3},{3,2},{4,5},{5,4},{6,7},{7,6},{8,9},{9,8},{10,11... | collective-permute-start | bytes 1376264 | tf_op jit(solution)/shard_map/ppermute | solution.py:332
  4.5 19.1 %all-to-all-start = ((bf16[64,16,128]{2,1,0:T(8,128)(2,1)}), bf16[64,16,128]{2,1,0:T(8,128)(2,1)S(1)}, u32[]{:S(2)}, u32[]{:S(2)}) async-start(bf16[64,16,128]{2,1,0:T(8,128)(2,1)} %bitcast.2), calls=%async_computation | async-start | bytes 524288 | tf_op jit(solution)/shard_map/all_to_all | solution.py:343
  17.1 6.4 %collective-permute-start.1 = (bf16[512,128]{1,0:T(8,128)(2,1)}, bf16[512,128]{1,0:T(8,128)(2,1)S(1)}, u32[]{:S(2)}, u32[]{:S(2)}) collective-permute-start(bf16[512,128]{1,0:T(8,128)(2,1)} %bitcast.26), channel_id=1, source_target_pairs={{0,1},{1,0},{2,3},{3,2},{4,5},{5,4},{6,7},{7,6},{8,9},{9,8},{10,11... | collective-permute-start | bytes 393224 | tf_op jit(solution)/shard_map/ppermute | solution.py:333
  23.7 0.9 copy-start.1
  24.8 1.3 %collective-permute-start.2 = (bf16[128,256]{1,0:T(8,128)(2,1)S(1)}, bf16[128,256]{1,0:T(8,128)(2,1)S(1)}, u32[]{:S(2)}, u32[]{:S(2)}) collective-permute-start(bf16[128,256]{1,0:T(8,128)(2,1)S(1)} %lift_values.1.own_values), channel_id=1, source_target_pairs={{0,64},{64,0},{1,65},{65,1},{2,66},{66,2},{3,67},{67,3},{4,68},{68... | collective-permute-start | bytes 196616 | tf_op jit(solution)/shard_map/ppermute | solution.py:346
  26.2 1.0 %copy-start = (bf16[1,128,1792]{2,1,0:T(8,128)(2,1)S(1)}, bf16[1,128,1792]{2,1,0:T(8,128)(2,1)}, u32[]{:S(2)}) copy-start(bf16[1,128,1792]{2,1,0:T(8,128)(2,1)} %param.19) | copy-start | bytes 1376260
  28.9 22.6 %all-to-all-start.1 = ((bf16[64,8,896]{2,1,0:T(8,128)(2,1)}), bf16[64,8,896]{2,1,0:T(8,128)(2,1)S(1)}, u32[]{:S(2)}, u32[]{:S(2)}) async-start(bf16[64,8,896]{2,1,0:T(8,128)(2,1)} %bitcast.6), calls=%async_computation.1 | async-start | bytes 1835008 | tf_op jit(solution)/shard_map/all_to_all | solution.py:348
  73.3 15.4 %copy-start.3 = (f32[8,8]{1,0:T(8,128)S(1)}, f32[8,8]{1,0:T(8,128)}, u32[]{:S(2)}) copy-start(f32[8,8]{1,0:T(8,128)} %param.22) | copy-start | bytes 772
  73.3 2.0 %collective-permute-start.3 = (bf16[128,2176]{1,0:T(8,128)(2,1)S(1)}, bf16[128,2176]{1,0:T(8,128)(2,1)S(1)}, u32[]{:S(2)}, u32[]{:S(2)}) collective-permute-start(bf16[128,2176]{1,0:T(8,128)(2,1)S(1)} %get-tuple-element.15), channel_id=1, source_target_pairs={{0,64},{64,0},{1,65},{65,1},{2,66},{66,2},{3,67},{67,3},{4,68},{68... | collective-permute-start | bytes 1671176 | tf_op jit(solution)/shard_map/ppermute | solution.py:375
  78.7 17.9 %all-to-all-start.3 = ((bf16[64,2,1792]{2,1,0:T(2,128)(2,1)}), bf16[64,2,1792]{2,1,0:T(2,128)(2,1)S(1)}, u32[]{:S(2)}, u32[]{:S(2)}) async-start(bf16[64,2,1792]{2,1,0:T(2,128)(2,1)} %all_to_all.26), calls=%async_computation.3 | async-start | bytes 917504 | tf_op jit(solution)/shard_map/all_to_all | solution.py:377

commit v3 on v2

--- a/solution.py
+++ b/solution.py
@@ -13,14 +13,6 @@
 f32 = jnp.float32
 
 
-def split_terms(value):
-    first = lax.reduce_precision(value, 8, 7)
-    rest = value - first
-    second = lax.reduce_precision(rest, 8, 7)
-    third = rest - second
-    return jnp.stack([first, second, third], axis=-1).astype(bf16)
-
-
 MIB = 1024 * 1024
 in_vmem = pl.BlockSpec(memory_space=pltpu.VMEM)
 in_smem = pl.BlockSpec(memory_space=pltpu.SMEM)
@@ -36,8 +28,43 @@
 
 
 def attend_kernel(
-    role, lengths, query, cache, sort, sent, queries, caches, sorts, valid, staged, done
+    role,
+    lengths,
+    query,
+    cache,
+    sort,
+    w_uv,
+    w_out,
+    resid,
+    ids_in,
+    scores_in,
+    places_in,
+    sent,
+    own_lift,
+    own_out,
+    own_resid,
+    taken,
+    combine,
+    queries,
+    caches,
+    sorts,
+    valid,
+    ids,
+    gates,
+    places,
+    staged,
+    done,
 ):
+    half_width = own_resid.shape[1]
+    start = pl.multiple_of(role[0] * half_width, half_width)
+    moves = [
+        pltpu.make_async_copy(ids_in, ids, done.at[6]),
+        pltpu.make_async_copy(scores_in, gates, done.at[7]),
+        pltpu.make_async_copy(places_in, places, done.at[8]),
+        pltpu.make_async_copy(w_uv, own_lift, done.at[9]),
+        pltpu.make_async_copy(w_out, own_out, done.at[10]),
+        pltpu.make_async_copy(resid.at[:, pl.ds(start, half_width)], own_resid, done.at[11]),
+    ]
     heads = query.shape[1]
     block = sent.shape[1]
     run = queries.shape[1]
@@ -51,7 +78,7 @@
         first = p * 2 * run + role[0] * run
         loads.append(pltpu.make_async_copy(query.at[pl.ds(first, run)], queries.at[p], done.at[2 + p]))
         loads.append(pltpu.make_async_copy(cache.at[pl.ds(first, run)], caches.at[p], done.at[4 + p]))
-    for copy in loads:
+    for copy in loads + moves:
         copy.start()
     for copy in loads:
         copy.wait()
@@ -87,34 +114,82 @@
                     i * half : (i + 1) * half, c * block : (c + 1) * block
                 ]
     sent[...] = staged[...].astype(bf16)
-
-
-def attend(role_index, lengths, query, cache, sort, latent_width, block):
+    for copy in moves:
+        copy.wait()
+    choose(ids, gates, places, taken, combine)
+
+
+def choose(ids, gates, places, taken, combine):
+    tokens, top_count = ids.shape
+    slots = places.shape[1]
+    weights = (2.5 * gates[...] / jnp.sum(gates[...], axis=1, keepdims=True)).astype(bf16)
+    weights = weights.astype(f32)
+    expert = jnp.broadcast_to(places[0:1], (tokens, slots))
+    chosen = jnp.zeros((tokens, slots), f32)
+    weight = jnp.zeros((tokens, slots), f32)
+    for k in range(top_count):
+        match = (ids[:, k : k + 1] == expert).astype(f32)
+        chosen += match
+        weight += match * weights[:, k : k + 1]
+    row = lax.broadcasted_iota(jnp.int32, (tokens, slots), 0)
+    rank = jnp.zeros((tokens, slots), f32)
+    for t in range(tokens - 1):
+        rank += jnp.where(row > t, jnp.broadcast_to(chosen[t : t + 1], (tokens, slots)), 0.0)
+    held = jnp.where(rank == places[1:2].astype(f32), chosen, 0.0)
+    taken[...] = held.astype(bf16)
+    combine[...] = (held * weight).astype(bf16)
+
+
+def attend(role_index, lengths, query, cache, sort, w_uv, w_out, resid, ids, gates, places):
+    latent_width, block = w_uv.shape
+    half_width = w_out.shape[1]
+    slots = places.shape[1]
     tokens, heads, key_width = query.shape
     positions = cache.shape[1]
     run = tokens // 4
     rows = heads * run * 2 * latent_width // block
     return pl.pallas_call(
         attend_kernel,
-        out_shape=jax.ShapeDtypeStruct((rows, block), bf16),
-        in_specs=[in_smem] + [in_hbm] * 4,
-        out_specs=in_vmem,
+        out_shape=[
+            jax.ShapeDtypeStruct((rows, block), bf16),
+            jax.ShapeDtypeStruct(w_uv.shape, bf16),
+            jax.ShapeDtypeStruct(w_out.shape, bf16),
+            jax.ShapeDtypeStruct((tokens, half_width), bf16),
+            jax.ShapeDtypeStruct((tokens, slots), bf16),
+            jax.ShapeDtypeStruct((tokens, slots), bf16),
+        ],
+        in_specs=[in_smem] + [in_hbm] * 10,
+        out_specs=[in_vmem] * 6,
         scratch_shapes=[
             pltpu.VMEM((2, run, heads, key_width), bf16),
             pltpu.VMEM((2, run, key_width, positions), bf16),
             pltpu.VMEM(sort.shape, bf16),
             pltpu.SMEM((tokens,), jnp.int32),
+            pltpu.VMEM(ids.shape, jnp.int32),
+            pltpu.VMEM(gates.shape, f32),
+            pltpu.VMEM(places.shape, jnp.int32),
             pltpu.VMEM((rows, block), f32),
-            pltpu.SemaphoreType.DMA((6,)),
+            pltpu.SemaphoreType.DMA((12,)),
         ],
         compiler_params=pltpu.CompilerParams(vmem_limit_bytes=8 * MIB),
         name="attend",
     )(
         role_index.reshape(1),
-        keep_hbm(lengths),
-        keep_hbm(query),
-        keep_hbm(jnp.swapaxes(cache, 1, 2)),
-        keep_hbm(sort),
+        *(
+            keep_hbm(value)
+            for value in (
+                lengths,
+                query,
+                jnp.swapaxes(cache, 1, 2),
+                sort,
+                w_uv,
+                w_out,
+                resid,
+                ids,
+                gates,
+                places,
+            )
+        ),
     )
 
 
@@ -135,8 +210,7 @@
 
 def lift_values(gathered, own, pair):
     total, block = gathered.shape
-    latent_width = own.shape[0]
-    rows = total * block // (2 * latent_width)
+    rows = total * block // (2 * own.shape[0])
     return pl.pallas_call(
         values_kernel,
         out_shape=jax.ShapeDtypeStruct((rows, 2 * block), bf16),
@@ -188,6 +262,51 @@
     )(role_index.reshape(1), own_values, other_values, own, pair)
 
 
+def settle_kernel(role, pieces, resid, gain, taken, hidden, packed, staged):
+    tokens, half = hidden.shape
+    quarter = pieces.shape[1]
+    group = 2 * tokens
+    total = jnp.zeros((group, quarter), f32)
+    for g in range(pieces.shape[0] // group):
+        total += pieces[g * group : (g + 1) * group].astype(f32)
+    staged[...] = total
+    run = tokens // 2
+    for p in range(2):
+        for c in range(2):
+            hidden[p * run : (p + 1) * run, c * quarter : (c + 1) * quarter] = staged[
+                p * tokens + c * run : p * tokens + (c + 1) * run
+            ]
+    own = hidden[...] + resid[...].astype(f32)
+    hidden[...] = own
+    square = jnp.sum(own * own, axis=1, keepdims=True)
+    first = square.astype(bf16).astype(f32)
+    second = (square - first).astype(bf16).astype(f32)
+    third = square - first - second
+    lane = lax.broadcasted_iota(jnp.int32, (tokens, packed.shape[1] - half), 1)
+    terms = jnp.where(lane == 0, first, jnp.where(lane == 1, second, third))
+    terms = jnp.where(lane < 3, terms, 0.0)
+    rows = jnp.concatenate([own * gain[pl.ds(role[0], 1)], terms], axis=1).astype(bf16)
+    packed[...] = lax.dot_general(
+        taken[...], rows, (((0,), (0,)), ((), ())), preferred_element_type=f32
+    ).astype(bf16)
+
+
+def settle(role_index, pieces, resid, gain, taken):
+    tokens, half = resid.shape
+    return pl.pallas_call(
+        settle_kernel,
+        out_shape=[
+            jax.ShapeDtypeStruct((tokens, half), f32),
+            jax.ShapeDtypeStruct((taken.shape[1], half + 128), bf16),
+        ],
+        in_specs=[in_smem] + [in_vmem] * 4,
+        out_specs=[in_vmem] * 2,
+        scratch_shapes=[pltpu.VMEM((2 * tokens, pieces.shape[1]), f32)],
+        compiler_params=pltpu.CompilerParams(vmem_limit_bytes=8 * MIB),
+        name="settle",
+    )(role_index.reshape(1), pieces, resid, gain, taken)
+
+
 def lift_kernel(role, arrived, gate, up, outward, own, terms, weights, done):
     blocks, step, hidden_units = weights.shape[1:]
     half = blocks * step
@@ -304,11 +423,8 @@
     role_index = lax.axis_index("role")
     tok_dev, width = resid.shape
     half_width = w_out.shape[2]
-    latent_width = w_uv.shape[0]
     n_dev = lax.axis_size("dev")
-    top_count = expert_ids.shape[1]
-    capacity = max(2, tok_dev * top_count * 2 // n_dev)
-    slots = n_dev * capacity
+    capacity = max(2, tok_dev * expert_ids.shape[1] * 2 // n_dev)
     swap = [(0, 1), (1, 0)]
 
     pairs = n_dev // 2
@@ -328,47 +444,31 @@
         for i in range(2):
             for g in range(pairs):
                 wanted[p, i * pairs + g, order[2 * g + p] ^ i] = 1.0
-    own_out, own_lift = w_out[0], w_uv[:, 0]
-    pair_out = lax.ppermute(own_out, "dev", neighbour)
-    pair_lift = lax.ppermute(own_lift, "dev", neighbour)
-    sent = attend(
+    places = np.stack([np.repeat(order, capacity), np.tile(np.arange(capacity), n_dev)])
+    pair_out = lax.ppermute(w_out[0], "dev", neighbour)
+    pair_lift = lax.ppermute(w_uv[:, 0], "dev", neighbour)
+    sent, own_lift, own_out, own_resid, taken, combine_weights = attend(
         role_index,
         lengths,
         query,
         cache,
         jnp.asarray(wanted, bf16),
-        latent_width,
-        own_lift.shape[1],
+        w_uv[:, 0],
+        w_out[0],
+        resid,
+        expert_ids,
+        gate_scores,
+        jnp.asarray(places, jnp.int32),
     )
     gathered = exchange(sent.reshape(n_dev, -1, sent.shape[1]))
-    gathered, pair_out, pair_lift = lax.optimization_barrier((gathered, pair_out, pair_lift))
+    gathered, pair_out, pair_lift, gain = lax.optimization_barrier(
+        (gathered, pair_out, pair_lift, norm_gain.reshape(2, half_width))
+    )
     own_values = lift_values(gathered.reshape(sent.shape), own_lift, pair_lift)
     other_values = lax.ppermute(own_values, "role", swap)
     partial = project(role_index, own_values, other_values, own_out, pair_out)
     pieces = exchange(partial.reshape(n_dev, tok_dev, quarter))
-    sums = jnp.sum(pieces.reshape(pairs, 2, tok_dev, quarter).astype(f32), axis=0)
-    attended = (
-        sums.reshape(2, 2, tok_dev // 2, quarter).transpose(0, 2, 1, 3).reshape(tok_dev, half_width)
-    )
-
-    own_resid = lax.dynamic_slice_in_dim(resid, role_index * half_width, half_width, 1)
-    own_gain = lax.dynamic_slice_in_dim(norm_gain, role_index * half_width, half_width, 0)
-    hidden = own_resid.astype(f32) + attended
-    squares = split_terms(jnp.sum(hidden * hidden, axis=-1))
-    rows = jnp.concatenate(
-        [(hidden * own_gain).astype(bf16), squares, jnp.zeros((tok_dev, 125), bf16)], axis=1
-    )
-
-    flat_ids = expert_ids.reshape(-1)
-    onehot = (flat_ids[:, None] == jnp.arange(n_dev, dtype=jnp.int32)[None, :]).astype(jnp.int32)
-    slot_rank = jnp.sum((jnp.cumsum(onehot, axis=0) - 1) * onehot, axis=1)
-    rank_of = np.zeros((n_dev,), np.int32)
-    rank_of[order] = np.arange(n_dev, dtype=np.int32)
-    expert_place = jnp.sum(onehot * jnp.asarray(rank_of)[None, :], axis=1)
-    placed = (expert_place * capacity + slot_rank).reshape(tok_dev, top_count)
-    slot_ids = jnp.arange(slots, dtype=jnp.int32)
-    lookup = jnp.any(slot_ids[:, None, None] == placed[None, :, :], axis=-1).astype(bf16)
-    packed = jnp.dot(lookup, rows, preferred_element_type=f32).astype(bf16)
+    hidden, packed = settle(role_index, pieces.reshape(partial.shape), own_resid, gain, taken)
     arrived = exchange(packed)
 
     outward, own_sums, square_terms = lift_rows(role_index, arrived, w_gate[0], w_up[0])
@@ -376,11 +476,6 @@
     produced = lower_rows(role_index, width, own_sums, inward, square_terms, w_down[0], capacity)
     returned = exchange(produced)
 
-    gate_weights = (2.5 * gate_scores / jnp.sum(gate_scores, axis=-1, keepdims=True)).astype(bf16)
-    spread = jnp.where(
-        slot_ids[None, None, :] == placed[:, :, None], gate_weights.astype(f32)[:, :, None], 0.0
-    )
-    combine_weights = jnp.sum(spread, axis=1).astype(bf16)
     combined = jnp.dot(combine_weights, returned, preferred_element_type=f32)
     return (hidden + combined).astype(bf16)
 

time: 98.1 us -> 93.2 us (0.950)
  blocking collectives: 17.1 us -> 56.9 us
  starting transfers between devices: 35.8 us -> 15.2 us
  waiting for transfers between devices: 25.6 us -> 8.13 us
  local copies, waits for them, and re-layouts: 5.31 us -> 1.45 us
  other arithmetic: 1.68 us -> 0.63 us
    all_to_all x0 -> x2, blocking collectives: none -> 39.8 us  [the longest x1 22.3 us: local(): pieces = exchange(partial.reshape(n_dev, tok_dev, quarter))]
    all_to_all x2 -> x0, starting transfers between devices: 20.6 us -> none  [the longest x1 10.6 us: local(): pieces = exchange(partial.reshape(n_dev, tok_dev, quarter))]
    all_to_all x2 -> x0, waiting for transfers between devices: 16.7 us -> none  [the longest x1 9.25 us: local(): pieces = exchange(partial.reshape(n_dev, tok_dev, quarter))]
    unnamed x9 -> x0, local copies, waits for them, and re-layouts: 1.94 us -> none
    reduce_sum x5 -> x0, other arithmetic: 1.33 us -> none  [the longest x1 0.84 us: local(): expert_place = jnp.sum(onehot * jnp.asarray(rank_of)[None, :], axis=1)]
    pallas_call x1 -> x2, Pallas kernels: 2.95 us -> 3.43 us  [the longest x1 3.04 us: attend(): pl.pallas_call(attend_kernel, out_shape=[jax.ShapeDtypeStruct((rows, bloc...]
  transfers between devices with their start and end apart: 7 -> 5, of which waited for: 6 -> 4; matrix products, arithmetic and copies ran while one was open for 3% -> 1% of each run, Pallas kernels for 3% -> 3%
where the time goes in v3:
time: 93.2 us; the launch traced here: 92.8 us
  blocking collectives  56.9 us (61%)
  starting transfers between devices  15.2 us (16%)
  Pallas kernels  10.3 us (11%)
  waiting for transfers between devices  8.13 us (9%)
  local copies, waits for them, and re-layouts  1.45 us (2%)
    all_to_all x1, blocking collectives, local(): pieces = exchange(partial.reshape(n_dev, tok_dev, quarter))  22.3 us
    all_to_all x1, blocking collectives, local(): returned = exchange(produced)  17.5 us
    all_to_all x1, blocking collectives, local(): arrived = exchange(packed)  17.1 us
    all_to_all x1, starting transfers between devices, local(): gathered = exchange(sent.reshape(n_dev, -1, sent.shape[1]))  12.5 us
    ppermute x1, waiting for transfers between devices, local(): pair_lift = lax.ppermute(w_uv[:, 0], 'dev', neighbour)  4.78 us
    pallas_call x1, Pallas kernels, lift_rows(): pl.pallas_call(lift_kernel, out_shape=[jax.ShapeDtypeStruct((rows, 2 * hi...  3.44 us
    pallas_call x1, Pallas kernels, attend(): pl.pallas_call(attend_kernel, out_shape=[jax.ShapeDtypeStruct((rows, bloc...  3.04 us
    pallas_call x1, Pallas kernels, lower_rows(): pl.pallas_call(functools.partial(lower_kernel, width), out_shape=jax.Shap...  2.35 us
  transfers between devices with their start and end apart: 5, of which 4 were waited for; matrix products, arithmetic and copies ran while one was open for 1% of the time, Pallas kernels for 3%

profile of v3, /device:TPU:0, one launch (start us, length us, event | category | flops | bytes accessed | tf_op | source)
XLA Modules:
  0.0 92.8 jit_solution(2683874341022912839)
XLA Ops:
  0.0 1.6 %collective-permute-start = (bf16[128,1792]{1,0:T(8,128)(2,1)}, bf16[128,1792]{1,0:T(8,128)(2,1)S(1)}, u32[]{:S(2)}, u32[]{:S(2)}) collective-permute-start(bf16[128,1792]{1,0:T(8,128)(2,1)} %bitcast.20), channel_id=1, source_target_pairs={{0,1},{1,0},{2,3},{3,2},{4,5},{5,4},{6,7},{7,6},{8,9},{9,8},{10,11... | collective-permute-start | bytes 1376264 | tf_op jit(solution)/shard_map/ppermute | solution.py:448
  1.6 3.0 %attend.1 = (bf16[1024,128]{1,0:T(8,128)(2,1)}, bf16[512,128]{1,0:T(8,128)(2,1)S(1)}, bf16[128,1792]{1,0:T(8,128)(2,1)S(1)}, bf16[8,1792]{1,0:T(8,128)(2,1)S(1)}...) custom-call(s32[1]{0:T(128)} %bitcast.role, s32[8]{0:T(128)} %lengths.1, bf16[8,64,576]{2,1,0:T(8,128)(2,1)} %query.1, ...), custom_call_target="tpu_custom_call" | custom-call | tf_op jit(solution)/shard_map/attend/pallas_call | solution.py:151
  4.6 12.5 %all-to-all-start = ((bf16[64,16,128]{2,1,0:T(8,128)(2,1)}), bf16[64,16,128]{2,1,0:T(8,128)(2,1)S(1)}, u32[]{:S(2)}, u32[]{:S(2)}) async-start(bf16[64,16,128]{2,1,0:T(8,128)(2,1)} %bitcast.4), calls=%async_computation | async-start | bytes 524288 | tf_op jit(solution)/shard_map/all_to_all | solution.py:463
  17.1 0.9 %collective-permute-start.1 = (bf16[512,128]{1,0:T(8,128)(2,1)}, bf16[512,128]{1,0:T(8,128)(2,1)S(1)}, u32[]{:S(2)}, u32[]{:S(2)}) collective-permute-start(bf16[512,128]{1,0:T(8,128)(2,1)} %bitcast.23), channel_id=1, source_target_pairs={{0,1},{1,0},{2,3},{3,2},{4,5},{5,4},{6,7},{7,6},{8,9},{9,8},{10,11... | collective-permute-start | bytes 393224 | tf_op jit(solution)/shard_map/ppermute | solution.py:449
  18.1 0.7 reshape.28.gain
  18.8 4.8 %collective-permute-done.1.pair = bf16[512,128]{1,0:T(8,128)(2,1)S(1)} collective-permute-done((bf16[512,128]{1,0:T(8,128)(2,1)}, bf16[512,128]{1,0:T(8,128)(2,1)S(1)}, u32[]{:S(2)}, u32[]{:S(2)}) %collective-permute-start.1) | collective-permute-done | bytes 131104 | tf_op jit(solution)/shard_map/ppermute | solution.py:449
  23.6 0.2 all-to-all-done
  23.7 0.0 collective-permute-done.pair
  23.7 0.2 lift_values.1.own_values
  24.0 0.1 collective-permute-start.2
  24.1 1.2 %collective-permute-done.2.other_values = bf16[128,256]{1,0:T(8,128)(2,1)S(1)} collective-permute-done((bf16[128,256]{1,0:T(8,128)(2,1)S(1)}, bf16[128,256]{1,0:T(8,128)(2,1)S(1)}, u32[]{:S(2)}, u32[]{:S(2)}) %collective-permute-start.2) | collective-permute-done | bytes 65568 | tf_op jit(solution)/shard_map/ppermute | solution.py:468
  25.3 0.8 project.1
  26.2 22.3 %all_to_all.33 = bf16[64,8,896]{2,1,0:T(8,128)(2,1)S(1)} all-to-all(bf16[64,8,896]{2,1,0:T(8,128)(2,1)S(1)} %bitcast.14), channel_id=1, replica_groups={{63,62,61,60,59,58,57,56,55,54,53,52,51,50,49,48,47,46,45,44,43,42,41,4..., dimensions={0} | all-to-all | bytes 1835008 | tf_op jit(solution)/shard_map/all_to_all | solution.py:470
  48.5 0.4 settle.1
  48.9 0.2 all_to_all.23
  49.1 17.1 %all_to_all.34 = bf16[64,2,1920]{2,1,0:T(2,128)(2,1)S(1)} all-to-all(bf16[64,2,1920]{2,1,0:T(2,128)(2,1)S(1)} %all_to_all.23), channel_id=1, replica_groups={{63,62,61,60,59,58,57,56,55,54,53,52,51,50,49,48,47,46,45,44,43,42,41,4..., dimensions={0} | all-to-all | bytes 983040 | tf_op jit(solution)/shard_map/all_to_all | solution.py:472
  66.1 0.2 all_to_all.25.arrived
  66.3 3.4 %lift_rows.1 = (bf16[128,2176]{1,0:T(8,128)(2,1)S(1)}, f32[128,2048]{1,0:T(8,128)S(1)}, f32[128,128]{1,0:T(8,128)S(1)}) custom-call(s32[1]{0:T(128)} %bitcast.role, bf16[128,1920]{1,0:T(8,128)(2,1)S(1)} %all_to_all.25.arrived, bf16[3584,1024]{1,0:T(8,128)(2,1)} %bitcast.16, bf16[3584,1024]{1,0:T(8,128)(2,1)} %bitcast.17), custom_call_target="tpu_custom_call" | custom-call | tf_op jit(solution)/shard_map/lift_rows/pallas_call | solution.py:344
  69.8 0.1 collective-permute-start.3
  69.9 1.9 %collective-permute-done.3.inward = bf16[128,2176]{1,0:T(8,128)(2,1)S(1)} collective-permute-done((bf16[128,2176]{1,0:T(8,128)(2,1)S(1)}, bf16[128,2176]{1,0:T(8,128)(2,1)S(1)}, u32[]{:S(2)}, u32[]{:S(2)}) %collective-permute-start.3) | collective-permute-done | bytes 557088 | tf_op jit(solution)/shard_map/ppermute | solution.py:475
  71.8 2.4 %lower_rows.1 = bf16[128,1792]{1,0:T(8,128)(2,1)S(1)} custom-call(s32[1]{0:T(128)} %bitcast.role, f32[128,2048]{1,0:T(8,128)S(1)} %get-tuple-element.32.own, bf16[128,2176]{1,0:T(8,128)(2,1)S(1)} %collective-permute-done.3.inward, f32[128,128]{1,0:T(8,128)S(1)} %get-tuple-element.34.terms, bf16[1024,3584]{1,0:T(8,128)(2,1)} %bitcast.18), custom_call_target="tpu_custom_call" | custom-call | tf_op jit(solution)/shard_map/lower_rows/pallas_call | solution.py:394
  74.2 0.2 all_to_all.26
  74.4 17.5 %all_to_all.35 = bf16[64,2,1792]{2,1,0:T(2,128)(2,1)S(1)} all-to-all(bf16[64,2,1792]{2,1,0:T(2,128)(2,1)S(1)} %all_to_all.26), channel_id=1, replica_groups={{63,62,61,60,59,58,57,56,55,54,53,52,51,50,49,48,47,46,45,44,43,42,41,4..., dimensions={0} | all-to-all | bytes 917504 | tf_op jit(solution)/shard_map/all_to_all | solution.py:477
  91.9 0.2 all_to_all.28
  92.0 0.2 fusion
  92.2 0.6 add_convert_fusion
Async XLA Ops:
  0.0 23.7 %collective-permute-start = (bf16[128,1792]{1,0:T(8,128)(2,1)}, bf16[128,1792]{1,0:T(8,128)(2,1)S(1)}, u32[]{:S(2)}, u32[]{:S(2)}) collective-permute-start(bf16[128,1792]{1,0:T(8,128)(2,1)} %bitcast.20), channel_id=1, source_target_pairs={{0,1},{1,0},{2,3},{3,2},{4,5},{5,4},{6,7},{7,6},{8,9},{9,8},{10,11... | collective-permute-start | bytes 1376264 | tf_op jit(solution)/shard_map/ppermute | solution.py:448
  4.6 19.1 %all-to-all-start = ((bf16[64,16,128]{2,1,0:T(8,128)(2,1)}), bf16[64,16,128]{2,1,0:T(8,128)(2,1)S(1)}, u32[]{:S(2)}, u32[]{:S(2)}) async-start(bf16[64,16,128]{2,1,0:T(8,128)(2,1)} %bitcast.4), calls=%async_computation | async-start | bytes 524288 | tf_op jit(solution)/shard_map/all_to_all | solution.py:463
  17.1 6.4 %collective-permute-start.1 = (bf16[512,128]{1,0:T(8,128)(2,1)}, bf16[512,128]{1,0:T(8,128)(2,1)S(1)}, u32[]{:S(2)}, u32[]{:S(2)}) collective-permute-start(bf16[512,128]{1,0:T(8,128)(2,1)} %bitcast.23), channel_id=1, source_target_pairs={{0,1},{1,0},{2,3},{3,2},{4,5},{5,4},{6,7},{7,6},{8,9},{9,8},{10,11... | collective-permute-start | bytes 393224 | tf_op jit(solution)/shard_map/ppermute | solution.py:449
  24.0 1.3 %collective-permute-start.2 = (bf16[128,256]{1,0:T(8,128)(2,1)S(1)}, bf16[128,256]{1,0:T(8,128)(2,1)S(1)}, u32[]{:S(2)}, u32[]{:S(2)}) collective-permute-start(bf16[128,256]{1,0:T(8,128)(2,1)S(1)} %lift_values.1.own_values), channel_id=1, source_target_pairs={{0,64},{64,0},{1,65},{65,1},{2,66},{66,2},{3,67},{67,3},{4,68},{68... | collective-permute-start | bytes 196616 | tf_op jit(solution)/shard_map/ppermute | solution.py:468
  69.8 2.0 %collective-permute-start.3 = (bf16[128,2176]{1,0:T(8,128)(2,1)S(1)}, bf16[128,2176]{1,0:T(8,128)(2,1)S(1)}, u32[]{:S(2)}, u32[]{:S(2)}) collective-permute-start(bf16[128,2176]{1,0:T(8,128)(2,1)S(1)} %get-tuple-element.33), channel_id=1, source_target_pairs={{0,64},{64,0},{1,65},{65,1},{2,66},{66,2},{3,67},{67,3},{4,68},{68... | collective-permute-start | bytes 1671176 | tf_op jit(solution)/shard_map/ppermute | solution.py:475

commit v4 on v3

v4 whole, which is shorter than its diff:
```python
import functools

import jax
import jax.numpy as jnp
import numpy as np
from jax import lax
from jax.experimental import pallas as pl
from jax.experimental.pallas import tpu as pltpu
from jax.sharding import PartitionSpec as P

softmax_scale = 0.07216878364870323
bf16 = jnp.bfloat16
f32 = jnp.float32


MIB = 1024 * 1024
in_vmem = pl.BlockSpec(memory_space=pltpu.VMEM)
in_smem = pl.BlockSpec(memory_space=pltpu.SMEM)
in_hbm = pl.BlockSpec(memory_space=pltpu.HBM)


def keep_hbm(value):
    return pltpu.with_memory_space_constraint(value, pltpu.HBM)


flips = (0, 1, 4, 16)


def token_class(dev):
    x, y, z = dev & 1, (dev >> 2) & 1, (dev >> 4) & 1
    return 2 * (x ^ y) + (y ^ z)


def visit_order(n_dev):
    return sorted(range(n_dev), key=lambda dev: (token_class(dev), -dev))


def attend_kernel(
    role,
    lengths,
    query,
    cache,
    sort,
    w_uv,
    w_out,
    resid,
    ids_in,
    scores_in,
    places_in,
    sent,
    own_lift,
    own_out,
    own_resid,
    taken,
    combine,
    queries,
    caches,
    sorts,
    valid,
    ids,
    gates,
    places,
    staged,
    done,
):
    half_width = own_resid.shape[1]
    start = pl.multiple_of(role[0] * half_width, half_width)
    moves = [
        pltpu.make_async_copy(ids_in, ids, done.at[10]),
        pltpu.make_async_copy(scores_in, gates, done.at[11]),
        pltpu.make_async_copy(places_in, places, done.at[12]),
        pltpu.make_async_copy(w_uv, own_lift, done.at[13]),
        pltpu.make_async_copy(w_out, own_out, done.at[14]),
        pltpu.make_async_copy(resid.at[:, pl.ds(start, half_width)], own_resid, done.at[15]),
    ]
    classes, heads = queries.shape[:2]
    block = sent.shape[1]
    latent_width = sent.shape[0] * block // (classes * heads)
    chunks = latent_width // block
    loads = [
        pltpu.make_async_copy(lengths, valid, done.at[0]),
        pltpu.make_async_copy(sort, sorts, done.at[1]),
    ]
    for i in range(classes):
        token = 2 * i + role[0]
        loads.append(pltpu.make_async_copy(query.at[token], queries.at[i], done.at[2 + i]))
        loads.append(pltpu.make_async_copy(cache.at[token], caches.at[i], done.at[6 + i]))
    for copy in loads + moves:
        copy.start()
    for copy in loads:
        copy.wait()
    tokens = range(classes)
    scores = [
        jnp.dot(queries[i], caches[i], preferred_element_type=f32) * softmax_scale for i in tokens
    ]
    position = lax.broadcasted_iota(jnp.int32, scores[0].shape, 1)
    usable = [position < valid[2 * i + role[0]] for i in tokens]
    scores = [jnp.where(u, x, -1e30) for u, x in zip(usable, scores)]
    peaks = [jnp.max(x, axis=1, keepdims=True) for x in scores]
    exponents = [jnp.where(u, jnp.exp(x - m), 0.0) for u, x, m in zip(usable, scores, peaks)]
    sums = [jnp.sum(x, axis=1, keepdims=True) for x in exponents]
    attention = [(x / total).astype(bf16) for x, total in zip(exponents, sums)]
    attention = [
        jnp.dot(sorts[i], x, preferred_element_type=f32).astype(bf16)
        for i, x in zip(tokens, attention)
    ]
    contexts = [
        lax.dot_general(
            x, caches[i, :latent_width], (((1,), (1,)), ((), ())), preferred_element_type=f32
        )
        for i, x in zip(tokens, attention)
    ]
    for i, context in zip(tokens, contexts):
        for c in range(chunks):
            staged[pl.ds(i * heads * chunks + c, heads, stride=chunks)] = context[
                :, c * block : (c + 1) * block
            ]
    sent[...] = staged[...].astype(bf16)
    for copy in moves:
        copy.wait()
    choose(ids, gates, places, taken, combine)


def choose(ids, gates, places, taken, combine):
    tokens, top_count = ids.shape
    slots = places.shape[1]
    weights = (2.5 * gates[...] / jnp.sum(gates[...], axis=1, keepdims=True)).astype(bf16)
    weights = weights.astype(f32)
    expert = jnp.broadcast_to(places[0:1], (tokens, slots))
    chosen = jnp.zeros((tokens, slots), f32)
    weight = jnp.zeros((tokens, slots), f32)
    for k in range(top_count):
        match = (ids[:, k : k + 1] == expert).astype(f32)
        chosen += match
        weight += match * weights[:, k : k + 1]
    row = lax.broadcasted_iota(jnp.int32, (tokens, slots), 0)
    rank = jnp.zeros((tokens, slots), f32)
    for t in range(tokens - 1):
        rank += jnp.where(row > t, jnp.broadcast_to(chosen[t : t + 1], (tokens, slots)), 0.0)
    held = jnp.where(rank == places[1:2].astype(f32), chosen, 0.0)
    taken[...] = held.astype(bf16)
    combine[...] = (held * weight).astype(bf16)


def attend(role_index, lengths, query, cache, sort, w_uv, w_out, resid, ids, gates, places):
    latent_width, block = w_uv.shape
    half_width = w_out.shape[1]
    slots = places.shape[1]
    tokens, heads, key_width = query.shape
    positions = cache.shape[1]
    classes = len(flips)
    rows = heads * classes * latent_width // block
    return pl.pallas_call(
        attend_kernel,
        out_shape=[
            jax.ShapeDtypeStruct((rows, block), bf16),
            jax.ShapeDtypeStruct(w_uv.shape, bf16),
            jax.ShapeDtypeStruct(w_out.shape, bf16),
            jax.ShapeDtypeStruct((tokens, half_width), bf16),
            jax.ShapeDtypeStruct((tokens, slots), bf16),
            jax.ShapeDtypeStruct((tokens, slots), bf16),
        ],
        in_specs=[in_smem] + [in_hbm] * 10,
        out_specs=[in_vmem] * 6,
        scratch_shapes=[
            pltpu.VMEM((classes, heads, key_width), bf16),
            pltpu.VMEM((classes, key_width, positions), bf16),
            pltpu.VMEM(sort.shape, bf16),
            pltpu.SMEM((tokens,), jnp.int32),
            pltpu.VMEM(ids.shape, jnp.int32),
            pltpu.VMEM(gates.shape, f32),
            pltpu.VMEM(places.shape, jnp.int32),
            pltpu.VMEM((rows, block), f32),
            pltpu.SemaphoreType.DMA((16,)),
        ],
        compiler_params=pltpu.CompilerParams(vmem_limit_bytes=8 * MIB),
        name="attend",
    )(
        role_index.reshape(1),
        *(
            keep_hbm(value)
            for value in (
                lengths,
                query,
                jnp.swapaxes(cache, 1, 2),
                sort,
                w_uv,
                w_out,
                resid,
                ids,
                gates,
                places,
            )
        ),
    )


def values_kernel(gathered, own, *rest):
    *others, values, staged = rest
    block = gathered.shape[1]
    rows = values.shape[0]
    stride = gathered.shape[0] // rows
    chunks = own.shape[0] // block
    staged[...] = gathered[...].astype(f32)
    for i, weights in enumerate([own, *others]):
        total = jnp.zeros((rows, block), f32)
        for c in range(chunks):
            part = staged[pl.ds(i * chunks + c, rows, stride=stride)].astype(bf16)
            total += jnp.dot(
                part, weights[c * block : (c + 1) * block], preferred_element_type=f32
            )
        values[:, i * block : (i + 1) * block] = total.astype(bf16)


def lift_values(gathered, weights):
    total, block = gathered.shape
    wide = len(weights) * block
    rows = total * block // (len(weights) * weights[0].shape[0])
    return pl.pallas_call(
        values_kernel,
        out_shape=jax.ShapeDtypeStruct((rows, wide), bf16),
        in_specs=[in_vmem] * (1 + len(weights)),
        out_specs=in_vmem,
        scratch_shapes=[pltpu.VMEM((total, block), f32)],
        compiler_params=pltpu.CompilerParams(vmem_limit_bytes=8 * MIB),
        name="lift_values",
    )(gathered, *weights)


def project_kernel(role, own_values, other_values, *rest):
    *weights, partial, spread = rest
    rows, block = own_values.shape[0], weights[0].shape[0]
    for place, values in ((role[0], own_values), (1 - role[0], other_values)):
        for i in range(len(weights)):
            spread[i, pl.ds(place, rows, stride=2)] = values[
                :, i * block : (i + 1) * block
            ].astype(f32)
    total = jnp.zeros((2 * rows, partial.shape[2]), f32)
    for i, part in enumerate(weights):
        total += jnp.dot(spread[i].astype(bf16), part[...], preferred_element_type=f32)
    partial[...] = total.astype(bf16).reshape(partial.shape)


def project(role_index, own_values, other_values, weights):
    rows, wide = own_values.shape
    return pl.pallas_call(
        project_kernel,
        out_shape=jax.ShapeDtypeStruct((rows, 2, weights[0].shape[1]), bf16),
        in_specs=[in_smem] + [in_vmem] * (2 + len(weights)),
        out_specs=in_vmem,
        scratch_shapes=[pltpu.VMEM((len(weights), 2 * rows, wide // len(weights)), f32)],
        compiler_params=pltpu.CompilerParams(vmem_limit_bytes=16 * MIB),
        name="project",
    )(role_index.reshape(1), own_values, other_values, *weights)


def settle_kernel(role, pieces, resid, gain, taken, hidden, packed):
    tokens, half = hidden.shape
    rows = pieces.shape[0] * pieces.shape[1]
    token = lax.broadcasted_iota(jnp.int32, (tokens, rows), 0)
    row = lax.broadcasted_iota(jnp.int32, (tokens, rows), 1)
    span = 2 * rows // tokens
    ours = (row // span == token // 2) & (row % 2 == token % 2)
    attended = jnp.dot(
        ours.astype(bf16), pieces[...].reshape(rows, half), preferred_element_type=f32
    )
    own = attended + resid[...].astype(f32)
    hidden[...] = own
    square = jnp.sum(own * own, axis=1, keepdims=True)
    first = square.astype(bf16).astype(f32)
    second = (square - first).astype(bf16).astype(f32)
    third = square - first - second
    lane = lax.broadcasted_iota(jnp.int32, (tokens, packed.shape[2] - half), 1)
    terms = jnp.where(lane == 0, first, jnp.where(lane == 1, second, third))
    terms = jnp.where(lane < 3, terms, 0.0)
    sent = jnp.concatenate([own * gain[pl.ds(role[0], 1)], terms], axis=1).astype(bf16)
    packed[...] = lax.dot_general(
        taken[...], sent, (((0,), (0,)), ((), ())), preferred_element_type=f32
    ).astype(bf16).reshape(packed.shape)


def settle(role_index, pieces, resid, gain, taken, capacity):
    tokens, half = resid.shape
    return pl.pallas_call(
        settle_kernel,
        out_shape=[
            jax.ShapeDtypeStruct((tokens, half), f32),
            jax.ShapeDtypeStruct((taken.shape[1] // capacity, capacity, half + 128), bf16),
        ],
        in_specs=[in_smem] + [in_vmem] * 4,
        out_specs=[in_vmem] * 2,
        compiler_params=pltpu.CompilerParams(vmem_limit_bytes=8 * MIB),
        name="settle",
    )(role_index.reshape(1), pieces, resid, gain, taken)


def keep_vmem(value):
    return pltpu.with_memory_space_constraint(value, pltpu.VMEM)


def lift_kernel(role, arrived, gate, up, outward, own, terms, weights, done):
    blocks, step, hidden_units = weights.shape[1:]
    half = blocks * step
    start = pl.multiple_of(role[0] * half, half)
    copies = [
        [
            pltpu.make_async_copy(
                source.at[pl.ds(start + i * step, step)], weights.at[s, i], done.at[s, i]
            )
            for i in range(blocks)
        ]
        for s, source in enumerate((gate, up))
    ]
    for part in copies:
        for copy in part:
            copy.start()
    rows = arrived[...].reshape(own.shape[0], arrived.shape[2])
    outward[:, 2 * hidden_units :] = rows[:, half:]
    terms[...] = rows[:, half:].astype(f32)
    for s, part in enumerate(copies):
        columns = slice(s * hidden_units, (s + 1) * hidden_units)
        for i, copy in enumerate(part):
            copy.wait()
            product = jnp.dot(
                rows[:, i * step : (i + 1) * step], weights[s, i], preferred_element_type=f32
            )
            own[:, columns] = product if i == 0 else own[:, columns] + product
        outward[:, columns] = own[:, columns].astype(bf16)


def lift_rows(role_index, arrived, gate, up):
    half, hidden_units = gate.shape[0] // 2, gate.shape[1]
    rows, extra = arrived.shape[0] * arrived.shape[1], arrived.shape[2] - half
    step = 256
    blocks = half // step
    return pl.pallas_call(
        lift_kernel,
        out_shape=[
            jax.ShapeDtypeStruct((rows, 2 * hidden_units + extra), bf16),
            jax.ShapeDtypeStruct((rows, 2 * hidden_units), f32),
            jax.ShapeDtypeStruct((rows, extra), f32),
        ],
        in_specs=[in_smem, in_vmem, in_hbm, in_hbm],
        out_specs=[in_vmem] * 3,
        scratch_shapes=[
            pltpu.VMEM((2, blocks, step, hidden_units), bf16),
            pltpu.SemaphoreType.DMA((2, blocks)),
        ],
        compiler_params=pltpu.CompilerParams(vmem_limit_bytes=20 * MIB),
        name="lift_rows",
    )(role_index.reshape(1), arrived, keep_hbm(gate), keep_hbm(up))


def lower_kernel(width, role, own, inward, terms, down, produced):
    hidden_units, half = down.shape[0], down.shape[1] // 2
    step = 256
    squares = jnp.sum(
        terms[...] + inward[:, 2 * hidden_units :].astype(f32), axis=1, keepdims=True
    )
    scale = lax.rsqrt(squares / width + 1e-06)
    ours = pl.ds(pl.multiple_of(role[0] * half, 128), half)
    total = jnp.zeros((own.shape[0], half), f32)
    for i in range(hidden_units // step):
        gate_at = slice(i * step, (i + 1) * step)
        up_at = slice(hidden_units + i * step, hidden_units + (i + 1) * step)
        gate_part = (own[:, gate_at] + inward[:, gate_at].astype(f32)) * scale
        up_part = (own[:, up_at] + inward[:, up_at].astype(f32)) * scale
        inner = (gate_part / (1.0 + jnp.exp(-gate_part)) * up_part).astype(bf16)
        total += jnp.dot(inner, down[gate_at, ours], preferred_element_type=f32)
    produced[...] = total.astype(bf16).reshape(produced.shape)


def lower_rows(role_index, width, own, inward, terms, down, capacity):
    rows, half = own.shape[0], down.shape[1] // 2
    return pl.pallas_call(
        functools.partial(lower_kernel, width),
        out_shape=jax.ShapeDtypeStruct((rows // capacity, capacity, half), bf16),
        in_specs=[in_smem] + [in_vmem] * 4,
        out_specs=in_vmem,
        compiler_params=pltpu.CompilerParams(vmem_limit_bytes=8 * MIB),
        name="lower_rows",
    )(role_index.reshape(1), own, inward, terms, keep_vmem(down))


def combine_kernel(weights, returned, hidden, out):
    rows = returned.shape[0] * returned.shape[1]
    combined = jnp.dot(
        weights[...], returned[...].reshape(rows, out.shape[1]), preferred_element_type=f32
    )
    out[...] = (hidden[...] + combined).astype(bf16)


def combine(weights, returned, hidden):
    return pl.pallas_call(
        combine_kernel,
        out_shape=jax.ShapeDtypeStruct(hidden.shape, bf16),
        in_specs=[in_vmem] * 3,
        out_specs=in_vmem,
        compiler_params=pltpu.CompilerParams(vmem_limit_bytes=8 * MIB),
        name="combine",
    )(weights, returned, hidden)


def local(
    resid,
    query,
    cache,
    lengths,
    w_uv,
    w_out,
    norm_gain,
    expert_ids,
    gate_scores,
    w_gate,
    w_up,
    w_down,
):
    role_index = lax.axis_index("role")
    tok_dev, width = resid.shape
    half_width = w_out.shape[2]
    n_dev = lax.axis_size("dev")
    capacity = max(2, tok_dev * expert_ids.shape[1] * 2 // n_dev)
    swap = [(0, 1), (1, 0)]

    order = visit_order(n_dev)
    exchange = functools.partial(
        lax.all_to_all,
        axis_name="dev",
        split_axis=0,
        concat_axis=0,
        axis_index_groups=[order],
        tiled=True,
    )
    span = n_dev // len(flips)
    wanted = np.zeros((len(flips), n_dev, n_dev), np.float32)
    for place, dev in enumerate(order):
        for i, flip in enumerate(flips):
            wanted[place // span, place % span * len(flips) + i, dev ^ flip] = 1.0
    places = np.stack([np.repeat(order, capacity), np.tile(np.arange(capacity), n_dev)])
    steps = [[(dev, dev ^ flip) for dev in range(n_dev)] for flip in flips[1:]]
    other_outs = [lax.ppermute(w_out[0], "dev", step) for step in steps]
    sent, own_lift, own_out, own_resid, taken, combine_weights = attend(
        role_index,
        lengths,
        query,
        cache,
        jnp.asarray(wanted, bf16),
        w_uv[:, 0],
        w_out[0],
        resid,
        expert_ids,
        gate_scores,
        jnp.asarray(places, jnp.int32),
    )
    other_lifts = [lax.ppermute(own_lift, "dev", step) for step in steps]
    gathered = exchange(sent.reshape(n_dev, -1, sent.shape[1]))
    gathered, other_outs, other_lifts, gain = lax.optimization_barrier(
        (gathered, other_outs, other_lifts, norm_gain.reshape(2, half_width))
    )
    own_values = lift_values(gathered.reshape(sent.shape), [own_lift, *other_lifts])
    other_values = lax.ppermute(own_values, "role", swap)
    partial = project(role_index, own_values, other_values, [own_out, *other_outs])
    pieces = exchange(partial)
    hidden, packed = settle(role_index, pieces, own_resid, gain, taken, capacity)
    arrived = exchange(packed)

    outward, own_sums, square_terms = lift_rows(role_index, arrived, w_gate[0], w_up[0])
    inward = lax.ppermute(outward, "role", swap)
    produced = lower_rows(role_index, width, own_sums, inward, square_terms, w_down[0], capacity)
    returned = exchange(produced)

    return combine(combine_weights, returned, hidden)


def solution(mesh):
    return jax.shard_map(
        local,
        mesh=mesh,
        in_specs=(
            P("dev", None),
            P("dev", None, None),
            P("dev", None, None),
            P("dev"),
            P(None, "dev", None),
            P("dev", None, "role"),
            P(),
            P("dev", None),
            P("dev", None),
            P("dev", None, None),
            P("dev", None, None),
            P("dev", None, None),
        ),
        out_specs=P("dev", "role"),
        check_vma=False,
    )
```

time: 93.2 us -> 88.2 us (0.946)
  blocking collectives: 56.9 us -> 52.2 us
  starting transfers between devices: 15.2 us -> 18.6 us
  waiting for transfers between devices: 8.13 us -> 6.8 us
    ppermute x2 -> x6, starting transfers between devices: 2.5 us -> 7.16 us  [the longest x3 5.07 us: local(): other_outs = [lax.ppermute(w_out[0], 'dev', step) for step in steps]]
    all_to_all x1, blocking collectives: 22.3 us -> 17.8 us  [local(): pieces = exchange(partial)]
    pallas_call x1, Pallas kernels: 2.35 us -> 0.79 us  [lower_rows(): pl.pallas_call(functools.partial(lower_kernel, width), out_shape=jax.Shap...]
    ppermute x2 -> x6, waiting for transfers between devices: 4.78 us -> 3.61 us  [the longest x3 3.6 us: local(): other_lifts = [lax.ppermute(own_lift, 'dev', step) for step in steps]]
    all_to_all x1, starting transfers between devices: 12.5 us -> 11.3 us  [local(): gathered = exchange(sent.reshape(n_dev, -1, sent.shape[1]))]
  transfers between devices with their start and end apart: 5 -> 9, of which waited for: 4 -> 4; matrix products, arithmetic and copies ran while one was open for 1% -> 1% of each run, Pallas kernels for 3% -> 3%
where the time goes in v4:
time: 88.2 us; the launch traced here: 87.9 us
  blocking collectives  52.2 us (59%)
  starting transfers between devices  18.6 us (21%)
  Pallas kernels  9.47 us (11%)
  waiting for transfers between devices  6.8 us (8%)
    all_to_all x1, blocking collectives, local(): pieces = exchange(partial)  17.8 us
    all_to_all x1, blocking collectives, local(): returned = exchange(produced)  17.5 us
    all_to_all x1, blocking collectives, local(): arrived = exchange(packed)  16.9 us
    all_to_all x1, starting transfers between devices, local(): gathered = exchange(sent.reshape(n_dev, -1, sent.shape[1]))  11.3 us
    ppermute x3, starting transfers between devices, local(): other_outs = [lax.ppermute(w_out[0], 'dev', step) for step in steps]  5.07 us
    ppermute x3, waiting for transfers between devices, local(): other_lifts = [lax.ppermute(own_lift, 'dev', step) for step in steps]  3.6 us
    pallas_call x1, Pallas kernels, lift_rows(): pl.pallas_call(lift_kernel, out_shape=[jax.ShapeDtypeStruct((rows, 2 * hi...  3.58 us
    pallas_call x1, Pallas kernels, attend(): pl.pallas_call(attend_kernel, out_shape=[jax.ShapeDtypeStruct((rows, bloc...  2.88 us
  transfers between devices with their start and end apart: 9, of which 4 were waited for; matrix products, arithmetic and copies ran while one was open for 1% of the time, Pallas kernels for 3%

profile of v4, /device:TPU:0, one launch (start us, length us, event | category | flops | bytes accessed | tf_op | source)
XLA Modules:
  0.0 87.9 jit_solution(2424055346746225304)
XLA Ops:
  0.0 2.0 %collective-permute-start.2 = (bf16[128,1792]{1,0:T(8,128)(2,1)}, bf16[128,1792]{1,0:T(8,128)(2,1)S(1)}, u32[]{:S(2)}, u32[]{:S(2)}) collective-permute-start(bf16[128,1792]{1,0:T(8,128)(2,1)} %bitcast.16), channel_id=1, source_target_pairs={{0,16},{1,17},{2,18},{3,19},{4,20},{5,21},{6,22},{7,23},{8,24},{9,... | collective-permute-start | bytes 1376264 | tf_op jit(solution)/shard_map/ppermute | solution.py:441
  2.0 1.6 %collective-permute-start.1 = (bf16[128,1792]{1,0:T(8,128)(2,1)}, bf16[128,1792]{1,0:T(8,128)(2,1)S(1)}, u32[]{:S(2)}, u32[]{:S(2)}) collective-permute-start(bf16[128,1792]{1,0:T(8,128)(2,1)} %bitcast.17), channel_id=1, source_target_pairs={{0,4},{1,5},{2,6},{3,7},{4,0},{5,1},{6,2},{7,3},{8,12},{9,13},{10,... | collective-permute-start | bytes 1376264 | tf_op jit(solution)/shard_map/ppermute | solution.py:441
  3.6 1.5 %collective-permute-start = (bf16[128,1792]{1,0:T(8,128)(2,1)}, bf16[128,1792]{1,0:T(8,128)(2,1)S(1)}, u32[]{:S(2)}, u32[]{:S(2)}) collective-permute-start(bf16[128,1792]{1,0:T(8,128)(2,1)} %bitcast.18), channel_id=1, source_target_pairs={{0,1},{1,0},{2,3},{3,2},{4,5},{5,4},{6,7},{7,6},{8,9},{9,8},{10,11... | collective-permute-start | bytes 1376264 | tf_op jit(solution)/shard_map/ppermute | solution.py:441
  5.1 2.9 %attend.1 = (bf16[1024,128]{1,0:T(8,128)(2,1)}, bf16[512,128]{1,0:T(8,128)(2,1)S(1)}, bf16[128,1792]{1,0:T(8,128)(2,1)S(1)}, bf16[8,1792]{1,0:T(8,128)(2,1)S(1)}...) custom-call(s32[1]{0:T(128)} %bitcast.role, s32[8]{0:T(128)} %lengths.1, bf16[8,64,576]{2,1,0:T(8,128)(2,1)} %query.1, ...), custom_call_target="tpu_custom_call" | custom-call | tf_op jit(solution)/shard_map/attend/pallas_call | solution.py:153
  8.0 0.2 collective-permute-start.5
  8.1 11.3 %all-to-all-start = ((bf16[64,16,128]{2,1,0:T(8,128)(2,1)}), bf16[64,16,128]{2,1,0:T(8,128)(2,1)S(1)}, u32[]{:S(2)}, u32[]{:S(2)}) async-start(bf16[64,16,128]{2,1,0:T(8,128)(2,1)} %bitcast.4), calls=%async_computation | async-start | bytes 524288 | tf_op jit(solution)/shard_map/all_to_all | solution.py:456
  19.5 1.3 %collective-permute-start.4 = (bf16[512,128]{1,0:T(8,128)(2,1)S(1)}, bf16[512,128]{1,0:T(8,128)(2,1)S(1)}, u32[]{:S(2)}, u32[]{:S(2)}) collective-permute-start(bf16[512,128]{1,0:T(8,128)(2,1)S(1)} %get-tuple-element.26.own), channel_id=1, source_target_pairs={{0,4},{1,5},{2,6},{3,7},{4,0},{5,1},{6,2},{7,3},{8,12},{9,13},{10,... | collective-permute-start | bytes 393224 | tf_op jit(solution)/shard_map/ppermute | solution.py:455
  20.8 0.0 collective-permute-done.5.rest_2_
  20.8 0.6 collective-permute-start.3
  21.4 0.7 reshape.18.gain
  22.1 3.2 %collective-permute-done.4.rest_1_ = bf16[512,128]{1,0:T(8,128)(2,1)S(1)} collective-permute-done((bf16[512,128]{1,0:T(8,128)(2,1)S(1)}, bf16[512,128]{1,0:T(8,128)(2,1)S(1)}, u32[]{:S(2)}, u32[]{:S(2)}) %collective-permute-start.4) | collective-permute-done | bytes 131104 | tf_op jit(solution)/shard_map/ppermute | solution.py:455
  25.3 0.4 collective-permute-done.3.rest_0_
  25.7 0.0 all-to-all-done
  25.7 0.0 collective-permute-done.2.rest_3_
  25.7 0.0 collective-permute-done.1.rest_2_
  25.7 0.0 collective-permute-done.rest_1_
  25.8 0.3 lift_values.1.own_values
  26.1 0.0 collective-permute-start.6
  26.1 1.2 %collective-permute-done.6.other_values = bf16[64,512]{1,0:T(8,128)(2,1)S(1)} collective-permute-done((bf16[64,512]{1,0:T(8,128)(2,1)S(1)}, bf16[64,512]{1,0:T(8,128)(2,1)S(1)}, u32[]{:S(2)}, u32[]{:S(2)}) %collective-permute-start.6) | collective-permute-done | bytes 65568 | tf_op jit(solution)/shard_map/ppermute | solution.py:461
  27.3 0.6 project.1
  28.0 17.8 %all_to_all.20.pieces = bf16[64,2,1792]{2,1,0:T(2,128)(2,1)S(1)} all-to-all(bf16[64,2,1792]{2,1,0:T(2,128)(2,1)S(1)} %project.1), channel_id=1, replica_groups={{63,61,55,53,42,40,34,32,31,29,23,21,10,8,2,0,58,56,50,48,47,45,39,37,2..., dimensions={0} | all-to-all | bytes 917504 | tf_op jit(solution)/shard_map/all_to_all | solution.py:463
  45.8 0.5 settle.1
  46.2 0.0 slice-start
  46.2 16.9 %all_to_all.21.arrived = bf16[64,2,1920]{2,1,0:T(2,128)(2,1)S(1)} all-to-all(bf16[64,2,1920]{2,1,0:T(2,128)(2,1)S(1)} %get-tuple-element.38), channel_id=1, replica_groups={{63,61,55,53,42,40,34,32,31,29,23,21,10,8,2,0,58,56,50,48,47,45,39,37,2..., dimensions={0} | all-to-all | bytes 983040 | tf_op jit(solution)/shard_map/all_to_all | solution.py:465
  63.1 0.0 slice-start.1
  63.2 3.6 %lift_rows.1 = (bf16[128,2176]{1,0:T(8,128)(2,1)S(1)}, f32[128,2048]{1,0:T(8,128)S(1)}, f32[128,128]{1,0:T(8,128)S(1)}) custom-call(s32[1]{0:T(128)} %bitcast.role, bf16[64,2,1920]{2,1,0:T(2,128)(2,1)S(1)} %all_to_all.21.arrived, bf16[3584,1024]{1,0:T(8,128)(2,1)} %bitcast.13, bf16[3584,1024]{1,0:T(8,128)(2,1)} %bitcast.14), custom_call_target="tpu_custom_call" | custom-call | tf_op jit(solution)/shard_map/lift_rows/pallas_call | solution.py:336
  66.7 0.1 collective-permute-start.7
  66.8 1.9 %collective-permute-done.7.inward = bf16[128,2176]{1,0:T(8,128)(2,1)S(1)} collective-permute-done((bf16[128,2176]{1,0:T(8,128)(2,1)S(1)}, bf16[128,2176]{1,0:T(8,128)(2,1)S(1)}, u32[]{:S(2)}, u32[]{:S(2)}) %collective-permute-start.7) | collective-permute-done | bytes 557088 | tf_op jit(solution)/shard_map/ppermute | solution.py:468
  68.8 0.0 slice-done
  68.8 0.0 slice-done.1
  68.8 0.8 lower_rows.1
  69.6 17.5 %all_to_all.22.returned = bf16[64,2,1792]{2,1,0:T(2,128)(2,1)S(1)} all-to-all(bf16[64,2,1792]{2,1,0:T(2,128)(2,1)S(1)} %lower_rows.1), channel_id=1, replica_groups={{63,61,55,53,42,40,34,32,31,29,23,21,10,8,2,0,58,56,50,48,47,45,39,37,2..., dimensions={0} | all-to-all | bytes 917504 | tf_op jit(solution)/shard_map/all_to_all | solution.py:470
  87.1 0.8 combine.1
  (1 shorter events, 0.0 us)
Async XLA Ops:
  0.0 25.7 %collective-permute-start.2 = (bf16[128,1792]{1,0:T(8,128)(2,1)}, bf16[128,1792]{1,0:T(8,128)(2,1)S(1)}, u32[]{:S(2)}, u32[]{:S(2)}) collective-permute-start(bf16[128,1792]{1,0:T(8,128)(2,1)} %bitcast.16), channel_id=1, source_target_pairs={{0,16},{1,17},{2,18},{3,19},{4,20},{5,21},{6,22},{7,23},{8,24},{9,... | collective-permute-start | bytes 1376264 | tf_op jit(solution)/shard_map/ppermute | solution.py:441
  2.0 23.7 %collective-permute-start.1 = (bf16[128,1792]{1,0:T(8,128)(2,1)}, bf16[128,1792]{1,0:T(8,128)(2,1)S(1)}, u32[]{:S(2)}, u32[]{:S(2)}) collective-permute-start(bf16[128,1792]{1,0:T(8,128)(2,1)} %bitcast.17), channel_id=1, source_target_pairs={{0,4},{1,5},{2,6},{3,7},{4,0},{5,1},{6,2},{7,3},{8,12},{9,13},{10,... | collective-permute-start | bytes 1376264 | tf_op jit(solution)/shard_map/ppermute | solution.py:441
  3.6 22.2 %collective-permute-start = (bf16[128,1792]{1,0:T(8,128)(2,1)}, bf16[128,1792]{1,0:T(8,128)(2,1)S(1)}, u32[]{:S(2)}, u32[]{:S(2)}) collective-permute-start(bf16[128,1792]{1,0:T(8,128)(2,1)} %bitcast.18), channel_id=1, source_target_pairs={{0,1},{1,0},{2,3},{3,2},{4,5},{5,4},{6,7},{7,6},{8,9},{9,8},{10,11... | collective-permute-start | bytes 1376264 | tf_op jit(solution)/shard_map/ppermute | solution.py:441
  8.0 12.8 %collective-permute-start.5 = (bf16[512,128]{1,0:T(8,128)(2,1)S(1)}, bf16[512,128]{1,0:T(8,128)(2,1)S(1)}, u32[]{:S(2)}, u32[]{:S(2)}) collective-permute-start(bf16[512,128]{1,0:T(8,128)(2,1)S(1)} %get-tuple-element.26.own), channel_id=1, source_target_pairs={{0,16},{1,17},{2,18},{3,19},{4,20},{5,21},{6,22},{7,23},{8,24},{9,... | collective-permute-start | bytes 393224 | tf_op jit(solution)/shard_map/ppermute | solution.py:455
  8.1 17.6 %all-to-all-start = ((bf16[64,16,128]{2,1,0:T(8,128)(2,1)}), bf16[64,16,128]{2,1,0:T(8,128)(2,1)S(1)}, u32[]{:S(2)}, u32[]{:S(2)}) async-start(bf16[64,16,128]{2,1,0:T(8,128)(2,1)} %bitcast.4), calls=%async_computation | async-start | bytes 524288 | tf_op jit(solution)/shard_map/all_to_all | solution.py:456
  19.5 5.8 %collective-permute-start.4 = (bf16[512,128]{1,0:T(8,128)(2,1)S(1)}, bf16[512,128]{1,0:T(8,128)(2,1)S(1)}, u32[]{:S(2)}, u32[]{:S(2)}) collective-permute-start(bf16[512,128]{1,0:T(8,128)(2,1)S(1)} %get-tuple-element.26.own), channel_id=1, source_target_pairs={{0,4},{1,5},{2,6},{3,7},{4,0},{5,1},{6,2},{7,3},{8,12},{9,13},{10,... | collective-permute-start | bytes 393224 | tf_op jit(solution)/shard_map/ppermute | solution.py:455
  20.8 5.0 %collective-permute-start.3 = (bf16[512,128]{1,0:T(8,128)(2,1)S(1)}, bf16[512,128]{1,0:T(8,128)(2,1)S(1)}, u32[]{:S(2)}, u32[]{:S(2)}) collective-permute-start(bf16[512,128]{1,0:T(8,128)(2,1)S(1)} %get-tuple-element.26.own), channel_id=1, source_target_pairs={{0,1},{1,0},{2,3},{3,2},{4,5},{5,4},{6,7},{7,6},{8,9},{9,8},{10,11... | collective-permute-start | bytes 393224 | tf_op jit(solution)/shard_map/ppermute | solution.py:455
  26.1 1.3 %collective-permute-start.6 = (bf16[64,512]{1,0:T(8,128)(2,1)S(1)}, bf16[64,512]{1,0:T(8,128)(2,1)S(1)}, u32[]{:S(2)}, u32[]{:S(2)}) collective-permute-start(bf16[64,512]{1,0:T(8,128)(2,1)S(1)} %lift_values.1.own_values), channel_id=1, source_target_pairs={{0,64},{64,0},{1,65},{65,1},{2,66},{66,2},{3,67},{67,3},{4,68},{68... | collective-permute-start | bytes 196616 | tf_op jit(solution)/shard_map/ppermute | solution.py:461
  46.2 22.5 %slice-start = ((s8[7340032]{0:T(1024)(128)(4,1)}), s8[4194304]{0:T(1024)(128)(4,1)S(1)}, s32[]{:S(2)}) async-start(s8[7340032]{0:T(1024)(128)(4,1)} %bitcast.9), calls=%async_computation.4 | async-start | bytes 8388608
  63.1 5.6 %slice-start.1 = ((s8[7340032]{0:T(1024)(128)(4,1)}), s8[3145728]{0:T(1024)(128)(4,1)S(1)}, s32[]{:S(2)}) async-start(s8[7340032]{0:T(1024)(128)(4,1)} %bitcast.9), calls=%async_computation.5 | async-start | bytes 6291456
  66.7 2.0 %collective-permute-start.7 = (bf16[128,2176]{1,0:T(8,128)(2,1)S(1)}, bf16[128,2176]{1,0:T(8,128)(2,1)S(1)}, u32[]{:S(2)}, u32[]{:S(2)}) collective-permute-start(bf16[128,2176]{1,0:T(8,128)(2,1)S(1)} %get-tuple-element.40), channel_id=1, source_target_pairs={{0,64},{64,0},{1,65},{65,1},{2,66},{66,2},{3,67},{67,3},{4,68},{68... | collective-permute-start | bytes 1671176 | tf_op jit(solution)/shard_map/ppermute | solution.py:468

commit v5 on v4

--- a/solution.py
+++ b/solution.py
@@ -32,7 +32,7 @@
 
 
 def visit_order(n_dev):
-    return sorted(range(n_dev), key=lambda dev: (token_class(dev), -dev))
+    return sorted(range(n_dev), key=lambda dev: (-token_class(dev), -dev))
 
 
 def attend_kernel(
@@ -254,7 +254,7 @@
     )(role_index.reshape(1), own_values, other_values, *weights)
 
 
-def settle_kernel(role, pieces, resid, gain, taken, hidden, packed):
+def settle_kernel(pieces, resid, taken, hidden, packed):
     tokens, half = hidden.shape
     rows = pieces.shape[0] * pieces.shape[1]
     token = lax.broadcasted_iota(jnp.int32, (tokens, rows), 0)
@@ -266,39 +266,31 @@
     )
     own = attended + resid[...].astype(f32)
     hidden[...] = own
-    square = jnp.sum(own * own, axis=1, keepdims=True)
-    first = square.astype(bf16).astype(f32)
-    second = (square - first).astype(bf16).astype(f32)
-    third = square - first - second
-    lane = lax.broadcasted_iota(jnp.int32, (tokens, packed.shape[2] - half), 1)
-    terms = jnp.where(lane == 0, first, jnp.where(lane == 1, second, third))
-    terms = jnp.where(lane < 3, terms, 0.0)
-    sent = jnp.concatenate([own * gain[pl.ds(role[0], 1)], terms], axis=1).astype(bf16)
     packed[...] = lax.dot_general(
-        taken[...], sent, (((0,), (0,)), ((), ())), preferred_element_type=f32
+        taken[...], own.astype(bf16), (((0,), (0,)), ((), ())), preferred_element_type=f32
     ).astype(bf16).reshape(packed.shape)
 
 
-def settle(role_index, pieces, resid, gain, taken, capacity):
+def settle(pieces, resid, taken, capacity):
     tokens, half = resid.shape
     return pl.pallas_call(
         settle_kernel,
         out_shape=[
             jax.ShapeDtypeStruct((tokens, half), f32),
-            jax.ShapeDtypeStruct((taken.shape[1] // capacity, capacity, half + 128), bf16),
+            jax.ShapeDtypeStruct((taken.shape[1] // capacity, capacity, half), bf16),
         ],
-        in_specs=[in_smem] + [in_vmem] * 4,
+        in_specs=[in_vmem] * 3,
         out_specs=[in_vmem] * 2,
         compiler_params=pltpu.CompilerParams(vmem_limit_bytes=8 * MIB),
         name="settle",
-    )(role_index.reshape(1), pieces, resid, gain, taken)
+    )(pieces, resid, taken)
 
 
 def keep_vmem(value):
     return pltpu.with_memory_space_constraint(value, pltpu.VMEM)
 
 
-def lift_kernel(role, arrived, gate, up, outward, own, terms, weights, done):
+def lift_kernel(role, arrived, gain, gate, up, outward, own, terms, weights, done):
     blocks, step, hidden_units = weights.shape[1:]
     half = blocks * step
     start = pl.multiple_of(role[0] * half, half)
@@ -314,9 +306,17 @@
     for part in copies:
         for copy in part:
             copy.start()
-    rows = arrived[...].reshape(own.shape[0], arrived.shape[2])
-    outward[:, 2 * hidden_units :] = rows[:, half:]
-    terms[...] = rows[:, half:].astype(f32)
+    rows = arrived[...].reshape(own.shape[0], half).astype(f32)
+    square = jnp.sum(rows * rows, axis=1, keepdims=True)
+    first = square.astype(bf16).astype(f32)
+    second = (square - first).astype(bf16).astype(f32)
+    third = square - first - second
+    lane = lax.broadcasted_iota(jnp.int32, terms.shape, 1)
+    split = jnp.where(lane == 0, first, jnp.where(lane == 1, second, third))
+    split = jnp.where(lane < 3, split, 0.0)
+    terms[...] = split
+    outward[:, 2 * hidden_units :] = split.astype(bf16)
+    rows = (rows * gain[pl.ds(role[0], 1)]).astype(bf16)
     for s, part in enumerate(copies):
         columns = slice(s * hidden_units, (s + 1) * hidden_units)
         for i, copy in enumerate(part):
@@ -328,9 +328,9 @@
         outward[:, columns] = own[:, columns].astype(bf16)
 
 
-def lift_rows(role_index, arrived, gate, up):
+def lift_rows(role_index, arrived, gain, gate, up):
     half, hidden_units = gate.shape[0] // 2, gate.shape[1]
-    rows, extra = arrived.shape[0] * arrived.shape[1], arrived.shape[2] - half
+    rows, extra = arrived.shape[0] * arrived.shape[1], 128
     step = 256
     blocks = half // step
     return pl.pallas_call(
@@ -340,7 +340,7 @@
             jax.ShapeDtypeStruct((rows, 2 * hidden_units), f32),
             jax.ShapeDtypeStruct((rows, extra), f32),
         ],
-        in_specs=[in_smem, in_vmem, in_hbm, in_hbm],
+        in_specs=[in_smem, in_vmem, in_vmem, in_hbm, in_hbm],
         out_specs=[in_vmem] * 3,
         scratch_shapes=[
             pltpu.VMEM((2, blocks, step, hidden_units), bf16),
@@ -348,7 +348,7 @@
         ],
         compiler_params=pltpu.CompilerParams(vmem_limit_bytes=20 * MIB),
         name="lift_rows",
-    )(role_index.reshape(1), arrived, keep_hbm(gate), keep_hbm(up))
+    )(role_index.reshape(1), arrived, gain, keep_hbm(gate), keep_hbm(up))
 
 
 def lower_kernel(width, role, own, inward, terms, down, produced):
@@ -461,10 +461,10 @@
     other_values = lax.ppermute(own_values, "role", swap)
     partial = project(role_index, own_values, other_values, [own_out, *other_outs])
     pieces = exchange(partial)
-    hidden, packed = settle(role_index, pieces, own_resid, gain, taken, capacity)
+    hidden, packed = settle(pieces, own_resid, taken, capacity)
     arrived = exchange(packed)
 
-    outward, own_sums, square_terms = lift_rows(role_index, arrived, w_gate[0], w_up[0])
+    outward, own_sums, square_terms = lift_rows(role_index, arrived, gain, w_gate[0], w_up[0])
     inward = lax.ppermute(outward, "role", swap)
     produced = lower_rows(role_index, width, own_sums, inward, square_terms, w_down[0], capacity)
     returned = exchange(produced)

time: 88.2 us -> 87 us (0.986)
  blocking collectives: 52.2 us -> 50.7 us
    ppermute x3, starting transfers between devices: 2.09 us -> 0.99 us  [local(): other_lifts = [lax.ppermute(own_lift, 'dev', step) for step in steps]]
    all_to_all x1, starting transfers between devices: 11.3 us -> 12.4 us  [local(): gathered = exchange(sent.reshape(n_dev, -1, sent.shape[1]))]
where the time goes in v5:
time: 87 us; the launch traced here: 86.6 us
  blocking collectives  50.7 us (58%)
  starting transfers between devices  18.6 us (21%)
  Pallas kernels  9.47 us (11%)
  waiting for transfers between devices  7.07 us (8%)
    all_to_all x1, blocking collectives, local(): returned = exchange(produced)  17.3 us
    all_to_all x1, blocking collectives, local(): pieces = exchange(partial)  17.2 us
    all_to_all x1, blocking collectives, local(): arrived = exchange(packed)  16.2 us
    all_to_all x1, starting transfers between devices, local(): gathered = exchange(sent.reshape(n_dev, -1, sent.shape[1]))  12.4 us
    ppermute x3, starting transfers between devices, local(): other_outs = [lax.ppermute(w_out[0], 'dev', step) for step in steps]  5.07 us
    ppermute x3, waiting for transfers between devices, local(): other_lifts = [lax.ppermute(own_lift, 'dev', step) for step in steps]  3.87 us
    pallas_call x1, Pallas kernels, lift_rows(): pl.pallas_call(lift_kernel, out_shape=[jax.ShapeDtypeStruct((rows, 2 * hi...  3.63 us
    pallas_call x1, Pallas kernels, attend(): pl.pallas_call(attend_kernel, out_shape=[jax.ShapeDtypeStruct((rows, bloc...  2.88 us
  transfers between devices with their start and end apart: 9, of which 4 were waited for; matrix products, arithmetic and copies ran while one was open for 1% of the time, Pallas kernels for 3%

profile of v5, /device:TPU:0, one launch (start us, length us, event | category | flops | bytes accessed | tf_op | source)
XLA Modules:
  0.0 86.6 jit_solution(10457334726301389336)
XLA Ops:
  0.0 2.0 %collective-permute-start.2 = (bf16[128,1792]{1,0:T(8,128)(2,1)}, bf16[128,1792]{1,0:T(8,128)(2,1)S(1)}, u32[]{:S(2)}, u32[]{:S(2)}) collective-permute-start(bf16[128,1792]{1,0:T(8,128)(2,1)} %bitcast.16), channel_id=1, source_target_pairs={{0,16},{1,17},{2,18},{3,19},{4,20},{5,21},{6,22},{7,23},{8,24},{9,... | collective-permute-start | bytes 1376264 | tf_op jit(solution)/shard_map/ppermute | solution.py:441
  2.0 1.6 %collective-permute-start.1 = (bf16[128,1792]{1,0:T(8,128)(2,1)}, bf16[128,1792]{1,0:T(8,128)(2,1)S(1)}, u32[]{:S(2)}, u32[]{:S(2)}) collective-permute-start(bf16[128,1792]{1,0:T(8,128)(2,1)} %bitcast.17), channel_id=1, source_target_pairs={{0,4},{1,5},{2,6},{3,7},{4,0},{5,1},{6,2},{7,3},{8,12},{9,13},{10,... | collective-permute-start | bytes 1376264 | tf_op jit(solution)/shard_map/ppermute | solution.py:441
  3.6 1.5 %collective-permute-start = (bf16[128,1792]{1,0:T(8,128)(2,1)}, bf16[128,1792]{1,0:T(8,128)(2,1)S(1)}, u32[]{:S(2)}, u32[]{:S(2)}) collective-permute-start(bf16[128,1792]{1,0:T(8,128)(2,1)} %bitcast.18), channel_id=1, source_target_pairs={{0,1},{1,0},{2,3},{3,2},{4,5},{5,4},{6,7},{7,6},{8,9},{9,8},{10,11... | collective-permute-start | bytes 1376264 | tf_op jit(solution)/shard_map/ppermute | solution.py:441
  5.1 2.9 %attend.1 = (bf16[1024,128]{1,0:T(8,128)(2,1)}, bf16[512,128]{1,0:T(8,128)(2,1)S(1)}, bf16[128,1792]{1,0:T(8,128)(2,1)S(1)}, bf16[8,1792]{1,0:T(8,128)(2,1)S(1)}...) custom-call(s32[1]{0:T(128)} %bitcast.role, s32[8]{0:T(128)} %lengths.1, bf16[8,64,576]{2,1,0:T(8,128)(2,1)} %query.1, ...), custom_call_target="tpu_custom_call" | custom-call | tf_op jit(solution)/shard_map/attend/pallas_call | solution.py:153
  8.0 0.2 collective-permute-start.5
  8.1 12.4 %all-to-all-start = ((bf16[64,16,128]{2,1,0:T(8,128)(2,1)}), bf16[64,16,128]{2,1,0:T(8,128)(2,1)S(1)}, u32[]{:S(2)}, u32[]{:S(2)}) async-start(bf16[64,16,128]{2,1,0:T(8,128)(2,1)} %bitcast.4), calls=%async_computation | async-start | bytes 524288 | tf_op jit(solution)/shard_map/all_to_all | solution.py:456
  20.5 0.1 collective-permute-start.4
  20.6 0.0 collective-permute-done.5.rest_2_
  20.6 0.7 collective-permute-start.3
  21.4 0.7 reshape.17.gain
  22.1 3.7 %collective-permute-done.4.rest_1_ = bf16[512,128]{1,0:T(8,128)(2,1)S(1)} collective-permute-done((bf16[512,128]{1,0:T(8,128)(2,1)S(1)}, bf16[512,128]{1,0:T(8,128)(2,1)S(1)}, u32[]{:S(2)}, u32[]{:S(2)}) %collective-permute-start.4) | collective-permute-done | bytes 131104 | tf_op jit(solution)/shard_map/ppermute | solution.py:455
  25.8 0.2 collective-permute-done.3.rest_0_
  26.0 0.0 all-to-all-done
  26.0 0.0 collective-permute-done.2.rest_3_
  26.0 0.0 collective-permute-done.1.rest_2_
  26.0 0.0 collective-permute-done.rest_1_
  26.0 0.3 lift_values.1.own_values
  26.3 0.0 collective-permute-start.6
  26.3 1.2 %collective-permute-done.6.other_values = bf16[64,512]{1,0:T(8,128)(2,1)S(1)} collective-permute-done((bf16[64,512]{1,0:T(8,128)(2,1)S(1)}, bf16[64,512]{1,0:T(8,128)(2,1)S(1)}, u32[]{:S(2)}, u32[]{:S(2)}) %collective-permute-start.6) | collective-permute-done | bytes 65568 | tf_op jit(solution)/shard_map/ppermute | solution.py:461
  27.6 0.6 project.1
  28.2 17.2 %all_to_all.20.pieces = bf16[64,2,1792]{2,1,0:T(2,128)(2,1)S(1)} all-to-all(bf16[64,2,1792]{2,1,0:T(2,128)(2,1)S(1)} %project.1), channel_id=1, replica_groups={{59,57,51,49,46,44,38,36,27,25,19,17,14,12,6,4,62,60,54,52,43,41,35,33,..., dimensions={0} | all-to-all | bytes 917504 | tf_op jit(solution)/shard_map/all_to_all | solution.py:463
  45.4 0.4 settle.1
  45.8 0.0 slice-start
  45.9 16.2 %all_to_all.21.arrived = bf16[64,2,1792]{2,1,0:T(2,128)(2,1)S(1)} all-to-all(bf16[64,2,1792]{2,1,0:T(2,128)(2,1)S(1)} %get-tuple-element.37), channel_id=1, replica_groups={{59,57,51,49,46,44,38,36,27,25,19,17,14,12,6,4,62,60,54,52,43,41,35,33,..., dimensions={0} | all-to-all | bytes 917504 | tf_op jit(solution)/shard_map/all_to_all | solution.py:465
  62.0 0.0 slice-start.1
  62.0 3.6 %lift_rows.1 = (bf16[128,2176]{1,0:T(8,128)(2,1)S(1)}, f32[128,2048]{1,0:T(8,128)S(1)}, f32[128,128]{1,0:T(8,128)S(1)}) custom-call(s32[1]{0:T(128)} %bitcast.role, bf16[64,2,1792]{2,1,0:T(2,128)(2,1)S(1)} %all_to_all.21.arrived, f32[2,1792]{1,0:T(2,128)S(1)} %reshape.17.gain, bf16[3584,1024]{1,0:T(8,128)(2,1)} %bitcast.13, bf16[3584,1024]{1,0:T(8,128)(2,1)} %bitcast.14), custom_call_target="tpu_custom_call" | custom-call | tf_op jit(solution)/shard_map/lift_rows/pallas_call | solution.py:336
  65.7 0.1 collective-permute-start.7
  65.8 1.9 %collective-permute-done.7.inward = bf16[128,2176]{1,0:T(8,128)(2,1)S(1)} collective-permute-done((bf16[128,2176]{1,0:T(8,128)(2,1)S(1)}, bf16[128,2176]{1,0:T(8,128)(2,1)S(1)}, u32[]{:S(2)}, u32[]{:S(2)}) %collective-permute-start.7) | collective-permute-done | bytes 557088 | tf_op jit(solution)/shard_map/ppermute | solution.py:468
  67.7 0.0 slice-done
  67.7 0.0 slice-done.1
  67.7 0.8 lower_rows.1
  68.5 17.3 %all_to_all.22.returned = bf16[64,2,1792]{2,1,0:T(2,128)(2,1)S(1)} all-to-all(bf16[64,2,1792]{2,1,0:T(2,128)(2,1)S(1)} %lower_rows.1), channel_id=1, replica_groups={{59,57,51,49,46,44,38,36,27,25,19,17,14,12,6,4,62,60,54,52,43,41,35,33,..., dimensions={0} | all-to-all | bytes 917504 | tf_op jit(solution)/shard_map/all_to_all | solution.py:470
  85.8 0.8 combine.1
  (1 shorter events, 0.0 us)
Async XLA Ops:
  0.0 26.0 %collective-permute-start.2 = (bf16[128,1792]{1,0:T(8,128)(2,1)}, bf16[128,1792]{1,0:T(8,128)(2,1)S(1)}, u32[]{:S(2)}, u32[]{:S(2)}) collective-permute-start(bf16[128,1792]{1,0:T(8,128)(2,1)} %bitcast.16), channel_id=1, source_target_pairs={{0,16},{1,17},{2,18},{3,19},{4,20},{5,21},{6,22},{7,23},{8,24},{9,... | collective-permute-start | bytes 1376264 | tf_op jit(solution)/shard_map/ppermute | solution.py:441
  2.0 24.0 %collective-permute-start.1 = (bf16[128,1792]{1,0:T(8,128)(2,1)}, bf16[128,1792]{1,0:T(8,128)(2,1)S(1)}, u32[]{:S(2)}, u32[]{:S(2)}) collective-permute-start(bf16[128,1792]{1,0:T(8,128)(2,1)} %bitcast.17), channel_id=1, source_target_pairs={{0,4},{1,5},{2,6},{3,7},{4,0},{5,1},{6,2},{7,3},{8,12},{9,13},{10,... | collective-permute-start | bytes 1376264 | tf_op jit(solution)/shard_map/ppermute | solution.py:441
  3.6 22.4 %collective-permute-start = (bf16[128,1792]{1,0:T(8,128)(2,1)}, bf16[128,1792]{1,0:T(8,128)(2,1)S(1)}, u32[]{:S(2)}, u32[]{:S(2)}) collective-permute-start(bf16[128,1792]{1,0:T(8,128)(2,1)} %bitcast.18), channel_id=1, source_target_pairs={{0,1},{1,0},{2,3},{3,2},{4,5},{5,4},{6,7},{7,6},{8,9},{9,8},{10,11... | collective-permute-start | bytes 1376264 | tf_op jit(solution)/shard_map/ppermute | solution.py:441
  8.0 12.7 %collective-permute-start.5 = (bf16[512,128]{1,0:T(8,128)(2,1)S(1)}, bf16[512,128]{1,0:T(8,128)(2,1)S(1)}, u32[]{:S(2)}, u32[]{:S(2)}) collective-permute-start(bf16[512,128]{1,0:T(8,128)(2,1)S(1)} %get-tuple-element.26.own), channel_id=1, source_target_pairs={{0,16},{1,17},{2,18},{3,19},{4,20},{5,21},{6,22},{7,23},{8,24},{9,... | collective-permute-start | bytes 393224 | tf_op jit(solution)/shard_map/ppermute | solution.py:455
  8.1 17.8 %all-to-all-start = ((bf16[64,16,128]{2,1,0:T(8,128)(2,1)}), bf16[64,16,128]{2,1,0:T(8,128)(2,1)S(1)}, u32[]{:S(2)}, u32[]{:S(2)}) async-start(bf16[64,16,128]{2,1,0:T(8,128)(2,1)} %bitcast.4), calls=%async_computation | async-start | bytes 524288 | tf_op jit(solution)/shard_map/all_to_all | solution.py:456
  20.5 5.2 %collective-permute-start.4 = (bf16[512,128]{1,0:T(8,128)(2,1)S(1)}, bf16[512,128]{1,0:T(8,128)(2,1)S(1)}, u32[]{:S(2)}, u32[]{:S(2)}) collective-permute-start(bf16[512,128]{1,0:T(8,128)(2,1)S(1)} %get-tuple-element.26.own), channel_id=1, source_target_pairs={{0,4},{1,5},{2,6},{3,7},{4,0},{5,1},{6,2},{7,3},{8,12},{9,13},{10,... | collective-permute-start | bytes 393224 | tf_op jit(solution)/shard_map/ppermute | solution.py:455
  20.6 5.3 %collective-permute-start.3 = (bf16[512,128]{1,0:T(8,128)(2,1)S(1)}, bf16[512,128]{1,0:T(8,128)(2,1)S(1)}, u32[]{:S(2)}, u32[]{:S(2)}) collective-permute-start(bf16[512,128]{1,0:T(8,128)(2,1)S(1)} %get-tuple-element.26.own), channel_id=1, source_target_pairs={{0,1},{1,0},{2,3},{3,2},{4,5},{5,4},{6,7},{7,6},{8,9},{9,8},{10,11... | collective-permute-start | bytes 393224 | tf_op jit(solution)/shard_map/ppermute | solution.py:455
  26.3 1.3 %collective-permute-start.6 = (bf16[64,512]{1,0:T(8,128)(2,1)S(1)}, bf16[64,512]{1,0:T(8,128)(2,1)S(1)}, u32[]{:S(2)}, u32[]{:S(2)}) collective-permute-start(bf16[64,512]{1,0:T(8,128)(2,1)S(1)} %lift_values.1.own_values), channel_id=1, source_target_pairs={{0,64},{64,0},{1,65},{65,1},{2,66},{66,2},{3,67},{67,3},{4,68},{68... | collective-permute-start | bytes 196616 | tf_op jit(solution)/shard_map/ppermute | solution.py:461
  45.8 21.9 %slice-start = ((s8[7340032]{0:T(1024)(128)(4,1)}), s8[4194304]{0:T(1024)(128)(4,1)S(1)}, s32[]{:S(2)}) async-start(s8[7340032]{0:T(1024)(128)(4,1)} %bitcast.9), calls=%async_computation.4 | async-start | bytes 8388608
  62.0 5.7 %slice-start.1 = ((s8[7340032]{0:T(1024)(128)(4,1)}), s8[3145728]{0:T(1024)(128)(4,1)S(1)}, s32[]{:S(2)}) async-start(s8[7340032]{0:T(1024)(128)(4,1)} %bitcast.9), calls=%async_computation.5 | async-start | bytes 6291456
  65.7 2.0 %collective-permute-start.7 = (bf16[128,2176]{1,0:T(8,128)(2,1)S(1)}, bf16[128,2176]{1,0:T(8,128)(2,1)S(1)}, u32[]{:S(2)}, u32[]{:S(2)}) collective-permute-start(bf16[128,2176]{1,0:T(8,128)(2,1)S(1)} %get-tuple-element.40), channel_id=1, source_target_pairs={{0,64},{64,0},{1,65},{65,1},{2,66},{66,2},{3,67},{67,3},{4,68},{68... | collective-permute-start | bytes 1671176 | tf_op jit(solution)/shard_map/ppermute | solution.py:468

commit v6 on v5

--- a/solution.py
+++ b/solution.py
@@ -115,7 +115,7 @@
             staged[pl.ds(i * heads * chunks + c, heads, stride=chunks)] = context[
                 :, c * block : (c + 1) * block
             ]
-    sent[...] = staged[...].astype(bf16)
+    sent[...] = staged[: sent.shape[0]].astype(bf16)
     for copy in moves:
         copy.wait()
     choose(ids, gates, places, taken, combine)
@@ -170,7 +170,7 @@
             pltpu.VMEM(ids.shape, jnp.int32),
             pltpu.VMEM(gates.shape, f32),
             pltpu.VMEM(places.shape, jnp.int32),
-            pltpu.VMEM((rows, block), f32),
+            pltpu.VMEM((rows + 32, block), f32),
             pltpu.SemaphoreType.DMA((16,)),
         ],
         compiler_params=pltpu.CompilerParams(vmem_limit_bytes=8 * MIB),
@@ -201,7 +201,7 @@
     rows = values.shape[0]
     stride = gathered.shape[0] // rows
     chunks = own.shape[0] // block
-    staged[...] = gathered[...].astype(f32)
+    staged[: gathered.shape[0]] = gathered[...].astype(f32)
     for i, weights in enumerate([own, *others]):
         total = jnp.zeros((rows, block), f32)
         for c in range(chunks):
@@ -221,7 +221,7 @@
         out_shape=jax.ShapeDtypeStruct((rows, wide), bf16),
         in_specs=[in_vmem] * (1 + len(weights)),
         out_specs=in_vmem,
-        scratch_shapes=[pltpu.VMEM((total, block), f32)],
+        scratch_shapes=[pltpu.VMEM((total + 32, block), f32)],
         compiler_params=pltpu.CompilerParams(vmem_limit_bytes=8 * MIB),
         name="lift_values",
     )(gathered, *weights)
@@ -237,7 +237,7 @@
             ].astype(f32)
     total = jnp.zeros((2 * rows, partial.shape[2]), f32)
     for i, part in enumerate(weights):
-        total += jnp.dot(spread[i].astype(bf16), part[...], preferred_element_type=f32)
+        total += jnp.dot(spread[i, : 2 * rows].astype(bf16), part[...], preferred_element_type=f32)
     partial[...] = total.astype(bf16).reshape(partial.shape)
 
 
@@ -248,7 +248,7 @@
         out_shape=jax.ShapeDtypeStruct((rows, 2, weights[0].shape[1]), bf16),
         in_specs=[in_smem] + [in_vmem] * (2 + len(weights)),
         out_specs=in_vmem,
-        scratch_shapes=[pltpu.VMEM((len(weights), 2 * rows, wide // len(weights)), f32)],
+        scratch_shapes=[pltpu.VMEM((len(weights), 2 * rows + 16, wide // len(weights)), f32)],
         compiler_params=pltpu.CompilerParams(vmem_limit_bytes=16 * MIB),
         name="project",
     )(role_index.reshape(1), own_values, other_values, *weights)

time: 87 us -> 87 us (level)
  no operation moved by 1% of the time
where the time goes in v6:
time: 87 us; the launch traced here: 86.6 us
  blocking collectives  50.7 us (58%)
  starting transfers between devices  18.6 us (21%)
  Pallas kernels  9.47 us (11%)
  waiting for transfers between devices  7.07 us (8%)
    all_to_all x1, blocking collectives, local(): returned = exchange(produced)  17.3 us
    all_to_all x1, blocking collectives, local(): pieces = exchange(partial)  17.2 us
    all_to_all x1, blocking collectives, local(): arrived = exchange(packed)  16.2 us
    all_to_all x1, starting transfers between devices, local(): gathered = exchange(sent.reshape(n_dev, -1, sent.shape[1]))  12.4 us
    ppermute x3, starting transfers between devices, local(): other_outs = [lax.ppermute(w_out[0], 'dev', step) for step in steps]  5.07 us
    ppermute x3, waiting for transfers between devices, local(): other_lifts = [lax.ppermute(own_lift, 'dev', step) for step in steps]  3.87 us
    pallas_call x1, Pallas kernels, lift_rows(): pl.pallas_call(lift_kernel, out_shape=[jax.ShapeDtypeStruct((rows, 2 * hi...  3.63 us
    pallas_call x1, Pallas kernels, attend(): pl.pallas_call(attend_kernel, out_shape=[jax.ShapeDtypeStruct((rows, bloc...  2.88 us
  transfers between devices with their start and end apart: 9, of which 4 were waited for; matrix products, arithmetic and copies ran while one was open for 1% of the time, Pallas kernels for 3%

profile of v6, /device:TPU:0, one launch (start us, length us, event | category | flops | bytes accessed | tf_op | source)
XLA Modules:
  0.0 86.6 jit_solution(15441863514117738036)
XLA Ops:
  0.0 2.0 %collective-permute-start.2 = (bf16[128,1792]{1,0:T(8,128)(2,1)}, bf16[128,1792]{1,0:T(8,128)(2,1)S(1)}, u32[]{:S(2)}, u32[]{:S(2)}) collective-permute-start(bf16[128,1792]{1,0:T(8,128)(2,1)} %bitcast.16), channel_id=1, source_target_pairs={{0,16},{1,17},{2,18},{3,19},{4,20},{5,21},{6,22},{7,23},{8,24},{9,... | collective-permute-start | bytes 1376264 | tf_op jit(solution)/shard_map/ppermute | solution.py:441
  2.0 1.6 %collective-permute-start.1 = (bf16[128,1792]{1,0:T(8,128)(2,1)}, bf16[128,1792]{1,0:T(8,128)(2,1)S(1)}, u32[]{:S(2)}, u32[]{:S(2)}) collective-permute-start(bf16[128,1792]{1,0:T(8,128)(2,1)} %bitcast.17), channel_id=1, source_target_pairs={{0,4},{1,5},{2,6},{3,7},{4,0},{5,1},{6,2},{7,3},{8,12},{9,13},{10,... | collective-permute-start | bytes 1376264 | tf_op jit(solution)/shard_map/ppermute | solution.py:441
  3.6 1.5 %collective-permute-start = (bf16[128,1792]{1,0:T(8,128)(2,1)}, bf16[128,1792]{1,0:T(8,128)(2,1)S(1)}, u32[]{:S(2)}, u32[]{:S(2)}) collective-permute-start(bf16[128,1792]{1,0:T(8,128)(2,1)} %bitcast.18), channel_id=1, source_target_pairs={{0,1},{1,0},{2,3},{3,2},{4,5},{5,4},{6,7},{7,6},{8,9},{9,8},{10,11... | collective-permute-start | bytes 1376264 | tf_op jit(solution)/shard_map/ppermute | solution.py:441
  5.1 2.9 %attend.1 = (bf16[1024,128]{1,0:T(8,128)(2,1)}, bf16[512,128]{1,0:T(8,128)(2,1)S(1)}, bf16[128,1792]{1,0:T(8,128)(2,1)S(1)}, bf16[8,1792]{1,0:T(8,128)(2,1)S(1)}...) custom-call(s32[1]{0:T(128)} %bitcast.role, s32[8]{0:T(128)} %lengths.1, bf16[8,64,576]{2,1,0:T(8,128)(2,1)} %query.1, ...), custom_call_target="tpu_custom_call" | custom-call | tf_op jit(solution)/shard_map/attend/pallas_call | solution.py:153
  8.0 0.2 collective-permute-start.5
  8.1 12.4 %all-to-all-start = ((bf16[64,16,128]{2,1,0:T(8,128)(2,1)}), bf16[64,16,128]{2,1,0:T(8,128)(2,1)S(1)}, u32[]{:S(2)}, u32[]{:S(2)}) async-start(bf16[64,16,128]{2,1,0:T(8,128)(2,1)} %bitcast.4), calls=%async_computation | async-start | bytes 524288 | tf_op jit(solution)/shard_map/all_to_all | solution.py:456
  20.5 0.1 collective-permute-start.4
  20.6 0.0 collective-permute-done.5.rest_2_
  20.6 0.7 collective-permute-start.3
  21.4 0.7 reshape.17.gain
  22.1 3.7 %collective-permute-done.4.rest_1_ = bf16[512,128]{1,0:T(8,128)(2,1)S(1)} collective-permute-done((bf16[512,128]{1,0:T(8,128)(2,1)S(1)}, bf16[512,128]{1,0:T(8,128)(2,1)S(1)}, u32[]{:S(2)}, u32[]{:S(2)}) %collective-permute-start.4) | collective-permute-done | bytes 131104 | tf_op jit(solution)/shard_map/ppermute | solution.py:455
  25.8 0.2 collective-permute-done.3.rest_0_
  26.0 0.0 all-to-all-done
  26.0 0.0 collective-permute-done.2.rest_3_
  26.0 0.0 collective-permute-done.1.rest_2_
  26.0 0.0 collective-permute-done.rest_1_
  26.0 0.3 lift_values.1.own_values
  26.3 0.0 collective-permute-start.6
  26.3 1.2 %collective-permute-done.6.other_values = bf16[64,512]{1,0:T(8,128)(2,1)S(1)} collective-permute-done((bf16[64,512]{1,0:T(8,128)(2,1)S(1)}, bf16[64,512]{1,0:T(8,128)(2,1)S(1)}, u32[]{:S(2)}, u32[]{:S(2)}) %collective-permute-start.6) | collective-permute-done | bytes 65568 | tf_op jit(solution)/shard_map/ppermute | solution.py:461
  27.6 0.6 project.1
  28.2 17.2 %all_to_all.20.pieces = bf16[64,2,1792]{2,1,0:T(2,128)(2,1)S(1)} all-to-all(bf16[64,2,1792]{2,1,0:T(2,128)(2,1)S(1)} %project.1), channel_id=1, replica_groups={{59,57,51,49,46,44,38,36,27,25,19,17,14,12,6,4,62,60,54,52,43,41,35,33,..., dimensions={0} | all-to-all | bytes 917504 | tf_op jit(solution)/shard_map/all_to_all | solution.py:463
  45.4 0.4 settle.1
  45.8 0.0 slice-start
  45.9 16.2 %all_to_all.21.arrived = bf16[64,2,1792]{2,1,0:T(2,128)(2,1)S(1)} all-to-all(bf16[64,2,1792]{2,1,0:T(2,128)(2,1)S(1)} %get-tuple-element.37), channel_id=1, replica_groups={{59,57,51,49,46,44,38,36,27,25,19,17,14,12,6,4,62,60,54,52,43,41,35,33,..., dimensions={0} | all-to-all | bytes 917504 | tf_op jit(solution)/shard_map/all_to_all | solution.py:465
  62.0 0.0 slice-start.1
  62.0 3.6 %lift_rows.1 = (bf16[128,2176]{1,0:T(8,128)(2,1)S(1)}, f32[128,2048]{1,0:T(8,128)S(1)}, f32[128,128]{1,0:T(8,128)S(1)}) custom-call(s32[1]{0:T(128)} %bitcast.role, bf16[64,2,1792]{2,1,0:T(2,128)(2,1)S(1)} %all_to_all.21.arrived, f32[2,1792]{1,0:T(2,128)S(1)} %reshape.17.gain, bf16[3584,1024]{1,0:T(8,128)(2,1)} %bitcast.13, bf16[3584,1024]{1,0:T(8,128)(2,1)} %bitcast.14), custom_call_target="tpu_custom_call" | custom-call | tf_op jit(solution)/shard_map/lift_rows/pallas_call | solution.py:336
  65.7 0.1 collective-permute-start.7
  65.8 1.9 %collective-permute-done.7.inward = bf16[128,2176]{1,0:T(8,128)(2,1)S(1)} collective-permute-done((bf16[128,2176]{1,0:T(8,128)(2,1)S(1)}, bf16[128,2176]{1,0:T(8,128)(2,1)S(1)}, u32[]{:S(2)}, u32[]{:S(2)}) %collective-permute-start.7) | collective-permute-done | bytes 557088 | tf_op jit(solution)/shard_map/ppermute | solution.py:468
  67.7 0.0 slice-done
  67.7 0.0 slice-done.1
  67.7 0.8 lower_rows.1
  68.5 17.3 %all_to_all.22.returned = bf16[64,2,1792]{2,1,0:T(2,128)(2,1)S(1)} all-to-all(bf16[64,2,1792]{2,1,0:T(2,128)(2,1)S(1)} %lower_rows.1), channel_id=1, replica_groups={{59,57,51,49,46,44,38,36,27,25,19,17,14,12,6,4,62,60,54,52,43,41,35,33,..., dimensions={0} | all-to-all | bytes 917504 | tf_op jit(solution)/shard_map/all_to_all | solution.py:470
  85.8 0.8 combine.1
  (1 shorter events, 0.0 us)
Async XLA Ops:
  0.0 26.0 %collective-permute-start.2 = (bf16[128,1792]{1,0:T(8,128)(2,1)}, bf16[128,1792]{1,0:T(8,128)(2,1)S(1)}, u32[]{:S(2)}, u32[]{:S(2)}) collective-permute-start(bf16[128,1792]{1,0:T(8,128)(2,1)} %bitcast.16), channel_id=1, source_target_pairs={{0,16},{1,17},{2,18},{3,19},{4,20},{5,21},{6,22},{7,23},{8,24},{9,... | collective-permute-start | bytes 1376264 | tf_op jit(solution)/shard_map/ppermute | solution.py:441
  2.0 24.0 %collective-permute-start.1 = (bf16[128,1792]{1,0:T(8,128)(2,1)}, bf16[128,1792]{1,0:T(8,128)(2,1)S(1)}, u32[]{:S(2)}, u32[]{:S(2)}) collective-permute-start(bf16[128,1792]{1,0:T(8,128)(2,1)} %bitcast.17), channel_id=1, source_target_pairs={{0,4},{1,5},{2,6},{3,7},{4,0},{5,1},{6,2},{7,3},{8,12},{9,13},{10,... | collective-permute-start | bytes 1376264 | tf_op jit(solution)/shard_map/ppermute | solution.py:441
  3.6 22.4 %collective-permute-start = (bf16[128,1792]{1,0:T(8,128)(2,1)}, bf16[128,1792]{1,0:T(8,128)(2,1)S(1)}, u32[]{:S(2)}, u32[]{:S(2)}) collective-permute-start(bf16[128,1792]{1,0:T(8,128)(2,1)} %bitcast.18), channel_id=1, source_target_pairs={{0,1},{1,0},{2,3},{3,2},{4,5},{5,4},{6,7},{7,6},{8,9},{9,8},{10,11... | collective-permute-start | bytes 1376264 | tf_op jit(solution)/shard_map/ppermute | solution.py:441
  8.0 12.7 %collective-permute-start.5 = (bf16[512,128]{1,0:T(8,128)(2,1)S(1)}, bf16[512,128]{1,0:T(8,128)(2,1)S(1)}, u32[]{:S(2)}, u32[]{:S(2)}) collective-permute-start(bf16[512,128]{1,0:T(8,128)(2,1)S(1)} %get-tuple-element.26.own), channel_id=1, source_target_pairs={{0,16},{1,17},{2,18},{3,19},{4,20},{5,21},{6,22},{7,23},{8,24},{9,... | collective-permute-start | bytes 393224 | tf_op jit(solution)/shard_map/ppermute | solution.py:455
  8.1 17.8 %all-to-all-start = ((bf16[64,16,128]{2,1,0:T(8,128)(2,1)}), bf16[64,16,128]{2,1,0:T(8,128)(2,1)S(1)}, u32[]{:S(2)}, u32[]{:S(2)}) async-start(bf16[64,16,128]{2,1,0:T(8,128)(2,1)} %bitcast.4), calls=%async_computation | async-start | bytes 524288 | tf_op jit(solution)/shard_map/all_to_all | solution.py:456
  20.5 5.2 %collective-permute-start.4 = (bf16[512,128]{1,0:T(8,128)(2,1)S(1)}, bf16[512,128]{1,0:T(8,128)(2,1)S(1)}, u32[]{:S(2)}, u32[]{:S(2)}) collective-permute-start(bf16[512,128]{1,0:T(8,128)(2,1)S(1)} %get-tuple-element.26.own), channel_id=1, source_target_pairs={{0,4},{1,5},{2,6},{3,7},{4,0},{5,1},{6,2},{7,3},{8,12},{9,13},{10,... | collective-permute-start | bytes 393224 | tf_op jit(solution)/shard_map/ppermute | solution.py:455
  20.6 5.3 %collective-permute-start.3 = (bf16[512,128]{1,0:T(8,128)(2,1)S(1)}, bf16[512,128]{1,0:T(8,128)(2,1)S(1)}, u32[]{:S(2)}, u32[]{:S(2)}) collective-permute-start(bf16[512,128]{1,0:T(8,128)(2,1)S(1)} %get-tuple-element.26.own), channel_id=1, source_target_pairs={{0,1},{1,0},{2,3},{3,2},{4,5},{5,4},{6,7},{7,6},{8,9},{9,8},{10,11... | collective-permute-start | bytes 393224 | tf_op jit(solution)/shard_map/ppermute | solution.py:455
  26.3 1.3 %collective-permute-start.6 = (bf16[64,512]{1,0:T(8,128)(2,1)S(1)}, bf16[64,512]{1,0:T(8,128)(2,1)S(1)}, u32[]{:S(2)}, u32[]{:S(2)}) collective-permute-start(bf16[64,512]{1,0:T(8,128)(2,1)S(1)} %lift_values.1.own_values), channel_id=1, source_target_pairs={{0,64},{64,0},{1,65},{65,1},{2,66},{66,2},{3,67},{67,3},{4,68},{68... | collective-permute-start | bytes 196616 | tf_op jit(solution)/shard_map/ppermute | solution.py:461
  45.8 21.9 %slice-start = ((s8[7340032]{0:T(1024)(128)(4,1)}), s8[4194304]{0:T(1024)(128)(4,1)S(1)}, s32[]{:S(2)}) async-start(s8[7340032]{0:T(1024)(128)(4,1)} %bitcast.9), calls=%async_computation.4 | async-start | bytes 8388608
  62.0 5.7 %slice-start.1 = ((s8[7340032]{0:T(1024)(128)(4,1)}), s8[3145728]{0:T(1024)(128)(4,1)S(1)}, s32[]{:S(2)}) async-start(s8[7340032]{0:T(1024)(128)(4,1)} %bitcast.9), calls=%async_computation.5 | async-start | bytes 6291456
  65.7 2.0 %collective-permute-start.7 = (bf16[128,2176]{1,0:T(8,128)(2,1)S(1)}, bf16[128,2176]{1,0:T(8,128)(2,1)S(1)}, u32[]{:S(2)}, u32[]{:S(2)}) collective-permute-start(bf16[128,2176]{1,0:T(8,128)(2,1)S(1)} %get-tuple-element.40), channel_id=1, source_target_pairs={{0,64},{64,0},{1,65},{65,1},{2,66},{66,2},{3,67},{67,3},{4,68},{68... | collective-permute-start | bytes 1671176 | tf_op jit(solution)/shard_map/ppermute | solution.py:468

commit v7 on v6

--- a/solution.py
+++ b/solution.py
@@ -68,7 +68,7 @@
     moves = [
         pltpu.make_async_copy(ids_in, ids, done.at[10]),
         pltpu.make_async_copy(scores_in, gates, done.at[11]),
-        pltpu.make_async_copy(places_in, places, done.at[12]),
+        pltpu.make_async_copy(places_in.at[role[0]], places, done.at[12]),
         pltpu.make_async_copy(w_uv, own_lift, done.at[13]),
         pltpu.make_async_copy(w_out, own_out, done.at[14]),
         pltpu.make_async_copy(resid.at[:, pl.ds(start, half_width)], own_resid, done.at[15]),
@@ -79,10 +79,10 @@
     chunks = latent_width // block
     loads = [
         pltpu.make_async_copy(lengths, valid, done.at[0]),
-        pltpu.make_async_copy(sort, sorts, done.at[1]),
+        pltpu.make_async_copy(sort.at[role[0]], sorts, done.at[1]),
     ]
     for i in range(classes):
-        token = 2 * i + role[0]
+        token = 2 * lax.rem(i + classes // 2 * role[0], classes) + role[0]
         loads.append(pltpu.make_async_copy(query.at[token], queries.at[i], done.at[2 + i]))
         loads.append(pltpu.make_async_copy(cache.at[token], caches.at[i], done.at[6 + i]))
     for copy in loads + moves:
@@ -94,7 +94,9 @@
         jnp.dot(queries[i], caches[i], preferred_element_type=f32) * softmax_scale for i in tokens
     ]
     position = lax.broadcasted_iota(jnp.int32, scores[0].shape, 1)
-    usable = [position < valid[2 * i + role[0]] for i in tokens]
+    usable = [
+        position < valid[2 * lax.rem(i + classes // 2 * role[0], classes) + role[0]] for i in tokens
+    ]
     scores = [jnp.where(u, x, -1e30) for u, x in zip(usable, scores)]
     peaks = [jnp.max(x, axis=1, keepdims=True) for x in scores]
     exponents = [jnp.where(u, jnp.exp(x - m), 0.0) for u, x, m in zip(usable, scores, peaks)]
@@ -145,7 +147,7 @@
 def attend(role_index, lengths, query, cache, sort, w_uv, w_out, resid, ids, gates, places):
     latent_width, block = w_uv.shape
     half_width = w_out.shape[1]
-    slots = places.shape[1]
+    slots = places.shape[2]
     tokens, heads, key_width = query.shape
     positions = cache.shape[1]
     classes = len(flips)
@@ -165,11 +167,11 @@
         scratch_shapes=[
             pltpu.VMEM((classes, heads, key_width), bf16),
             pltpu.VMEM((classes, key_width, positions), bf16),
-            pltpu.VMEM(sort.shape, bf16),
+            pltpu.VMEM(sort.shape[1:], bf16),
             pltpu.SMEM((tokens,), jnp.int32),
             pltpu.VMEM(ids.shape, jnp.int32),
             pltpu.VMEM(gates.shape, f32),
-            pltpu.VMEM(places.shape, jnp.int32),
+            pltpu.VMEM(places.shape[1:], jnp.int32),
             pltpu.VMEM((rows + 32, block), f32),
             pltpu.SemaphoreType.DMA((16,)),
         ],
@@ -227,10 +229,15 @@
     )(gathered, *weights)
 
 
+def turned(value):
+    half = value.shape[0] // 2
+    return jnp.concatenate([value[half:], value[:half]], axis=0)
+
+
 def project_kernel(role, own_values, other_values, *rest):
     *weights, partial, spread = rest
     rows, block = own_values.shape[0], weights[0].shape[0]
-    for place, values in ((role[0], own_values), (1 - role[0], other_values)):
+    for place, values in ((role[0], own_values[...]), (1 - role[0], turned(other_values[...]))):
         for i in range(len(weights)):
             spread[i, pl.ds(place, rows, stride=2)] = values[
                 :, i * block : (i + 1) * block
@@ -254,13 +261,14 @@
     )(role_index.reshape(1), own_values, other_values, *weights)
 
 
-def settle_kernel(pieces, resid, taken, hidden, packed):
+def settle_kernel(role, pieces, resid, taken, hidden, packed):
     tokens, half = hidden.shape
     rows = pieces.shape[0] * pieces.shape[1]
     token = lax.broadcasted_iota(jnp.int32, (tokens, rows), 0)
     row = lax.broadcasted_iota(jnp.int32, (tokens, rows), 1)
     span = 2 * rows // tokens
-    ours = (row // span == token // 2) & (row % 2 == token % 2)
+    source = (row // span + tokens // 4 * role[0]) % (tokens // 2)
+    ours = (source == token // 2) & (row % 2 == token % 2)
     attended = jnp.dot(
         ours.astype(bf16), pieces[...].reshape(rows, half), preferred_element_type=f32
     )
@@ -271,7 +279,7 @@
     ).astype(bf16).reshape(packed.shape)
 
 
-def settle(pieces, resid, taken, capacity):
+def settle(role_index, pieces, resid, taken, capacity):
     tokens, half = resid.shape
     return pl.pallas_call(
         settle_kernel,
@@ -279,11 +287,11 @@
             jax.ShapeDtypeStruct((tokens, half), f32),
             jax.ShapeDtypeStruct((taken.shape[1] // capacity, capacity, half), bf16),
         ],
-        in_specs=[in_vmem] * 3,
+        in_specs=[in_smem] + [in_vmem] * 3,
         out_specs=[in_vmem] * 2,
         compiler_params=pltpu.CompilerParams(vmem_limit_bytes=8 * MIB),
         name="settle",
-    )(pieces, resid, taken)
+    )(role_index.reshape(1), pieces, resid, taken)
 
 
 def keep_vmem(value):
@@ -355,7 +363,7 @@
     hidden_units, half = down.shape[0], down.shape[1] // 2
     step = 256
     squares = jnp.sum(
-        terms[...] + inward[:, 2 * hidden_units :].astype(f32), axis=1, keepdims=True
+        terms[...] + turned(inward[:, 2 * hidden_units :]).astype(f32), axis=1, keepdims=True
     )
     scale = lax.rsqrt(squares / width + 1e-06)
     ours = pl.ds(pl.multiple_of(role[0] * half, 128), half)
@@ -363,8 +371,8 @@
     for i in range(hidden_units // step):
         gate_at = slice(i * step, (i + 1) * step)
         up_at = slice(hidden_units + i * step, hidden_units + (i + 1) * step)
-        gate_part = (own[:, gate_at] + inward[:, gate_at].astype(f32)) * scale
-        up_part = (own[:, up_at] + inward[:, up_at].astype(f32)) * scale
+        gate_part = (own[:, gate_at] + turned(inward[:, gate_at]).astype(f32)) * scale
+        up_part = (own[:, up_at] + turned(inward[:, up_at]).astype(f32)) * scale
         inner = (gate_part / (1.0 + jnp.exp(-gate_part)) * up_part).astype(bf16)
         total += jnp.dot(inner, down[gate_at, ours], preferred_element_type=f32)
     produced[...] = total.astype(bf16).reshape(produced.shape)
@@ -423,20 +431,27 @@
     swap = [(0, 1), (1, 0)]
 
     order = visit_order(n_dev)
+    orders = [order, order[n_dev // 2 :] + order[: n_dev // 2]]
     exchange = functools.partial(
         lax.all_to_all,
-        axis_name="dev",
+        axis_name=("role", "dev"),
         split_axis=0,
         concat_axis=0,
-        axis_index_groups=[order],
+        axis_index_groups=[orders[0], [n_dev + dev for dev in orders[1]]],
         tiled=True,
     )
     span = n_dev // len(flips)
-    wanted = np.zeros((len(flips), n_dev, n_dev), np.float32)
-    for place, dev in enumerate(order):
-        for i, flip in enumerate(flips):
-            wanted[place // span, place % span * len(flips) + i, dev ^ flip] = 1.0
-    places = np.stack([np.repeat(order, capacity), np.tile(np.arange(capacity), n_dev)])
+    wanted = np.zeros((2, len(flips), n_dev, n_dev), np.float32)
+    for r in range(2):
+        for place, dev in enumerate(orders[r]):
+            for i, flip in enumerate(flips):
+                wanted[r, place // span, place % span * len(flips) + i, dev ^ flip] = 1.0
+    places = np.stack(
+        [
+            np.stack([np.repeat(each, capacity), np.tile(np.arange(capacity), n_dev)])
+            for each in orders
+        ]
+    )
     steps = [[(dev, dev ^ flip) for dev in range(n_dev)] for flip in flips[1:]]
     other_outs = [lax.ppermute(w_out[0], "dev", step) for step in steps]
     sent, own_lift, own_out, own_resid, taken, combine_weights = attend(
@@ -461,7 +476,7 @@
     other_values = lax.ppermute(own_values, "role", swap)
     partial = project(role_index, own_values, other_values, [own_out, *other_outs])
     pieces = exchange(partial)
-    hidden, packed = settle(pieces, own_resid, taken, capacity)
+    hidden, packed = settle(role_index, pieces, own_resid, taken, capacity)
     arrived = exchange(packed)
 
     outward, own_sums, square_terms = lift_rows(role_index, arrived, gain, w_gate[0], w_up[0])

time: 87 us -> 87 us (level)
  no operation moved by 1% of the time
where the time goes in v7:
time: 87 us; the launch traced here: 86.5 us
  blocking collectives  50.2 us (58%)
  starting transfers between devices  18.6 us (21%)
  Pallas kernels  9.46 us (11%)
  waiting for transfers between devices  7.49 us (9%)
    all_to_all x1, blocking collectives, local(): returned = exchange(produced)  17.5 us
    all_to_all x1, blocking collectives, local(): pieces = exchange(partial)  16.5 us
    all_to_all x1, blocking collectives, local(): arrived = exchange(packed)  16.1 us
    all_to_all x1, starting transfers between devices, local(): gathered = exchange(sent.reshape(n_dev, -1, sent.shape[1]))  12.4 us
    ppermute x3, starting transfers between devices, local(): other_outs = [lax.ppermute(w_out[0], 'dev', step) for step in steps]  5.07 us
    ppermute x3, waiting for transfers between devices, local(): other_lifts = [lax.ppermute(own_lift, 'dev', step) for step in steps]  4.29 us
    pallas_call x1, Pallas kernels, lift_rows(): pl.pallas_call(lift_kernel, out_shape=[jax.ShapeDtypeStruct((rows, 2 * hi...  3.63 us
    pallas_call x1, Pallas kernels, attend(): pl.pallas_call(attend_kernel, out_shape=[jax.ShapeDtypeStruct((rows, bloc...  2.89 us
  transfers between devices with their start and end apart: 9, of which 4 were waited for; matrix products, arithmetic and copies ran while one was open for 1% of the time, Pallas kernels for 3%

profile of v7, /device:TPU:0, one launch (start us, length us, event | category | flops | bytes accessed | tf_op | source)
XLA Modules:
  0.0 86.5 jit_solution(18279465614816207778)
XLA Ops:
  0.0 2.0 %collective-permute-start.2 = (bf16[128,1792]{1,0:T(8,128)(2,1)}, bf16[128,1792]{1,0:T(8,128)(2,1)S(1)}, u32[]{:S(2)}, u32[]{:S(2)}) collective-permute-start(bf16[128,1792]{1,0:T(8,128)(2,1)} %bitcast.16), channel_id=1, source_target_pairs={{0,16},{1,17},{2,18},{3,19},{4,20},{5,21},{6,22},{7,23},{8,24},{9,... | collective-permute-start | bytes 1376264 | tf_op jit(solution)/shard_map/ppermute | solution.py:456
  2.0 1.6 %collective-permute-start.1 = (bf16[128,1792]{1,0:T(8,128)(2,1)}, bf16[128,1792]{1,0:T(8,128)(2,1)S(1)}, u32[]{:S(2)}, u32[]{:S(2)}) collective-permute-start(bf16[128,1792]{1,0:T(8,128)(2,1)} %bitcast.17), channel_id=1, source_target_pairs={{0,4},{1,5},{2,6},{3,7},{4,0},{5,1},{6,2},{7,3},{8,12},{9,13},{10,... | collective-permute-start | bytes 1376264 | tf_op jit(solution)/shard_map/ppermute | solution.py:456
  3.6 1.5 %collective-permute-start = (bf16[128,1792]{1,0:T(8,128)(2,1)}, bf16[128,1792]{1,0:T(8,128)(2,1)S(1)}, u32[]{:S(2)}, u32[]{:S(2)}) collective-permute-start(bf16[128,1792]{1,0:T(8,128)(2,1)} %bitcast.18), channel_id=1, source_target_pairs={{0,1},{1,0},{2,3},{3,2},{4,5},{5,4},{6,7},{7,6},{8,9},{9,8},{10,11... | collective-permute-start | bytes 1376264 | tf_op jit(solution)/shard_map/ppermute | solution.py:456
  5.1 2.9 %attend.1 = (bf16[1024,128]{1,0:T(8,128)(2,1)}, bf16[512,128]{1,0:T(8,128)(2,1)S(1)}, bf16[128,1792]{1,0:T(8,128)(2,1)S(1)}, bf16[8,1792]{1,0:T(8,128)(2,1)S(1)}...) custom-call(s32[1]{0:T(128)} %bitcast.role, s32[8]{0:T(128)} %lengths.1, bf16[8,64,576]{2,1,0:T(8,128)(2,1)} %query.1, ...), custom_call_target="tpu_custom_call" | custom-call | tf_op jit(solution)/shard_map/attend/pallas_call | solution.py:155
  8.0 0.2 collective-permute-start.5
  8.2 12.4 %all-to-all-start = ((bf16[64,16,128]{2,1,0:T(8,128)(2,1)}), bf16[64,16,128]{2,1,0:T(8,128)(2,1)S(1)}, u32[]{:S(2)}, u32[]{:S(2)}) async-start(bf16[64,16,128]{2,1,0:T(8,128)(2,1)} %bitcast.4), calls=%async_computation | async-start | bytes 524288 | tf_op jit(solution)/shard_map/all_to_all | solution.py:471
  20.5 0.1 collective-permute-start.4
  20.6 0.0 collective-permute-done.5.rest_2_
  20.6 0.7 collective-permute-start.3
  21.4 0.7 reshape.18.gain
  22.1 3.7 %collective-permute-done.4.rest_1_ = bf16[512,128]{1,0:T(8,128)(2,1)S(1)} collective-permute-done((bf16[512,128]{1,0:T(8,128)(2,1)S(1)}, bf16[512,128]{1,0:T(8,128)(2,1)S(1)}, u32[]{:S(2)}, u32[]{:S(2)}) %collective-permute-start.4) | collective-permute-done | bytes 131104 | tf_op jit(solution)/shard_map/ppermute | solution.py:470
  25.8 0.6 collective-permute-done.3.rest_0_
  26.4 0.0 all-to-all-done
  26.4 0.0 collective-permute-done.2.rest_3_
  26.4 0.0 collective-permute-done.1.rest_2_
  26.4 0.0 collective-permute-done.rest_1_
  26.4 0.3 lift_values.1.own_values
  26.7 0.0 collective-permute-start.6
  26.8 1.2 %collective-permute-done.6.other_values = bf16[64,512]{1,0:T(8,128)(2,1)S(1)} collective-permute-done((bf16[64,512]{1,0:T(8,128)(2,1)S(1)}, bf16[64,512]{1,0:T(8,128)(2,1)S(1)}, u32[]{:S(2)}, u32[]{:S(2)}) %collective-permute-start.6) | collective-permute-done | bytes 65568 | tf_op jit(solution)/shard_map/ppermute | solution.py:476
  28.0 0.6 project.1
  28.7 16.5 %all_to_all.20.pieces = bf16[64,2,1792]{2,1,0:T(2,128)(2,1)S(1)} all-to-all(bf16[64,2,1792]{2,1,0:T(2,128)(2,1)S(1)} %project.1), channel_id=1, replica_groups={{59,57,51,49,46,44,38,36,27,25,19,17,14,12,6,4,62,60,54,52,43,41,35,33,..., dimensions={0} | all-to-all | bytes 917504 | tf_op jit(solution)/shard_map/all_to_all | solution.py:478
  45.2 0.4 settle.1
  45.6 0.0 slice-start
  45.6 16.1 %all_to_all.21.arrived = bf16[64,2,1792]{2,1,0:T(2,128)(2,1)S(1)} all-to-all(bf16[64,2,1792]{2,1,0:T(2,128)(2,1)S(1)} %get-tuple-element.37), channel_id=1, replica_groups={{59,57,51,49,46,44,38,36,27,25,19,17,14,12,6,4,62,60,54,52,43,41,35,33,..., dimensions={0} | all-to-all | bytes 917504 | tf_op jit(solution)/shard_map/all_to_all | solution.py:480
  61.8 0.0 slice-start.1
  61.8 3.6 %lift_rows.1 = (bf16[128,2176]{1,0:T(8,128)(2,1)S(1)}, f32[128,2048]{1,0:T(8,128)S(1)}, f32[128,128]{1,0:T(8,128)S(1)}) custom-call(s32[1]{0:T(128)} %bitcast.role, bf16[64,2,1792]{2,1,0:T(2,128)(2,1)S(1)} %all_to_all.21.arrived, f32[2,1792]{1,0:T(2,128)S(1)} %reshape.18.gain, bf16[3584,1024]{1,0:T(8,128)(2,1)} %bitcast.13, bf16[3584,1024]{1,0:T(8,128)(2,1)} %bitcast.14), custom_call_target="tpu_custom_call" | custom-call | tf_op jit(solution)/shard_map/lift_rows/pallas_call | solution.py:344
  65.4 0.1 collective-permute-start.7
  65.5 1.9 %collective-permute-done.7.inward = bf16[128,2176]{1,0:T(8,128)(2,1)S(1)} collective-permute-done((bf16[128,2176]{1,0:T(8,128)(2,1)S(1)}, bf16[128,2176]{1,0:T(8,128)(2,1)S(1)}, u32[]{:S(2)}, u32[]{:S(2)}) %collective-permute-start.7) | collective-permute-done | bytes 557088 | tf_op jit(solution)/shard_map/ppermute | solution.py:483
  67.4 0.0 slice-done
  67.4 0.0 slice-done.1
  67.4 0.8 lower_rows.1
  68.2 17.5 %all_to_all.22.returned = bf16[64,2,1792]{2,1,0:T(2,128)(2,1)S(1)} all-to-all(bf16[64,2,1792]{2,1,0:T(2,128)(2,1)S(1)} %lower_rows.1), channel_id=1, replica_groups={{59,57,51,49,46,44,38,36,27,25,19,17,14,12,6,4,62,60,54,52,43,41,35,33,..., dimensions={0} | all-to-all | bytes 917504 | tf_op jit(solution)/shard_map/all_to_all | solution.py:485
  85.7 0.8 combine.1
  (1 shorter events, 0.0 us)
Async XLA Ops:
  0.0 26.4 %collective-permute-start.2 = (bf16[128,1792]{1,0:T(8,128)(2,1)}, bf16[128,1792]{1,0:T(8,128)(2,1)S(1)}, u32[]{:S(2)}, u32[]{:S(2)}) collective-permute-start(bf16[128,1792]{1,0:T(8,128)(2,1)} %bitcast.16), channel_id=1, source_target_pairs={{0,16},{1,17},{2,18},{3,19},{4,20},{5,21},{6,22},{7,23},{8,24},{9,... | collective-permute-start | bytes 1376264 | tf_op jit(solution)/shard_map/ppermute | solution.py:456
  2.0 24.4 %collective-permute-start.1 = (bf16[128,1792]{1,0:T(8,128)(2,1)}, bf16[128,1792]{1,0:T(8,128)(2,1)S(1)}, u32[]{:S(2)}, u32[]{:S(2)}) collective-permute-start(bf16[128,1792]{1,0:T(8,128)(2,1)} %bitcast.17), channel_id=1, source_target_pairs={{0,4},{1,5},{2,6},{3,7},{4,0},{5,1},{6,2},{7,3},{8,12},{9,13},{10,... | collective-permute-start | bytes 1376264 | tf_op jit(solution)/shard_map/ppermute | solution.py:456
  3.6 22.8 %collective-permute-start = (bf16[128,1792]{1,0:T(8,128)(2,1)}, bf16[128,1792]{1,0:T(8,128)(2,1)S(1)}, u32[]{:S(2)}, u32[]{:S(2)}) collective-permute-start(bf16[128,1792]{1,0:T(8,128)(2,1)} %bitcast.18), channel_id=1, source_target_pairs={{0,1},{1,0},{2,3},{3,2},{4,5},{5,4},{6,7},{7,6},{8,9},{9,8},{10,11... | collective-permute-start | bytes 1376264 | tf_op jit(solution)/shard_map/ppermute | solution.py:456
  8.0 12.7 %collective-permute-start.5 = (bf16[512,128]{1,0:T(8,128)(2,1)S(1)}, bf16[512,128]{1,0:T(8,128)(2,1)S(1)}, u32[]{:S(2)}, u32[]{:S(2)}) collective-permute-start(bf16[512,128]{1,0:T(8,128)(2,1)S(1)} %get-tuple-element.26.own), channel_id=1, source_target_pairs={{0,16},{1,17},{2,18},{3,19},{4,20},{5,21},{6,22},{7,23},{8,24},{9,... | collective-permute-start | bytes 393224 | tf_op jit(solution)/shard_map/ppermute | solution.py:470
  8.2 18.2 %all-to-all-start = ((bf16[64,16,128]{2,1,0:T(8,128)(2,1)}), bf16[64,16,128]{2,1,0:T(8,128)(2,1)S(1)}, u32[]{:S(2)}, u32[]{:S(2)}) async-start(bf16[64,16,128]{2,1,0:T(8,128)(2,1)} %bitcast.4), calls=%async_computation | async-start | bytes 524288 | tf_op jit(solution)/shard_map/all_to_all | solution.py:471
  20.5 5.3 %collective-permute-start.4 = (bf16[512,128]{1,0:T(8,128)(2,1)S(1)}, bf16[512,128]{1,0:T(8,128)(2,1)S(1)}, u32[]{:S(2)}, u32[]{:S(2)}) collective-permute-start(bf16[512,128]{1,0:T(8,128)(2,1)S(1)} %get-tuple-element.26.own), channel_id=1, source_target_pairs={{0,4},{1,5},{2,6},{3,7},{4,0},{5,1},{6,2},{7,3},{8,12},{9,13},{10,... | collective-permute-start | bytes 393224 | tf_op jit(solution)/shard_map/ppermute | solution.py:470
  20.6 5.7 %collective-permute-start.3 = (bf16[512,128]{1,0:T(8,128)(2,1)S(1)}, bf16[512,128]{1,0:T(8,128)(2,1)S(1)}, u32[]{:S(2)}, u32[]{:S(2)}) collective-permute-start(bf16[512,128]{1,0:T(8,128)(2,1)S(1)} %get-tuple-element.26.own), channel_id=1, source_target_pairs={{0,1},{1,0},{2,3},{3,2},{4,5},{5,4},{6,7},{7,6},{8,9},{9,8},{10,11... | collective-permute-start | bytes 393224 | tf_op jit(solution)/shard_map/ppermute | solution.py:470
  26.7 1.3 %collective-permute-start.6 = (bf16[64,512]{1,0:T(8,128)(2,1)S(1)}, bf16[64,512]{1,0:T(8,128)(2,1)S(1)}, u32[]{:S(2)}, u32[]{:S(2)}) collective-permute-start(bf16[64,512]{1,0:T(8,128)(2,1)S(1)} %lift_values.1.own_values), channel_id=1, source_target_pairs={{0,64},{64,0},{1,65},{65,1},{2,66},{66,2},{3,67},{67,3},{4,68},{68... | collective-permute-start | bytes 196616 | tf_op jit(solution)/shard_map/ppermute | solution.py:476
  45.6 21.8 %slice-start = ((s8[7340032]{0:T(1024)(128)(4,1)}), s8[4194304]{0:T(1024)(128)(4,1)S(1)}, s32[]{:S(2)}) async-start(s8[7340032]{0:T(1024)(128)(4,1)} %bitcast.9), calls=%async_computation.4 | async-start | bytes 8388608
  61.8 5.7 %slice-start.1 = ((s8[7340032]{0:T(1024)(128)(4,1)}), s8[3145728]{0:T(1024)(128)(4,1)S(1)}, s32[]{:S(2)}) async-start(s8[7340032]{0:T(1024)(128)(4,1)} %bitcast.9), calls=%async_computation.5 | async-start | bytes 6291456
  65.4 2.0 %collective-permute-start.7 = (bf16[128,2176]{1,0:T(8,128)(2,1)S(1)}, bf16[128,2176]{1,0:T(8,128)(2,1)S(1)}, u32[]{:S(2)}, u32[]{:S(2)}) collective-permute-start(bf16[128,2176]{1,0:T(8,128)(2,1)S(1)} %get-tuple-element.40), channel_id=1, source_target_pairs={{0,64},{64,0},{1,65},{65,1},{2,66},{66,2},{3,67},{67,3},{4,68},{68... | collective-permute-start | bytes 1671176 | tf_op jit(solution)/shard_map/ppermute | solution.py:483
